TPU v7x, 32 devices: a whole 2x2x4 slice. The times are simulated.
32 devices in a mesh: dp: 8 (over z, core), ctx: 2 (over y), exp: 2 (over x).
Axes of the slice: x: 2, y: 2, z: 4, core: 2. Of those that a mesh axis runs over, the one named last changes fastest.
Arguments:
- residual_in: bfloat16 [16, 1024, 768], P(('dp', 'exp'), 'ctx'), may hold values from -6 to 6
- lengths: int32 [16], P(('dp', 'exp')), may hold values from 256 to 1024, as said below
- routes: int32 [16, 1024, 2], P(('dp', 'exp'), 'ctx'), may hold values from 0 to 11, all different within a row; in each aligned block of 512 rows (0 to 511, 512 to 1023, ..., all dimensions but the last counted through in order) at most 128 rows name the same one
- prev_logits: float32 [16, 1024, 12], P(('dp', 'exp'), 'ctx'), may hold values from -4 to 4
- cotangent: float32 [16, 1024, 768], P(('dp', 'exp'), 'ctx'), may hold values from -6 to 6
- w_qkv: bfloat16 [768, 2304], P(('dp', 'ctx', 'exp')), may hold values from -0.21875 to 0.21875
- w_out: bfloat16 [768, 768], P(('dp', 'ctx', 'exp')), may hold values from -0.875 to 0.875
- attn_gain: bfloat16 [768], P(('dp', 'ctx', 'exp')), may hold values from 0.5 to 1.5
- ffn_gain: bfloat16 [768], P(('dp', 'ctx', 'exp')), may hold values from 0.5 to 1.5
- router: bfloat16 [768, 12], P(('dp', 'ctx', 'exp')), may hold values from -0.15625 to 0.15625
- const_gate: bfloat16 [768, 4], P(('dp', 'ctx', 'exp')), may hold values from -0.21875 to 0.21875
- const_vec: bfloat16 [768, 2], P(('dp', 'ctx', 'exp')), may hold values from -24 to 24
- w_gate: bfloat16 [8, 768, 2048], P('exp', None, ('dp', 'ctx')), may hold values from -0.21875 to 0.21875
- w_up: bfloat16 [8, 768, 2048], P('exp', None, ('dp', 'ctx')), may hold values from -0.21875 to 0.21875
- w_down: bfloat16 [8, 2048, 768], P('exp', ('dp', 'ctx')), may hold values from -1 to 1
Outputs:
- output: float32 [16, 1024, 768], P(('dp', 'exp'), 'ctx')
- grad_x: float32 [16, 1024, 768], P(('dp', 'exp'), 'ctx')
- grad_w_qkv: float32 [768, 2304], P(('dp', 'ctx', 'exp'))
- grad_w_out: float32 [768, 768], P(('dp', 'ctx', 'exp'))
- grad_attn_gain: float32 [768], P(('dp', 'ctx', 'exp'))
- grad_ffn_gain: float32 [768], P(('dp', 'ctx', 'exp'))
- grad_router: float32 [768, 12], P(('dp', 'ctx', 'exp'))
- grad_const_gate: float32 [768, 4], P(('dp', 'ctx', 'exp'))
- grad_const_vec: float32 [768, 2], P(('dp', 'ctx', 'exp'))
- grad_w_gate: float32 [8, 768, 2048], P('exp', None, ('dp', 'ctx'))
- grad_w_up: float32 [8, 768, 2048], P('exp', None, ('dp', 'ctx'))
- grad_w_down: float32 [8, 2048, 768], P('exp', ('dp', 'ctx'))
Inputs may be any that keep to these rules, and one draw needn't show every extreme that they name: `lengths`: one sequence has all 1024 slots used in every draw. `routes`: the two ids of a token differ; among the 512 rows of one device no id is named more than 128 times, a bound that some block reaches.
All inputs are finite; a program needn't handle non-finite values.
Results may differ from a plain program's by a relative error of at most 0.015.
Values may be sent and summed in bfloat16 or wider, within the bound.
No kernel may reach another device: no remote copies, remote signals or barrier semaphores. Data moves between devices by JAX's collectives and lax.ppermute only.
A program may use at most 256 MiB of HBM per device.

v0:
```python
import jax
import jax.numpy as jnp
from jax import lax
from jax.sharding import PartitionSpec as P

HEADS = 12
KBLK = 512


norm_eps = 1e-06
top_precision = lax.Precision.HIGHEST


def rms_forward(in_rows, gain_vec):
    inv_scale = lax.rsqrt(jnp.mean(in_rows * in_rows, axis=-1, keepdims=True) + norm_eps)
    return (in_rows * inv_scale * gain_vec, inv_scale)


def rms_backward(in_rows, inv_scale, gain_vec, grad_rows):
    normed = in_rows * inv_scale
    gain_grad = jnp.sum(grad_rows * normed, axis=0)
    inner_grad = grad_rows * gain_vec
    back_rows = inv_scale * (
        inner_grad - normed * jnp.mean(inner_grad * normed, axis=-1, keepdims=True)
    )
    return (back_rows, gain_grad)


def rotate(in_rows, positions, sign_value):
    half_size = in_rows.shape[-1] // 2
    inv_freq = 10000.0 ** (-2.0 * jnp.arange(half_size, dtype=jnp.float32) / in_rows.shape[-1])
    angles = positions.astype(jnp.float32)[:, None] * inv_freq[None, :]
    cosine = jnp.cos(angles)[:, None, :]
    sine_part = sign_value * jnp.sin(angles)[:, None, :]
    first_half = in_rows[..., :half_size]
    second_half = in_rows[..., half_size:]
    return jnp.concatenate(
        [
            first_half * cosine - second_half * sine_part,
            second_half * cosine + first_half * sine_part,
        ],
        axis=-1,
    )


def slot_rank(route_ids, expert_total):
    flat_ids = route_ids.reshape(-1)
    onehot = (flat_ids[:, None] == jnp.arange(expert_total, dtype=jnp.int32)[None, :]).astype(
        jnp.int32
    )
    earlier = jnp.cumsum(onehot, axis=0) - onehot
    return jnp.sum(earlier * onehot, axis=1).reshape(route_ids.shape)


def local(
    residual_in,
    lengths,
    routes,
    prev_logits,
    cotangent,
    w_qkv,
    w_out,
    attn_gain,
    ffn_gain,
    router,
    const_gate,
    const_vec,
    w_gate,
    w_up,
    w_down,
):
    tok_rows = residual_in.shape[1]
    feat_width = residual_in.shape[2]
    head_size = feat_width // HEADS
    score_scale = head_size ** (-0.5)
    n_ctx = lax.axis_size("ctx")
    n_exp = lax.axis_size("exp")
    seq_rows = tok_rows * n_ctx
    ctx_rank = lax.axis_index("ctx")
    positions = ctx_rank * tok_rows + jnp.arange(tok_rows, dtype=jnp.int32)
    length = lengths[0]
    valid_rows = (positions < length).astype(jnp.float32)[:, None]
    in_rows = residual_in[0].astype(jnp.float32)
    gathered = (
        lax.all_gather(w_qkv, ("dp", "ctx", "exp"), axis=0, tiled=True),
        lax.all_gather(w_out, ("dp", "ctx", "exp"), axis=0, tiled=True),
        lax.all_gather(attn_gain, ("dp", "ctx", "exp"), axis=0, tiled=True),
        lax.all_gather(ffn_gain, ("dp", "ctx", "exp"), axis=0, tiled=True),
        lax.all_gather(router, ("dp", "ctx", "exp"), axis=0, tiled=True),
        lax.all_gather(const_gate, ("dp", "ctx", "exp"), axis=0, tiled=True),
        lax.all_gather(const_vec, ("dp", "ctx", "exp"), axis=0, tiled=True),
    )
    full_qkv, full_out, gain_first, gain_second, full_router, full_const_gate, full_const_vec = (
        gathered
    )
    gain_attn = gain_first.astype(jnp.float32)
    gain_ffn = gain_second.astype(jnp.float32)
    normed_one, scale_one = rms_forward(in_rows, gain_attn)
    hidden_one = normed_one.astype(jnp.bfloat16)
    qkv_rows = jnp.dot(hidden_one, full_qkv, preferred_element_type=jnp.float32).reshape(
        tok_rows, 3, HEADS, head_size
    )
    queries = rotate(qkv_rows[:, 0], positions, 1.0).astype(jnp.bfloat16)
    own_keys = (
        rotate(qkv_rows[:, 1], positions, 1.0).astype(jnp.bfloat16).reshape(tok_rows, feat_width)
    )
    own_values = qkv_rows[:, 2].astype(jnp.bfloat16).reshape(tok_rows, feat_width)
    all_keys, all_values = (
        lax.all_gather(own_keys, "ctx", axis=0, tiled=True),
        lax.all_gather(own_values, "ctx", axis=0, tiled=True),
    )
    key_count = jnp.minimum((ctx_rank + 1) * tok_rows, length)
    blk_count = (key_count + KBLK - 1) // KBLK

    def block_scores(blk_index):
        blk_start = blk_index * KBLK
        key_rows = lax.dynamic_slice_in_dim(all_keys, blk_start, KBLK, 0).reshape(
            KBLK, HEADS, head_size
        )
        value_rows = lax.dynamic_slice_in_dim(all_values, blk_start, KBLK, 0).reshape(
            KBLK, HEADS, head_size
        )
        key_pos = blk_start + jnp.arange(KBLK, dtype=jnp.int32)
        allowed = (key_pos[None, :] <= positions[:, None]) & (key_pos[None, :] < length)
        raw_scores = (
            jnp.einsum("qhd,khd->hqk", queries, key_rows, preferred_element_type=jnp.float32)
            * score_scale
        )
        return (jnp.where(allowed[None], raw_scores, -1e30), key_rows, value_rows)

    def forward_step(blk_index, loop_state):
        run_max, run_total, run_acc = loop_state
        blk_scores, key_rows, value_rows = block_scores(blk_index)
        new_max = jnp.maximum(run_max, jnp.max(blk_scores, axis=-1))
        expo_vals = jnp.exp(blk_scores - new_max[..., None])
        factor = jnp.exp(run_max - new_max)
        run_total = run_total * factor + jnp.sum(expo_vals, axis=-1)
        run_acc = run_acc * jnp.transpose(factor)[:, :, None] + jnp.einsum(
            "hqk,khd->qhd",
            expo_vals.astype(jnp.bfloat16),
            value_rows,
            preferred_element_type=jnp.float32,
        )
        return (new_max, run_total, run_acc)

    start_state = (
        jnp.full((HEADS, tok_rows), -1e30, jnp.float32),
        jnp.zeros((HEADS, tok_rows), jnp.float32),
        jnp.zeros((tok_rows, HEADS, head_size), jnp.float32),
    )
    run_max, run_total, run_acc = lax.fori_loop(0, blk_count, forward_step, start_state)
    attended = run_acc / jnp.transpose(run_total)[:, :, None]
    log_total = run_max + jnp.log(run_total)
    attended_low = attended.reshape(tok_rows, feat_width).astype(jnp.bfloat16)
    mid_rows = in_rows + jnp.dot(attended_low, full_out, preferred_element_type=jnp.float32)
    normed_two, scale_two = rms_forward(mid_rows, gain_ffn)
    hidden = normed_two.astype(jnp.bfloat16)
    hidden_f = hidden.astype(jnp.float32)
    n_all = full_router.shape[1]
    n_ffn = n_all - 4
    exp_dev = w_gate.shape[0]
    cap_rows = tok_rows // 4
    logits = jnp.dot(hidden, full_router, preferred_element_type=jnp.float32) + prev_logits[0]
    gate_probs = jax.nn.softmax(logits, axis=-1)
    route_ids = routes[0]
    choose = (route_ids[:, :, None] == jnp.arange(n_all, dtype=jnp.int32)[None, None, :]).astype(
        jnp.float32
    )
    gate_vals = jnp.sum(choose * gate_probs[:, None, :], axis=-1)
    slot_ids = slot_rank(route_ids, n_all)
    is_ffn = route_ids < n_ffn
    is_ffn_f = is_ffn.astype(jnp.float32)
    expert_index = jnp.where(is_ffn, route_ids, n_ffn)
    safe_index = jnp.where(is_ffn, route_ids, 0)
    spread_rows = jnp.broadcast_to(hidden[:, None, :], (tok_rows, 2, feat_width))
    send_buf = (
        jnp.zeros((n_ffn, cap_rows, feat_width), jnp.bfloat16)
        .at[expert_index, slot_ids]
        .set(spread_rows, mode="drop")
    )
    arrived = lax.all_to_all(
        send_buf.reshape(n_exp, exp_dev * cap_rows, feat_width),
        "exp",
        split_axis=0,
        concat_axis=0,
        tiled=True,
    )
    arrived = arrived.reshape(n_exp, exp_dev, cap_rows, feat_width)
    gate_full, up_full, down_full = (
        lax.all_gather(w_gate, ("dp", "ctx"), axis=2, tiled=True),
        lax.all_gather(w_up, ("dp", "ctx"), axis=2, tiled=True),
        lax.all_gather(w_down, ("dp", "ctx"), axis=1, tiled=True),
    )
    gate_pre = jnp.einsum("secd,edf->secf", arrived, gate_full, preferred_element_type=jnp.float32)
    up_pre = jnp.einsum("secd,edf->secf", arrived, up_full, preferred_element_type=jnp.float32)
    sigmoid_gate = jax.nn.sigmoid(gate_pre)
    silu_gate = gate_pre * sigmoid_gate
    act_vals = (silu_gate * up_pre).astype(jnp.bfloat16)
    expert_out = jnp.einsum(
        "secf,efd->secd", act_vals, down_full, preferred_element_type=jnp.float32
    ).astype(jnp.bfloat16)
    returned = lax.all_to_all(
        expert_out.reshape(n_exp, exp_dev * cap_rows, feat_width),
        "exp",
        split_axis=0,
        concat_axis=0,
        tiled=True,
    )
    returned = returned.reshape(n_ffn, cap_rows, feat_width)
    ffn_rows = returned[safe_index, slot_ids].astype(jnp.float32) * is_ffn_f[..., None]
    const_mix = jax.nn.softmax(
        jnp.dot(hidden, full_const_gate, preferred_element_type=jnp.float32).reshape(
            tok_rows, 2, 2
        ),
        axis=-1,
    )
    vectors = jnp.transpose(full_const_vec.astype(jnp.float32))
    const_rows = const_mix[..., 0:1] * hidden_f[:, None, :] + const_mix[..., 1:2] * vectors[None]
    is_copy = (route_ids == n_ffn + 1).astype(jnp.float32)
    pick_const = (
        route_ids[:, :, None] == n_ffn + 2 + jnp.arange(2, dtype=jnp.int32)[None, None, :]
    ).astype(jnp.float32)
    chosen = (
        ffn_rows
        + is_copy[..., None] * hidden_f[:, None, :]
        + jnp.sum(pick_const[..., None] * const_rows[:, None, :, :], axis=2)
    )
    moe_out = jnp.sum(gate_vals[..., None] * chosen, axis=1)
    output = (mid_rows + moe_out) * valid_rows
    grad_out = cotangent[0] * valid_rows
    grad_gates = jnp.sum(grad_out[:, None, :] * chosen, axis=-1)
    grad_chosen = gate_vals[..., None] * grad_out[:, None, :]
    grad_ffn_rows = (grad_chosen * is_ffn_f[..., None]).astype(jnp.bfloat16)
    grad_send = (
        jnp.zeros((n_ffn, cap_rows, feat_width), jnp.bfloat16)
        .at[expert_index, slot_ids]
        .set(grad_ffn_rows, mode="drop")
    )
    grad_arrived = lax.all_to_all(
        grad_send.reshape(n_exp, exp_dev * cap_rows, feat_width),
        "exp",
        split_axis=0,
        concat_axis=0,
        tiled=True,
    )
    grad_arrived = grad_arrived.reshape(n_exp, exp_dev, cap_rows, feat_width)
    gate_back, up_back, down_back = (
        lax.all_gather(w_gate, ("dp", "ctx"), axis=2, tiled=True),
        lax.all_gather(w_up, ("dp", "ctx"), axis=2, tiled=True),
        lax.all_gather(w_down, ("dp", "ctx"), axis=1, tiled=True),
    )
    grad_act = jnp.einsum(
        "secd,efd->secf", grad_arrived, down_back, preferred_element_type=jnp.float32
    )
    grad_gate_pre = (
        grad_act * up_pre * sigmoid_gate * (1.0 + gate_pre * (1.0 - sigmoid_gate))
    ).astype(jnp.bfloat16)
    grad_up_pre = (grad_act * silu_gate).astype(jnp.bfloat16)
    grad_down_w = jnp.einsum(
        "secf,secd->efd", act_vals, grad_arrived, preferred_element_type=jnp.float32
    )
    grad_gate_w = jnp.einsum(
        "secd,secf->edf", arrived, grad_gate_pre, preferred_element_type=jnp.float32
    )
    grad_up_w = jnp.einsum(
        "secd,secf->edf", arrived, grad_up_pre, preferred_element_type=jnp.float32
    )
    grad_in_rows = jnp.einsum(
        "secf,edf->secd", grad_gate_pre, gate_back, preferred_element_type=jnp.float32
    )
    grad_in_rows = (
        grad_in_rows
        + jnp.einsum("secf,edf->secd", grad_up_pre, up_back, preferred_element_type=jnp.float32)
    ).astype(jnp.bfloat16)
    grad_returned = lax.all_to_all(
        grad_in_rows.reshape(n_exp, exp_dev * cap_rows, feat_width),
        "exp",
        split_axis=0,
        concat_axis=0,
        tiled=True,
    )
    grad_returned = grad_returned.reshape(n_ffn, cap_rows, feat_width)
    expert_grads = (
        lax.psum_scatter(grad_gate_w, ("dp", "ctx"), scatter_dimension=2, tiled=True),
        lax.psum_scatter(grad_up_w, ("dp", "ctx"), scatter_dimension=2, tiled=True),
        lax.psum_scatter(grad_down_w, ("dp", "ctx"), scatter_dimension=1, tiled=True),
    )
    grad_hidden = jnp.sum(
        grad_returned[safe_index, slot_ids].astype(jnp.float32) * is_ffn_f[..., None], axis=1
    )
    grad_hidden = grad_hidden + jnp.sum(is_copy[..., None] * grad_chosen, axis=1)
    grad_const_rows = jnp.sum(pick_const[..., None] * grad_chosen[:, :, None, :], axis=1)
    grad_hidden = grad_hidden + jnp.sum(const_mix[..., 0:1] * grad_const_rows, axis=1)
    grad_mix_first = jnp.sum(grad_const_rows * hidden_f[:, None, :], axis=-1)
    grad_mix_second = jnp.sum(grad_const_rows * vectors[None], axis=-1)
    grad_vectors = jnp.sum(const_mix[..., 1:2] * grad_const_rows, axis=0)
    grad_mix = jnp.stack([grad_mix_first, grad_mix_second], axis=-1)
    grad_mix_logits = (
        const_mix * (grad_mix - jnp.sum(const_mix * grad_mix, axis=-1, keepdims=True))
    ).reshape(tok_rows, 4)
    grad_hidden = grad_hidden + jnp.dot(
        grad_mix_logits, jnp.transpose(full_const_gate.astype(jnp.float32)), precision=top_precision
    )
    grad_const_gate = jnp.dot(jnp.transpose(hidden_f), grad_mix_logits, precision=top_precision)
    grad_probs = jnp.sum(choose * grad_gates[:, :, None], axis=1)
    grad_logits = gate_probs * (
        grad_probs - jnp.sum(gate_probs * grad_probs, axis=-1, keepdims=True)
    )
    grad_hidden = grad_hidden + jnp.dot(
        grad_logits, jnp.transpose(full_router.astype(jnp.float32)), precision=top_precision
    )
    grad_router = jnp.dot(jnp.transpose(hidden_f), grad_logits, precision=top_precision)
    grad_mid_norm, grad_gain_two = rms_backward(mid_rows, scale_two, gain_ffn, grad_hidden)
    grad_mid = grad_out + grad_mid_norm
    grad_attn = grad_mid.astype(jnp.bfloat16)
    grad_w_out = jnp.dot(jnp.transpose(attended_low), grad_attn, preferred_element_type=jnp.float32)
    grad_attended = (
        jnp.dot(grad_attn, jnp.transpose(full_out), preferred_element_type=jnp.float32)
        .reshape(tok_rows, HEADS, head_size)
        .astype(jnp.bfloat16)
    )
    row_delta = jnp.transpose(jnp.sum(grad_attended.astype(jnp.float32) * attended, axis=-1))

    def query_part(blk_index):
        blk_scores, key_rows, value_rows = block_scores(blk_index)
        blk_probs = jnp.exp(blk_scores - log_total[..., None])
        grad_probs_blk = jnp.einsum(
            "qhd,khd->hqk", grad_attended, value_rows, preferred_element_type=jnp.float32
        )
        grad_scores = (blk_probs * (grad_probs_blk - row_delta[..., None])).astype(jnp.bfloat16)
        return (
            blk_probs,
            grad_scores,
            jnp.einsum("hqk,khd->qhd", grad_scores, key_rows, preferred_element_type=jnp.float32),
        )

    def backward_step(blk_index, loop_state):
        grad_queries, grad_key_rows, grad_value_rows = loop_state
        blk_probs, grad_scores, query_grad = query_part(blk_index)
        grad_queries = grad_queries + query_grad
        key_part = jnp.einsum(
            "hqk,qhd->khd", grad_scores, queries, preferred_element_type=jnp.float32
        ).reshape(KBLK, feat_width)
        value_part = jnp.einsum(
            "hqk,qhd->khd",
            blk_probs.astype(jnp.bfloat16),
            grad_attended,
            preferred_element_type=jnp.float32,
        ).reshape(KBLK, feat_width)
        blk_start = blk_index * KBLK
        grad_key_rows = lax.dynamic_update_slice_in_dim(
            grad_key_rows,
            lax.dynamic_slice_in_dim(grad_key_rows, blk_start, KBLK, 0) + key_part,
            blk_start,
            0,
        )
        grad_value_rows = lax.dynamic_update_slice_in_dim(
            grad_value_rows,
            lax.dynamic_slice_in_dim(grad_value_rows, blk_start, KBLK, 0) + value_part,
            blk_start,
            0,
        )
        return (grad_queries, grad_key_rows, grad_value_rows)

    back_state = (
        jnp.zeros((tok_rows, HEADS, head_size), jnp.float32),
        jnp.zeros((seq_rows, feat_width), jnp.float32),
        jnp.zeros((seq_rows, feat_width), jnp.float32),
    )
    grad_queries, grad_key_rows, grad_value_rows = lax.fori_loop(
        0, blk_count, backward_step, back_state
    )
    own_key_grads, own_value_grads = (
        lax.psum_scatter(
            grad_key_rows.astype(jnp.bfloat16), "ctx", scatter_dimension=0, tiled=True
        ).astype(jnp.float32),
        lax.psum_scatter(
            grad_value_rows.astype(jnp.bfloat16), "ctx", scatter_dimension=0, tiled=True
        ).astype(jnp.float32),
    )
    grad_q_rows = rotate(grad_queries * score_scale, positions, -1.0).reshape(tok_rows, feat_width)
    grad_k_rows = rotate(
        (own_key_grads * score_scale).reshape(tok_rows, HEADS, head_size), positions, -1.0
    ).reshape(tok_rows, feat_width)
    grad_qkv = jnp.concatenate([grad_q_rows, grad_k_rows, own_value_grads], axis=1).astype(
        jnp.bfloat16
    )
    grad_w_qkv = jnp.dot(jnp.transpose(hidden_one), grad_qkv, preferred_element_type=jnp.float32)
    grad_hidden_one = jnp.dot(grad_qkv, jnp.transpose(full_qkv), preferred_element_type=jnp.float32)
    grad_in_norm, grad_gain_one = rms_backward(in_rows, scale_one, gain_attn, grad_hidden_one)
    grad_x = grad_mid + grad_in_norm
    param_grads = (
        lax.psum_scatter(grad_w_qkv, ("dp", "ctx", "exp"), scatter_dimension=0, tiled=True),
        lax.psum_scatter(grad_w_out, ("dp", "ctx", "exp"), scatter_dimension=0, tiled=True),
        lax.psum_scatter(grad_gain_one, ("dp", "ctx", "exp"), scatter_dimension=0, tiled=True),
        lax.psum_scatter(grad_gain_two, ("dp", "ctx", "exp"), scatter_dimension=0, tiled=True),
        lax.psum_scatter(grad_router, ("dp", "ctx", "exp"), scatter_dimension=0, tiled=True),
        lax.psum_scatter(grad_const_gate, ("dp", "ctx", "exp"), scatter_dimension=0, tiled=True),
        lax.psum_scatter(
            jnp.transpose(grad_vectors), ("dp", "ctx", "exp"), scatter_dimension=0, tiled=True
        ),
    )
    return (
        output[None],
        grad_x[None],
        param_grads[0],
        param_grads[1],
        param_grads[2],
        param_grads[3],
        param_grads[4],
        param_grads[5],
        param_grads[6],
        expert_grads[0],
        expert_grads[1],
        expert_grads[2],
    )


def solution(mesh):
    in_specs = (
        P(("dp", "exp"), "ctx", None),
        P(("dp", "exp")),
        P(("dp", "exp"), "ctx", None),
        P(("dp", "exp"), "ctx", None),
        P(("dp", "exp"), "ctx", None),
        P(("dp", "ctx", "exp"), None),
        P(("dp", "ctx", "exp"), None),
        P(("dp", "ctx", "exp")),
        P(("dp", "ctx", "exp")),
        P(("dp", "ctx", "exp"), None),
        P(("dp", "ctx", "exp"), None),
        P(("dp", "ctx", "exp"), None),
        P("exp", None, ("dp", "ctx")),
        P("exp", None, ("dp", "ctx")),
        P("exp", ("dp", "ctx"), None),
    )
    out_specs = (
        P(("dp", "exp"), "ctx", None),
        P(("dp", "exp"), "ctx", None),
        P(("dp", "ctx", "exp"), None),
        P(("dp", "ctx", "exp"), None),
        P(("dp", "ctx", "exp")),
        P(("dp", "ctx", "exp")),
        P(("dp", "ctx", "exp"), None),
        P(("dp", "ctx", "exp"), None),
        P(("dp", "ctx", "exp"), None),
        P("exp", None, ("dp", "ctx")),
        P("exp", None, ("dp", "ctx")),
        P("exp", ("dp", "ctx"), None),
    )
    return jax.shard_map(local, mesh=mesh, in_specs=in_specs, out_specs=out_specs, check_vma=False)
```

profile of v0, /device:TPU:0, one launch (start us, length us, event | category | flops | bytes accessed | tf_op | source)
XLA Modules:
  0.0 1749.4 jit_solution(1715870992530106072)
XLA Ops:
  9.7 42.1 %all-reduce.8 = (bf16[768]{0:T(1024)(128)(2,1)S(1)}, bf16[768]{0:T(1024)(128)(2,1)S(1)}) all-reduce(bf16[768]{0:T(1024)(128)(2,1)S(1)} %dynamic-update-slice, bf16[768]{0:T(1024)(128)(2,1)S(1)} %dynamic-update-slice.1), channel_id=1, replica_groups=mesh['dp'=8,'ctx'=2,'exp'=2] {'dp','ctx','exp'}, use_global_device_ids=true, to_apply=%add | all-reduce | flops 1536 | bytes 6144
  54.1 19.7 %all-gather.11.cloned.1.call-done = bf16[768,2304]{1,0:T(8,128)(2,1)} async-done(((bf16[24,2304]{1,0:T(8,128)(2,1)}), bf16[768,2304]{1,0:T(8,128)(2,1)}) %all-gather.11.cloned.1.call-update) | async-done | bytes 3538960 | tf_op jit(solution)/shard_map/all_gather | solution.py:85
  73.8 4.5 copy.222
  98.4 67.4 %all-gather = bf16[32,24,12]{1,2,0:T(8,128)(2,1)S(1)} all-gather(bf16[1,24,12]{1,2,0:T(8,128)(2,1)S(1)} %bitcast.374), channel_id=1, replica_groups=mesh['dp'=8,'ctx'=2,'exp'=2] {'dp','ctx','exp'}, dimensions={0}, use_global_device_ids=true | all-gather | bytes 19008 | tf_op jit(solution)/shard_map/all_gather | solution.py:89
  166.2 63.6 %all-gather.1 = bf16[32,24,4]{1,2,0:T(4,128)(2,1)S(1)} all-gather(bf16[1,24,4]{1,2,0:T(4,128)(2,1)S(1)} %bitcast.375), channel_id=1, replica_groups=mesh['dp'=8,'ctx'=2,'exp'=2] {'dp','ctx','exp'}, dimensions={0}, use_global_device_ids=true | all-gather | bytes 6336 | tf_op jit(solution)/shard_map/all_gather | solution.py:90
  229.9 65.9 %all-gather.2 = bf16[32,24,2]{1,2,0:T(2,128)(2,1)S(1)} all-gather(bf16[1,24,2]{1,2,0:T(2,128)(2,1)S(1)} %bitcast.376), channel_id=1, replica_groups=mesh['dp'=8,'ctx'=2,'exp'=2] {'dp','ctx','exp'}, dimensions={0}, use_global_device_ids=true | all-gather | bytes 3168 | tf_op jit(solution)/shard_map/all_gather | solution.py:91
  300.2 12.4 while.30
  304.7 5.3 bitcast_add_fusion.6
  321.1 7.4 scatter_custom_fusion
  328.5 3.7 all-to-all-start
  338.9 4.7 reshape.522
  343.9 7.0 scatter_custom_fusion.1
  351.0 4.7 all-to-all-start.2
  355.7 10.4 fusion.26
  366.1 41.5 %all-gather.19.cloned.1.call-done = bf16[4,768,2048]{2,1,0:T(8,128)(2,1)} async-done(((bf16[4,768,128]{2,1,0:T(8,128)(2,1)}), bf16[4,768,2048]{2,1,0:T(8,128)(2,1)}) %all-gather.19.cloned.1.call-update) | async-done | bytes 12582928 | tf_op jit(solution)/shard_map/all_gather | solution.py:190
  407.7 10.3 fusion.30
  418.0 91.0 %all-gather.23.cloned.1.call-done = bf16[4,2048,768]{2,1,0:T(8,128)(2,1)} async-done(((bf16[4,128,768]{2,1,0:T(8,128)(2,1)}), bf16[4,2048,768]{2,1,0:T(8,128)(2,1)}) %all-gather.23.cloned.1.call-update) | async-done | bytes 12582928 | tf_op jit(solution)/shard_map/all_gather | solution.py:192
  509.0 16.7 fusion.38
  525.7 11.0 fusion.24
  536.7 10.1 fusion.72
  548.1 3.7 all-to-all-start.3
  551.8 9.3 fusion.75
  562.3 9.4 all-to-all-done.3
  571.7 4.6 all-to-all-start.1
  578.8 4.4 multiply_reduce_fusion
  583.2 14.0 gather_fusion.1
  597.2 4.9 reshape.527
  602.0 19.8 %gather_fusion = bf16[1024,768]{1,0:T(8,128)(2,1)} fusion(bf16[8,128,768]{2,1,0:T(8,128)(2,1)} %bitcast.30, s32[1024]{0:T(1024)S(1)} %reshape.502), kind=kCustom, calls=%fused_computation | custom fusion | bytes 3153920 | tf_op jit(solution)/shard_map/gather | solution.py:210
  621.8 5.0 reshape.526
  626.8 10.5 multiply_reduce_fusion.2
  639.0 4.6 multiply_reduce_fusion.9
  653.6 29.3 %while.31 = (s32[]{:T(128)}, f32[512,12,64]{0,2,1:T(8,128)S(1)}, f32[1024,768]{0,1:T(8,128)}, f32[1024,768]{0,1:T(8,128)}, s32[]{:T(128)}, /*index=5*/bf16[1024,...) while((s32[]{:T(128)}, f32[512,12,64]{0,2,1:T(8,128)S(1)}, ...), condition=%wide.region_31.32_spmd.clone, body=%wide.region_30.31_spmd.clone.sunk | while | flops 2046429184 | bytes 88163584 | solution.py:370
  654.9 6.4 fusion.196
  662.3 7.0 fusion.197
  671.3 6.2 fusion.198
  677.5 4.1 constant_dynamic-update-slice_fusion.3
  695.8 44.6 %reduce-scatter.11.cloned.1.call-done = bf16[512,768]{0,1:T(8,128)(2,1)} async-done(((bf16[1024,768]{0,1:T(8,128)(2,1)}), bf16[512,768]{0,1:T(8,128)(2,1)}) %reduce-scatter.11.cloned.1.call-update) | async-done | bytes 786448 | tf_op jit(solution)/shard_map/reduce_scatter | solution.py:374
  742.5 26.9 %reduce-scatter.13.cloned.1.call-done = bf16[512,768]{0,1:T(8,128)(2,1)} async-done(((bf16[1024,768]{0,1:T(8,128)(2,1)}), bf16[512,768]{0,1:T(8,128)(2,1)}) %reduce-scatter.13.cloned.1.call-update) | async-done | bytes 786448 | tf_op jit(solution)/shard_map/reduce_scatter | solution.py:377
  769.5 6.4 fusion.82
  776.0 14.8 convolution_bitcast_fusion
  792.2 12.6 convolution_bitcast_fusion.2
  805.1 12.5 convolution_bitcast_fusion.1
  819.5 6.0 fusion.68
  825.6 40.9 %all-reduce.7 = (f32[768]{0:T(1024)S(1)}, f32[768]{0:T(1024)S(1)}, f32[768,12]{0,1:T(8,128)S(1)}, f32[768,4]{0,1:T(4,128)S(1)}, f32[768,2]{0,1:T(2,128)S(1)}) all-reduce(f32[768]{0:T(1024)S(1)} %get-tuple-element.218, f32[768]{0:T(1024)S(1)} %copy-done.38, ...), channel_id=6, replica_groups=mesh['dp'=8,'ctx'=2,'exp'=2] {'dp','ctx','exp'}, use_global_device_ids=true, to_apply=%region_38.39.clone | all-reduce | flops 15360 | bytes 122880
  874.4 125.4 %reduce-scatter.15.cloned.1.call-done = f32[24,2304]{1,0:T(8,128)} async-done(((f32[768,2304]{1,0:T(8,128)}), f32[24,2304]{1,0:T(8,128)}) %reduce-scatter.15.cloned.1.call-update) | async-done | bytes 221200 | tf_op jit(solution)/shard_map/reduce_scatter | solution.py:393
  999.8 247.6 %reduce-scatter.23.cloned.1.call-done = f32[4,128,768]{2,1,0:T(8,128)} async-done(((f32[4,2048,768]{2,1,0:T(8,128)}), f32[4,128,768]{2,1,0:T(8,128)}) %reduce-scatter.23.cloned.1.call-update) | async-done | bytes 1572880 | tf_op jit(solution)/shard_map/reduce_scatter | solution.py:286
  1247.4 247.7 %reduce-scatter.19.cloned.1.call-done = f32[4,768,128]{2,1,0:T(8,128)} async-done(((f32[4,768,2048]{2,1,0:T(8,128)}), f32[4,768,128]{2,1,0:T(8,128)}) %reduce-scatter.19.cloned.1.call-update) | async-done | bytes 1572880 | tf_op jit(solution)/shard_map/reduce_scatter | solution.py:284
  1495.1 247.6 %reduce-scatter.21.cloned.1.call-done = f32[4,768,128]{2,1,0:T(8,128)} async-done(((f32[4,768,2048]{2,1,0:T(8,128)}), f32[4,768,128]{2,1,0:T(8,128)}) %reduce-scatter.21.cloned.1.call-update) | async-done | bytes 1572880 | tf_op jit(solution)/shard_map/reduce_scatter | solution.py:285
  (272 shorter events, 99.3 us)
Async XLA Ops:
  7.2 66.7 %all-gather.11.cloned.1.call-start = ((), (), s32[]{:S(2)}) async-start(), calls=%async_computation.11 | async-start | bytes 3649536 | tf_op jit(solution)/shard_map/all_gather | solution.py:85
  7.9 290.3 %all-gather.13.cloned.1.call-start = ((), (), s32[]{:S(2)}) async-start(), calls=%async_computation.12 | async-start | bytes 2359296 | tf_op jit(solution)/shard_map/all_gather | solution.py:109
  51.8 26.6 %copy-start.39 = (f32[768]{0:T(1024)}, f32[768]{0:T(1024)S(1)}, u32[]{:S(2)}) copy-start(f32[768]{0:T(1024)S(1)} %convert_element_type.160) | copy-start | bytes 9220
  53.1 25.2 %copy-start.42 = (f32[512]{0:T(512)}, f32[512]{0:T(512)S(1)}, u32[]{:S(2)}) copy-start(f32[512]{0:T(512)S(1)} %add_rsqrt_fusion.1) | copy-start | bytes 6148
  85.5 212.8 %all-gather.15.cloned.1.call-start = ((), (), s32[]{:S(2)}) async-start(), calls=%async_computation.13 | async-start | bytes 2359296 | tf_op jit(solution)/shard_map/all_gather | solution.py:110
  88.0 226.4 %all-gather.17.cloned.1.call-start = ((), (), s32[]{:S(2)}) async-start(), calls=%async_computation.14 | async-start | bytes 1216512 | tf_op jit(solution)/shard_map/all_gather | solution.py:86
  88.5 267.2 %all-gather.21.cloned.1.call-start = ((), (), s32[]{:S(2)}) async-start(), calls=%async_computation.16 | async-start | bytes 13369344 | tf_op jit(solution)/shard_map/all_gather | solution.py:191
  89.1 318.5 %all-gather.19.cloned.1.call-start = ((), (), s32[]{:S(2)}) async-start(), calls=%async_computation.15 | async-start | bytes 13369344 | tf_op jit(solution)/shard_map/all_gather | solution.py:190
  89.7 419.3 %all-gather.23.cloned.1.call-start = ((), (), s32[]{:S(2)}) async-start(), calls=%async_computation.17 | async-start | bytes 13369344 | tf_op jit(solution)/shard_map/all_gather | solution.py:192
  91.4 6.4 copy-start.47
  91.5 6.5 copy-start.48
  95.8 70.4 %copy-start.45 = (bf16[24,4]{0,1:T(4,128)(2,1)S(1)}, bf16[24,4]{0,1:T(4,128)(2,1)}, u32[]{:S(2)}) copy-start(bf16[24,4]{0,1:T(4,128)(2,1)} %param.29) | copy-start | bytes 580
  95.8 134.2 %copy-start.46 = (bf16[24,2]{0,1:T(2,128)(2,1)S(1)}, bf16[24,2]{0,1:T(2,128)(2,1)}, u32[]{:S(2)}) copy-start(bf16[24,2]{0,1:T(2,128)(2,1)} %param.30) | copy-start | bytes 292
  95.8 201.1 %copy-start.14 = (f32[1,512,768]{2,1,0:T(8,128)S(1)}, f32[1,512,768]{2,1,0:T(8,128)}, u32[]{:S(2)}) copy-start(f32[1,512,768]{2,1,0:T(8,128)} %param.23) | copy-start | bytes 4718596
  318.8 24.8 %copy-start.4 = (bf16[512,768]{1,0:T(8,128)(2,1)}, bf16[512,768]{1,0:T(8,128)(2,1)S(1)}, u32[]{:S(2)}) copy-start(bf16[512,768]{1,0:T(8,128)(2,1)S(1)} %get-tuple-element.283) | copy-start | bytes 2359300
  328.5 3.7 copy-start.32
  328.5 22.5 %all-to-all-start = ((bf16[2,512,768]{2,1,0:T(8,128)(2,1)}), bf16[2,512,768]{2,1,0:T(8,128)(2,1)S(1)}, u32[]{:S(2)}, u32[]{:S(2)}) async-start(bf16[2,512,768]{2,1,0:T(8,128)(2,1)} %bitcast.344), calls=%async_computation | async-start | bytes 3145728 | tf_op jit(solution)/shard_map/all_to_all | solution.py:181
  332.6 306.3 %copy-start.23 = (f32[512,12]{0,1:T(8,128)}, f32[512,12]{0,1:T(8,128)S(1)}, u32[]{:S(2)}) copy-start(f32[512,12]{0,1:T(8,128)S(1)} %fusion.106) | copy-start | bytes 73732
  351.0 56.6 %copy-start.2 = (bf16[2,512,768]{2,1,0:T(8,128)(2,1)}, bf16[2,512,768]{2,1,0:T(8,128)(2,1)S(1)}, u32[]{:S(2)}) copy-start(bf16[2,512,768]{2,1,0:T(8,128)(2,1)S(1)} %all-to-all-done) | copy-start | bytes 4718596
  351.0 67.0 %all-to-all-start.2 = ((bf16[2,512,768]{2,1,0:T(8,128)(2,1)}), bf16[2,512,768]{2,1,0:T(8,128)(2,1)}, u32[]{:S(2)}, u32[]{:S(2)}) async-start(bf16[2,512,768]{2,1,0:T(8,128)(2,1)} %bitcast.345), calls=%async_computation.2 | async-start | bytes 3145728 | tf_op jit(solution)/shard_map/all_to_all | solution.py:239
  548.1 23.6 %all-to-all-start.3 = ((bf16[2,512,768]{2,1,0:T(8,128)(2,1)}), bf16[2,512,768]{2,1,0:T(8,128)(2,1)S(1)}, u32[]{:S(2)}, u32[]{:S(2)}) async-start(bf16[2,512,768]{2,1,0:T(8,128)(2,1)} %bitcast.346), calls=%async_computation.3 | async-start | bytes 3145728 | tf_op jit(solution)/shard_map/all_to_all | solution.py:275
  571.7 30.4 %all-to-all-start.1 = ((bf16[2,512,768]{2,1,0:T(8,128)(2,1)}), bf16[2,512,768]{2,1,0:T(8,128)(2,1)}, u32[]{:S(2)}, u32[]{:S(2)}) async-start(bf16[2,512,768]{2,1,0:T(8,128)(2,1)} %bitcast.343), calls=%async_computation.1 | async-start | bytes 3145728 | tf_op jit(solution)/shard_map/all_to_all | solution.py:202
  576.3 164.1 %reduce-scatter.11.cloned.1.call-start = ((), (), s32[]{:S(2)}) async-start(), calls=%async_computation.18 | async-start | bytes 2359296 | tf_op jit(solution)/shard_map/reduce_scatter | solution.py:374
  621.8 5.0 copy-start.6
  621.8 5.0 copy-start.41
  637.3 6.2 copy-start.25
  637.4 6.2 copy-start.34
  638.1 5.5 copy-start.30
  638.9 4.6 copy-start.13
  638.9 4.6 copy-start.15
  639.0 4.6 copy-start.37
  654.9 6.4 copy-start.1
  686.2 83.2 %reduce-scatter.13.cloned.1.call-start = ((), (), s32[]{:S(2)}) async-start(), calls=%async_computation.19 | async-start | bytes 2359296 | tf_op jit(solution)/shard_map/reduce_scatter | solution.py:377
  689.6 184.8 %reduce-scatter.17.cloned.1.call-start = ((), (), s32[]{:S(2)}) async-start(), calls=%async_computation.21 | async-start | bytes 2433024 | tf_op jit(solution)/shard_map/reduce_scatter | solution.py:394
  694.3 305.5 %reduce-scatter.15.cloned.1.call-start = ((), (), s32[]{:S(2)}) async-start(), calls=%async_computation.20 | async-start | bytes 7299072 | tf_op jit(solution)/shard_map/reduce_scatter | solution.py:393
  695.8 46.0 %copy-start.12 = (f32[512,12,64]{0,2,1:T(8,128)S(1)}, f32[512,12,64]{0,2,1:T(8,128)}, u32[]{:S(2)}) copy-start(f32[512,12,64]{0,2,1:T(8,128)} %broadcast_multiply_fusion.1) | copy-start | bytes 4718596
  695.8 46.0 %copy-start.22 = (f32[512,32]{0,1:T(8,128)S(1)}, f32[512,32]{0,1:T(8,128)}, u32[]{:S(2)}) copy-start(f32[512,32]{0,1:T(8,128)} %get-tuple-element.322) | copy-start | bytes 196612
  695.8 46.0 %copy-start.27 = (f32[512,32]{0,1:T(8,128)S(1)}, f32[512,32]{0,1:T(8,128)}, u32[]{:S(2)}) copy-start(f32[512,32]{0,1:T(8,128)} %get-tuple-element.320) | copy-start | bytes 196612
  742.3 27.1 %copy-start.19 = (bf16[1,512,768]{2,1,0:T(8,128)(2,1)S(1)}, bf16[1,512,768]{2,1,0:T(8,128)(2,1)}, u32[]{:S(2)}) copy-start(bf16[1,512,768]{2,1,0:T(8,128)(2,1)} %param.19) | copy-start | bytes 2359300
  742.3 27.1 %copy-start.40 = (f32[768]{0:T(1024)S(1)}, f32[768]{0:T(1024)}, u32[]{:S(2)}) copy-start(f32[768]{0:T(1024)} %copy-done.39) | copy-start | bytes 9220
  742.4 27.1 %copy-start.43 = (f32[512]{0:T(512)S(1)}, f32[512]{0:T(512)}, u32[]{:S(2)}) copy-start(f32[512]{0:T(512)} %copy-done.42) | copy-start | bytes 6148
  742.5 33.3 %copy-start.20 = (bf16[512,12,64]{0,2,1:T(8,128)(2,1)}, bf16[512,12,64]{0,2,1:T(8,128)(2,1)S(1)}, u32[]{:S(2)}) copy-start(bf16[512,12,64]{0,2,1:T(8,128)(2,1)S(1)} %pad_maximum_fusion.6) | copy-start | bytes 2359300
  775.9 471.5 %reduce-scatter.23.cloned.1.call-start = ((), (), s32[]{:S(2)}) async-start(), calls=%async_computation.24 | async-start | bytes 26738688 | tf_op jit(solution)/shard_map/reduce_scatter | solution.py:286
  790.8 704.3 %reduce-scatter.19.cloned.1.call-start = ((), (), s32[]{:S(2)}) async-start(), calls=%async_computation.22 | async-start | bytes 26738688 | tf_op jit(solution)/shard_map/reduce_scatter | solution.py:284
  804.8 937.9 %reduce-scatter.21.cloned.1.call-start = ((), (), s32[]{:S(2)}) async-start(), calls=%async_computation.23 | async-start | bytes 26738688 | tf_op jit(solution)/shard_map/reduce_scatter | solution.py:285
  819.5 6.1 copy-start.33
  819.5 6.1 copy-start.38
  819.5 50.1 %copy-start.10 = (f32[512,768]{1,0:T(8,128)S(1)}, f32[512,768]{1,0:T(8,128)}, u32[]{:S(2)}) copy-start(f32[512,768]{1,0:T(8,128)} %copy-done.9) | copy-start | bytes 4718596
  (20 other events, 38.5 us)
Sparse Core Ops, SparseCore 0:
  10.9 62.8 all-gather.10
  85.6 26.2 all-gather.12
  114.0 27.6 all-gather.14
  144.4 54.0 all-gather.16
  200.5 103.0 all-gather.20
  305.5 102.0 all-gather.18
  410.0 98.9 all-gather.22
  686.4 54.0 reduce-scatter.10
  743.4 26.0 reduce-scatter.12
  775.2 99.2 reduce-scatter.16
  881.6 118.1 reduce-scatter.14
  1004.3 243.0 reduce-scatter.22
  1252.1 242.9 reduce-scatter.18
  1499.6 242.9 reduce-scatter.20
where the time goes:
time: 1760 us; the launch traced here: 1750 us
  waiting for transfers between devices  1110 us (63%)
  blocking collectives  280 us (16%)
  matrix products  168 us (10%)
  local copies, waits for them, and re-layouts  102 us (6%)
  other arithmetic  59.3 us (3%)
    reduce_scatter x1, waiting for transfers between devices, local(): lax.psum_scatter(grad_gate_w, ('dp', 'ctx'), scatter_dimension=2, tiled=T...  248 us
    reduce_scatter x1, waiting for transfers between devices, local(): lax.psum_scatter(grad_down_w, ('dp', 'ctx'), scatter_dimension=1, tiled=T...  248 us
    reduce_scatter x1, waiting for transfers between devices, local(): lax.psum_scatter(grad_up_w, ('dp', 'ctx'), scatter_dimension=2, tiled=True)  248 us
    reduce_scatter x1, waiting for transfers between devices, local(): lax.psum_scatter(grad_w_qkv, ('dp', 'ctx', 'exp'), scatter_dimension=0, t...  125 us
    all_gather x1, waiting for transfers between devices, local(): lax.all_gather(w_down, ('dp', 'ctx'), axis=1, tiled=True)  91 us
    unnamed x2, blocking collectives  83 us
    all_gather x1, blocking collectives, local(): lax.all_gather(router, ('dp', 'ctx', 'exp'), axis=0, tiled=True)  67.4 us
    all_gather x1, blocking collectives, local(): lax.all_gather(const_vec, ('dp', 'ctx', 'exp'), axis=0, tiled=True)  65.9 us
  transfers between devices with their start and end apart: 18, of which 11 were waited for; matrix products, arithmetic and copies ran while one was open for 11% of the time, Pallas kernels for 0%

commit v1 on v0

v1 whole, which is shorter than its diff:
```python
import jax
import jax.numpy as jnp
from jax import lax
from jax.sharding import PartitionSpec as P

HEADS = 12
KBLK = 512

norm_eps = 1e-06
top_precision = lax.Precision.HIGHEST
f32 = jnp.float32
bf16 = jnp.bfloat16


def dot32(a, b, dims=((1,), (0,)), precision=None):
    return lax.dot_general(a, b, (dims, ((), ())), precision=precision, preferred_element_type=f32)


def swap(block, axis, bit):
    return lax.ppermute(block, axis, [(i, i ^ bit) for i in range(lax.axis_size(axis))])


def bits_of(axis, low=1, high=None):
    high = lax.axis_size(axis) if high is None else high
    found = []
    while low < high:
        found.append(low)
        low *= 2
    return found[::-1]


def row_weight(axis):
    x = lax.axis_size("exp")
    c = lax.axis_size("ctx")
    return {"exp": 1, "ctx": x, "dp": x * c}[axis]


def plan_steps(middle):
    far = [("dp", bit) for bit in bits_of("dp", 2)]
    mid = [(axis, bit) for axis in middle for bit in bits_of(axis)]
    near = [("dp", bit) for bit in bits_of("dp", 1, 2)]
    return far + mid + near


def gather_rows(block, steps):
    placed = []
    shape = block.shape
    whole = block
    for axis, bit in steps:
        other = swap(whole, axis, bit)
        upper = (lax.axis_index(axis) & bit) != 0
        weight = row_weight(axis) * bit
        pos = sum(1 for w in placed if w > weight)
        whole = jnp.stack(
            [jnp.where(upper, other, whole), jnp.where(upper, whole, other)], axis=pos
        )
        placed.insert(pos, weight)
    return whole.reshape((-1,) + shape[1:])


def scatter_rows(whole, steps):
    placed = sorted([row_weight(axis) * bit for axis, bit in steps], reverse=True)
    part = whole.reshape((2,) * len(placed) + (-1,) + whole.shape[1:])
    for axis, bit in reversed(steps):
        pos = placed.index(row_weight(axis) * bit)
        upper = (lax.axis_index(axis) & bit) != 0
        low = lax.index_in_dim(part, 0, pos, keepdims=False)
        high = lax.index_in_dim(part, 1, pos, keepdims=False)
        sent = jnp.where(upper, low, high).astype(bf16)
        part = jnp.where(upper, high, low).astype(f32) + swap(sent, axis, bit).astype(f32)
        placed.pop(pos)
    return part


def gather_expert(shards, ff_axis):
    n_own = shards.shape[0]
    reps = lax.axis_size("dp") // n_own
    mine = lax.axis_index("dp") // reps
    pieces = [lax.dynamic_index_in_dim(shards, mine, 0, keepdims=False)]
    for k in range(1, n_own):
        sent = lax.dynamic_index_in_dim(shards, mine ^ k, 0, keepdims=False)
        pieces.append(swap(sent, "dp", reps * k))
    whole = jnp.concatenate(pieces, axis=ff_axis)
    for bit in bits_of("ctx"):
        whole = jnp.concatenate([whole, swap(whole, "ctx", bit)], axis=ff_axis)
    for bit in bits_of("dp", 1, reps):
        whole = jnp.concatenate([whole, swap(whole, "dp", bit)], axis=ff_axis)
    return whole


def scatter_expert(grad, n_own, ff_axis):
    reps = lax.axis_size("dp") // n_own
    mine = lax.axis_index("dp") // reps
    steps = [("ctx", bit) for bit in bits_of("ctx")] + [("dp", bit) for bit in bits_of("dp", 1, reps)]
    for axis, bit in reversed(steps):
        keep, sent = jnp.split(grad, 2, axis=ff_axis)
        grad = keep.astype(f32) + swap(sent.astype(bf16), axis, bit).astype(f32)
    pieces = jnp.split(grad, n_own, axis=ff_axis)
    back = [pieces[0].astype(f32)]
    for k in range(1, n_own):
        back.append(swap(pieces[k].astype(bf16), "dp", reps * k).astype(f32))
    bit = 1
    while bit < n_own:
        flip = (mine & bit) != 0
        back = [jnp.where(flip, back[i ^ bit], back[i]) for i in range(n_own)]
        bit *= 2
    return jnp.stack(back)


def rms_scale(rows):
    return lax.rsqrt(jnp.mean(rows * rows, axis=-1, keepdims=True) + norm_eps)


def rms_backward(in_rows, inv_scale, gain_vec, grad_rows):
    normed = in_rows * inv_scale
    gain_grad = jnp.sum(grad_rows * normed, axis=0)
    inner_grad = grad_rows * gain_vec
    back_rows = inv_scale * (
        inner_grad - normed * jnp.mean(inner_grad * normed, axis=-1, keepdims=True)
    )
    return (back_rows, gain_grad)


def rotate(in_rows, positions, sign_value):
    half_size = in_rows.shape[-1] // 2
    inv_freq = 10000.0 ** (-2.0 * jnp.arange(half_size, dtype=f32) / in_rows.shape[-1])
    angles = positions.astype(f32)[:, None] * inv_freq[None, :]
    cosine = jnp.cos(angles)[:, None, :]
    sine_part = sign_value * jnp.sin(angles)[:, None, :]
    first_half = in_rows[..., :half_size]
    second_half = in_rows[..., half_size:]
    return jnp.concatenate(
        [
            first_half * cosine - second_half * sine_part,
            second_half * cosine + first_half * sine_part,
        ],
        axis=-1,
    )


def local(
    residual_in,
    lengths,
    routes,
    prev_logits,
    cotangent,
    w_qkv,
    w_out,
    attn_gain,
    ffn_gain,
    router,
    const_gate,
    const_vec,
    w_gate,
    w_up,
    w_down,
):
    tok_rows = residual_in.shape[1]
    feat = residual_in.shape[2]
    head_size = feat // HEADS
    score_scale = head_size ** (-0.5)
    n_dp = lax.axis_size("dp")
    n_ctx = lax.axis_size("ctx")
    n_exp = lax.axis_size("exp")
    own_exp = w_gate.shape[0]
    reps = n_dp // own_exp
    n_all = router.shape[1]
    n_ffn = n_all - 4
    cap_rows = tok_rows // 4
    sub_rows = cap_rows // reps
    n_slots = n_ffn * cap_rows
    ctx_rank = lax.axis_index("ctx")
    positions = ctx_rank * tok_rows + jnp.arange(tok_rows, dtype=jnp.int32)
    length = lengths[0]
    valid_rows = (positions < length).astype(f32)[:, None]
    in_rows = residual_in[0].astype(f32)
    grad_out = cotangent[0] * valid_rows

    steps_a = plan_steps(("ctx", "exp"))
    steps_b = plan_steps(("exp", "ctx"))
    small = jnp.concatenate(
        [router, const_gate, const_vec, attn_gain[:, None], ffn_gain[:, None]], axis=1
    )
    small = jnp.pad(small, ((0, 0), (0, 128 - small.shape[1])))
    key_pack = gather_rows(jnp.concatenate([w_qkv[:, feat : 2 * feat], small], axis=1), steps_a)
    full_v = gather_rows(w_qkv[:, 2 * feat :], steps_b)
    full_q = gather_rows(w_qkv[:, :feat], steps_a)
    full_out = gather_rows(w_out, steps_b)
    full_k = key_pack[:, :feat]
    small = key_pack[:, feat:]
    full_router = small[:, :n_all]
    full_cg = small[:, n_all : n_all + 4]
    full_cv = small[:, n_all + 4 : n_all + 6]
    gain_attn = small[:, n_all + 6].astype(f32)
    gain_ffn = small[:, n_all + 7].astype(f32)

    route_ids = routes[0]
    choose = (route_ids[:, :, None] == jnp.arange(n_all, dtype=jnp.int32)[None, None, :]).astype(f32)
    both = jnp.sum(choose, axis=1)
    before = jnp.arange(tok_rows)
    before = (before[None, :] < before[:, None]).astype(bf16)
    counts = dot32(before, both.astype(bf16))
    slot_ids = jnp.sum(choose * counts[:, None, :], axis=-1).astype(jnp.int32)
    is_ffn = route_ids < n_ffn
    place = (
        ((route_ids % own_exp) * reps + slot_ids // sub_rows) * n_exp + route_ids // own_exp
    ) * sub_rows + slot_ids % sub_rows
    place = jnp.where(is_ffn, place, -1)
    row_ids = jnp.arange(n_slots, dtype=jnp.int32)
    hit = [row_ids[:, None] == place[None, :, j] for j in range(2)]
    spread = (hit[0] | hit[1]).astype(bf16)
    pick = [(place[:, j][:, None] == row_ids[None, :]).astype(bf16) for j in range(2)]

    def to_experts(rows):
        return lax.all_to_all(
            rows.reshape(n_dp * n_exp, sub_rows, -1),
            ("dp", "exp"),
            split_axis=0,
            concat_axis=0,
            tiled=True,
        ).reshape(n_slots, -1)

    grad_rows_in = to_experts(dot32(spread, grad_out.astype(bf16)).astype(bf16))

    scale_one = rms_scale(in_rows)
    hidden_one = (in_rows * scale_one * gain_attn).astype(bf16)

    def heads_of(rows):
        return rows.reshape(tok_rows, HEADS, head_size)

    own_keys = (
        rotate(heads_of(dot32(hidden_one, full_k)), positions, 1.0)
        .astype(bf16)
        .reshape(tok_rows, feat)
    )
    own_values = dot32(hidden_one, full_v).astype(bf16)
    queries = rotate(heads_of(dot32(hidden_one, full_q)), positions, 1.0).astype(bf16)

    def gather_ctx(rows):
        for bit in reversed(bits_of("ctx")):
            other = swap(rows, "ctx", bit)
            upper = (ctx_rank & bit) != 0
            rows = jnp.concatenate([jnp.where(upper, other, rows), jnp.where(upper, rows, other)], axis=0)
        return rows

    def scatter_ctx(rows):
        for bit in bits_of("ctx"):
            low, high = jnp.split(rows, 2, axis=0)
            upper = (ctx_rank & bit) != 0
            sent = jnp.where(upper, low, high).astype(bf16)
            rows = jnp.where(upper, high, low) + swap(sent, "ctx", bit).astype(f32)
        return rows

    all_keys = gather_ctx(own_keys)
    all_values = gather_ctx(own_values)
    key_count = jnp.minimum((ctx_rank + 1) * tok_rows, length)
    blk_count = (key_count + KBLK - 1) // KBLK

    def block_scores(blk_index):
        blk_start = blk_index * KBLK
        key_rows = lax.dynamic_slice_in_dim(all_keys, blk_start, KBLK, 0).reshape(
            KBLK, HEADS, head_size
        )
        value_rows = lax.dynamic_slice_in_dim(all_values, blk_start, KBLK, 0).reshape(
            KBLK, HEADS, head_size
        )
        key_pos = blk_start + jnp.arange(KBLK, dtype=jnp.int32)
        allowed = (key_pos[None, :] <= positions[:, None]) & (key_pos[None, :] < length)
        raw_scores = (
            jnp.einsum("qhd,khd->hqk", queries, key_rows, preferred_element_type=f32) * score_scale
        )
        return (jnp.where(allowed[None], raw_scores, -1e30), key_rows, value_rows)

    def forward_step(blk_index, loop_state):
        run_max, run_total, run_acc = loop_state
        blk_scores, key_rows, value_rows = block_scores(blk_index)
        new_max = jnp.maximum(run_max, jnp.max(blk_scores, axis=-1))
        expo_vals = jnp.exp(blk_scores - new_max[..., None])
        factor = jnp.exp(run_max - new_max)
        run_total = run_total * factor + jnp.sum(expo_vals, axis=-1)
        run_acc = run_acc * jnp.transpose(factor)[:, :, None] + jnp.einsum(
            "hqk,khd->qhd", expo_vals.astype(bf16), value_rows, preferred_element_type=f32
        )
        return (new_max, run_total, run_acc)

    start_state = (
        jnp.full((HEADS, tok_rows), -1e30, f32),
        jnp.zeros((HEADS, tok_rows), f32),
        jnp.zeros((tok_rows, HEADS, head_size), f32),
    )
    run_max, run_total, run_acc = lax.fori_loop(0, blk_count, forward_step, start_state)
    attended = run_acc / jnp.transpose(run_total)[:, :, None]
    log_total = run_max + jnp.log(run_total)
    attended_low = attended.reshape(tok_rows, feat).astype(bf16)

    mid_rows = in_rows + dot32(attended_low, full_out)
    scale_two = rms_scale(mid_rows)
    hidden = (mid_rows * scale_two * gain_ffn).astype(bf16)
    hidden_f = hidden.astype(f32)
    logits = dot32(hidden, full_router) + prev_logits[0]
    gate_probs = jax.nn.softmax(logits, axis=-1)
    gate_vals = jnp.sum(choose * gate_probs[:, None, :], axis=-1)
    rows_in = to_experts(dot32(spread, hidden).astype(bf16))
    gate_rows = jnp.sum(
        jnp.where(hit[0], gate_vals[None, :, 0], 0.0) + jnp.where(hit[1], gate_vals[None, :, 1], 0.0),
        axis=1,
    )
    gates_in = to_experts(gate_rows)

    w_g = gather_expert(w_gate, 1)
    w_u = gather_expert(w_up, 1)
    w_d = gather_expert(w_down, 0)
    gate_pre = dot32(rows_in, w_g)
    up_pre = dot32(rows_in, w_u)
    sig = jax.nn.sigmoid(gate_pre)
    silu_gate = gate_pre * sig
    act = (silu_gate * up_pre).astype(bf16)
    expert_out = dot32(act, w_d).astype(bf16)
    grad_rows_f = grad_rows_in.astype(f32)
    gate_grad_rows = jnp.sum(grad_rows_f * expert_out.astype(f32), axis=1)
    grad_expert_out = (grad_rows_f * gates_in).astype(bf16)
    grad_act = dot32(grad_expert_out, w_d, ((1,), (1,)))
    grad_gate_pre = (grad_act * up_pre * sig * (1.0 + gate_pre * (1.0 - sig))).astype(bf16)
    grad_up_pre = (grad_act * silu_gate).astype(bf16)
    grad_in = (
        dot32(grad_gate_pre, w_g, ((1,), (1,))) + dot32(grad_up_pre, w_u, ((1,), (1,)))
    ).astype(bf16)
    back_gates = to_experts(gate_grad_rows)
    back_grads = to_experts(grad_in)
    back_rows = to_experts(expert_out)
    grad_down = dot32(act, grad_expert_out, ((0,), (0,)))
    grad_gate = dot32(rows_in, grad_gate_pre, ((0,), (0,)))
    grad_up = dot32(rows_in, grad_up_pre, ((0,), (0,)))
    expert_grads = (
        scatter_expert(grad_gate, own_exp, 1),
        scatter_expert(grad_up, own_exp, 1),
        scatter_expert(grad_down, own_exp, 0),
    )

    const_mix = jax.nn.softmax(dot32(hidden, full_cg).reshape(tok_rows, 2, 2), axis=-1)
    vectors = jnp.transpose(full_cv.astype(f32))
    copy_gate = jnp.sum(jnp.where(route_ids == n_ffn + 1, gate_vals, 0.0), axis=1)
    const_sel = choose[:, :, n_ffn + 2 :]
    const_gates = jnp.sum(const_sel * gate_vals[:, :, None], axis=1)
    hidden_coef = copy_gate + jnp.sum(const_mix[..., 0] * const_gates, axis=1)
    vec_coef = const_mix[..., 1] * const_gates
    picked = [dot32(pick[j], back_rows) for j in range(2)]
    moe_out = (
        gate_vals[:, 0:1] * picked[0]
        + gate_vals[:, 1:2] * picked[1]
        + hidden_coef[:, None] * hidden_f
        + dot32(vec_coef, vectors, precision=top_precision)
    )
    output = (mid_rows + moe_out) * valid_rows

    g_hidden = jnp.sum(grad_out * hidden_f, axis=1)
    g_vec = dot32(grad_out, vectors, ((1,), (1,)), precision=top_precision)
    const_dots = const_mix[..., 0] * g_hidden[:, None] + const_mix[..., 1] * g_vec
    ffn_dots = jnp.stack(
        [
            jnp.sum(jnp.where(jnp.transpose(hit[j]), jnp.transpose(back_gates), 0.0), axis=1)
            for j in range(2)
        ],
        axis=1,
    )
    grad_gates = (
        ffn_dots
        + jnp.where(route_ids == n_ffn + 1, g_hidden[:, None], 0.0)
        + jnp.sum(const_sel * const_dots[:, None, :], axis=2)
    )
    grad_mix = jnp.stack([const_gates * g_hidden[:, None], const_gates * g_vec], axis=-1)
    grad_mix_logits = (
        const_mix * (grad_mix - jnp.sum(const_mix * grad_mix, axis=-1, keepdims=True))
    ).reshape(tok_rows, 4)
    grad_vectors = dot32(vec_coef, grad_out, ((0,), (0,)), precision=top_precision)
    grad_probs = jnp.sum(choose * grad_gates[:, :, None], axis=1)
    grad_logits = gate_probs * (
        grad_probs - jnp.sum(gate_probs * grad_probs, axis=-1, keepdims=True)
    )
    grad_hidden = (
        dot32(pick[0], back_grads)
        + dot32(pick[1], back_grads)
        + hidden_coef[:, None] * grad_out
        + dot32(grad_mix_logits, full_cg.astype(f32), ((1,), (1,)), precision=top_precision)
        + dot32(grad_logits, full_router.astype(f32), ((1,), (1,)), precision=top_precision)
    )
    grad_router = dot32(hidden_f, grad_logits, ((0,), (0,)), precision=top_precision)
    grad_cg = dot32(hidden_f, grad_mix_logits, ((0,), (0,)), precision=top_precision)
    grad_mid_norm, grad_gain_two = rms_backward(mid_rows, scale_two, gain_ffn, grad_hidden)
    grad_mid = grad_out + grad_mid_norm
    grad_attn = grad_mid.astype(bf16)
    grad_w_out = dot32(attended_low, grad_attn, ((0,), (0,)))
    grad_attended = dot32(grad_attn, full_out, ((1,), (1,))).astype(bf16)
    grad_attended = grad_attended.reshape(tok_rows, HEADS, head_size)
    row_delta = jnp.transpose(jnp.sum(grad_attended.astype(f32) * attended, axis=-1))

    def backward_step(blk_index, loop_state):
        grad_queries, grad_key_rows, grad_value_rows = loop_state
        blk_scores, key_rows, value_rows = block_scores(blk_index)
        blk_probs = jnp.exp(blk_scores - log_total[..., None])
        grad_probs_blk = jnp.einsum(
            "qhd,khd->hqk", grad_attended, value_rows, preferred_element_type=f32
        )
        grad_scores = (blk_probs * (grad_probs_blk - row_delta[..., None])).astype(bf16)
        grad_queries = grad_queries + jnp.einsum(
            "hqk,khd->qhd", grad_scores, key_rows, preferred_element_type=f32
        )
        key_part = jnp.einsum(
            "hqk,qhd->khd", grad_scores, queries, preferred_element_type=f32
        ).reshape(KBLK, feat)
        value_part = jnp.einsum(
            "hqk,qhd->khd", blk_probs.astype(bf16), grad_attended, preferred_element_type=f32
        ).reshape(KBLK, feat)
        blk_start = blk_index * KBLK
        grad_key_rows = lax.dynamic_update_slice_in_dim(grad_key_rows, key_part, blk_start, 0)
        grad_value_rows = lax.dynamic_update_slice_in_dim(grad_value_rows, value_part, blk_start, 0)
        return (grad_queries, grad_key_rows, grad_value_rows)

    back_state = (
        jnp.zeros((tok_rows, HEADS, head_size), f32),
        jnp.zeros((tok_rows * n_ctx, feat), f32),
        jnp.zeros((tok_rows * n_ctx, feat), f32),
    )
    grad_queries, grad_key_rows, grad_value_rows = lax.fori_loop(
        0, blk_count, backward_step, back_state
    )
    own_key_grads = scatter_ctx(grad_key_rows)
    own_value_grads = scatter_ctx(grad_value_rows)
    grad_q = (
        rotate(grad_queries * score_scale, positions, -1.0).reshape(tok_rows, feat).astype(bf16)
    )
    grad_k = (
        rotate(heads_of(own_key_grads * score_scale), positions, -1.0)
        .reshape(tok_rows, feat)
        .astype(bf16)
    )
    grad_v = own_value_grads.astype(bf16)
    grad_hidden_one = (
        dot32(grad_q, full_q, ((1,), (1,)))
        + dot32(grad_k, full_k, ((1,), (1,)))
        + dot32(grad_v, full_v, ((1,), (1,)))
    )
    grad_in_norm, grad_gain_one = rms_backward(in_rows, scale_one, gain_attn, grad_hidden_one)
    grad_x = grad_mid + grad_in_norm
    small_grads = jnp.concatenate(
        [
            grad_router,
            grad_cg,
            jnp.transpose(grad_vectors),
            grad_gain_one[:, None],
            grad_gain_two[:, None],
        ],
        axis=1,
    )
    small_grads = jnp.pad(small_grads, ((0, 0), (0, 128 - small_grads.shape[1])))
    out_out = scatter_rows(grad_w_out, steps_b)
    q_out = scatter_rows(dot32(hidden_one, grad_q, ((0,), (0,))), steps_a)
    v_out = scatter_rows(dot32(hidden_one, grad_v, ((0,), (0,))), steps_b)
    k_out = scatter_rows(
        jnp.concatenate([dot32(hidden_one, grad_k, ((0,), (0,))), small_grads], axis=1), steps_a
    )
    small_out = k_out[:, feat:]
    return (
        output[None],
        grad_x[None],
        jnp.concatenate([q_out, k_out[:, :feat], v_out], axis=1),
        out_out,
        small_out[:, n_all + 6],
        small_out[:, n_all + 7],
        small_out[:, :n_all],
        small_out[:, n_all : n_all + 4],
        small_out[:, n_all + 4 : n_all + 6],
        expert_grads[0],
        expert_grads[1],
        expert_grads[2],
    )


def solution(mesh):
    in_specs = (
        P(("dp", "exp"), "ctx", None),
        P(("dp", "exp")),
        P(("dp", "exp"), "ctx", None),
        P(("dp", "exp"), "ctx", None),
        P(("dp", "exp"), "ctx", None),
        P(("dp", "ctx", "exp"), None),
        P(("dp", "ctx", "exp"), None),
        P(("dp", "ctx", "exp")),
        P(("dp", "ctx", "exp")),
        P(("dp", "ctx", "exp"), None),
        P(("dp", "ctx", "exp"), None),
        P(("dp", "ctx", "exp"), None),
        P("exp", None, ("dp", "ctx")),
        P("exp", None, ("dp", "ctx")),
        P("exp", ("dp", "ctx"), None),
    )
    out_specs = (
        P(("dp", "exp"), "ctx", None),
        P(("dp", "exp"), "ctx", None),
        P(("dp", "ctx", "exp"), None),
        P(("dp", "ctx", "exp"), None),
        P(("dp", "ctx", "exp")),
        P(("dp", "ctx", "exp")),
        P(("dp", "ctx", "exp"), None),
        P(("dp", "ctx", "exp"), None),
        P(("dp", "ctx", "exp"), None),
        P("exp", None, ("dp", "ctx")),
        P("exp", None, ("dp", "ctx")),
        P("exp", ("dp", "ctx"), None),
    )
    return jax.shard_map(local, mesh=mesh, in_specs=in_specs, out_specs=out_specs, check_vma=False)
```

time: 1760 us -> 743 us (0.42)
  waiting for transfers between devices: 1110 us -> 224 us
  blocking collectives: 280 us -> 0 us
  starting transfers between devices: 17.4 us -> 187 us
  matrix products: 168 us -> 147 us
    reduce_scatter x7 -> x0, waiting for transfers between devices: 942 us -> none  [the longest x1 248 us: local(): lax.psum_scatter(grad_gate_w, ('dp', 'ctx'), scatter_dimension=2, tiled=T...]
    ppermute x0 -> x74, waiting for transfers between devices: none -> 203 us  [swap(): lax.ppermute(block, axis, [(i, i ^ bit) for i in range(lax.axis_size(axis...]
    all_gather x3 -> x0, blocking collectives: 197 us -> none  [the longest x1 67.4 us: local(): lax.all_gather(router, ('dp', 'ctx', 'exp'), axis=0, tiled=True)]
    all_gather x7 -> x0, waiting for transfers between devices: 152 us -> none  [the longest x1 91 us: local(): lax.all_gather(w_down, ('dp', 'ctx'), axis=1, tiled=True)]
    ppermute x0 -> x74, starting transfers between devices: none -> 149 us  [swap(): lax.ppermute(block, axis, [(i, i ^ bit) for i in range(lax.axis_size(axis...]
    unnamed x2 -> x0, blocking collectives: 83 us -> none
    gather x2 -> x0, local copies, waits for them, and re-layouts: 33.7 us -> none  [the longest x1 19.8 us: local(): returned[safe_index, slot_ids].astype(jnp.float32) * is_ffn_f[..., None]]
    concatenate x1 -> x9, local copies, waits for them, and re-layouts: 0.17 us -> 23.3 us  [the longest x3 8.21 us: gather_expert(): whole = jnp.concatenate([whole, swap(whole, 'dp', bit)], axis=ff_axis)]
  transfers between devices with their start and end apart: 18 -> 80, of which waited for: 11 -> 34; matrix products, arithmetic and copies ran while one was open for 11% -> 35% of each run, Pallas kernels for 0% -> 0%
where the time goes in v1:
time: 743 us; the launch traced here: 732 us
  waiting for transfers between devices  224 us (30%)
  starting transfers between devices  187 us (25%)
  matrix products  147 us (20%)
  local copies, waits for them, and re-layouts  102 us (14%)
  other arithmetic  66.1 us (9%)
    ppermute x74, waiting for transfers between devices, swap(): lax.ppermute(block, axis, [(i, i ^ bit) for i in range(lax.axis_size(axis...  203 us
    ppermute x74, starting transfers between devices, swap(): lax.ppermute(block, axis, [(i, i ^ bit) for i in range(lax.axis_size(axis...  149 us
    dot_general x37, matrix products, dot32(): lax.dot_general(a, b, (dims, ((), ())), precision=precision, preferred_el...  116 us
    all_to_all x6, starting transfers between devices, to_experts(): lax.all_to_all(rows.reshape(n_dp * n_exp, sub_rows, -1), ('dp', 'exp'), s...  38.3 us
    unnamed x213, local copies, waits for them, and re-layouts  33 us
    all_to_all x6, waiting for transfers between devices, to_experts(): lax.all_to_all(rows.reshape(n_dp * n_exp, sub_rows, -1), ('dp', 'exp'), s...  21.2 us
  transfers between devices with their start and end apart: 80, of which 34 were waited for; matrix products, arithmetic and copies ran while one was open for 35% of the time, Pallas kernels for 0%

profile of v1, /device:TPU:0, one launch (start us, length us, event | category | flops | bytes accessed | tf_op | source)
XLA Modules:
  0.0 731.9 jit_solution(15033782590516412888)
XLA Ops:
  23.1 5.6 collective-permute-done.11
  56.2 4.0 collective-permute-start.29
  66.9 8.0 %collective-permute-done.28 = bf16[768,128]{1,0:T(8,128)(2,1)S(1)} collective-permute-done((bf16[768,128]{1,0:T(8,128)(2,1)S(1)}, bf16[768,128]{1,0:T(8,128)(2,1)S(1)}, u32[]{:S(2)}, u32[]{:S(2)}) %collective-permute-start.28) | collective-permute-done | bytes 196640 | tf_op jit(solution)/shard_map/ppermute | solution.py:20
  93.5 52.4 %collective-permute-done.20 = bf16[2,2,2,24,768]{4,3,0,1,2:T(8,128)(2,1)S(1)} collective-permute-done((bf16[2,2,2,24,768]{4,3,0,1,2:T(8,128)(2,1)S(1)}, bf16[2,2,2,24,768]{4,3,0,1,2:T(8,128)(2,1)S(1)}, u32[]{:S(2)}, u32[]{:S(2)}) %collective-permute-start.20) | collective-permute-done | bytes 294944 | tf_op jit(solution)/shard_map/ppermute | solution.py:20
  173.6 11.6 %collective-permute-done.16 = bf16[512,768]{1,0:T(8,128)(2,1)} collective-permute-done((bf16[512,768]{1,0:T(8,128)(2,1)}, bf16[512,768]{1,0:T(8,128)(2,1)}, u32[]{:S(2)}, u32[]{:S(2)}) %collective-permute-start.16) | collective-permute-done | bytes 786464 | tf_op jit(solution)/shard_map/ppermute | solution.py:20
  188.4 13.2 %collective-permute-done.5 = bf16[512,768]{1,0:T(8,128)(2,1)} collective-permute-done((bf16[512,768]{1,0:T(8,128)(2,1)}, bf16[512,768]{1,0:T(8,128)(2,1)}, u32[]{:S(2)}, u32[]{:S(2)}) %collective-permute-start.5) | collective-permute-done | bytes 786464 | tf_op jit(solution)/shard_map/ppermute | solution.py:20
  205.0 10.8 %while.30 = (s32[]{:T(128)}, f32[12,512]{1,0:T(8,128)S(1)}, f32[12,512]{1,0:T(8,128)S(1)}, f32[512,12,64]{0,2,1:T(8,128)S(1)}, s32[]{:T(128)}, /*index=5*/s32[]{...) while((s32[]{:T(128)}, f32[12,512]{1,0:T(8,128)S(1)}, ...), condition=%wide.region_4.5_spmd.clone, body=%wide.region_1.4_spmd.clone.sunk | while | flops 841240576 | bytes 47850696 | solution.py:291
  223.0 5.8 all-to-all-start.3
  231.1 4.1 all-to-all-done.3
  235.1 4.9 all-to-all-start
  262.5 10.5 %all-to-all-done = bf16[16,64,768]{2,1,0:T(8,128)(2,1)} async-done(((bf16[16,64,768]{2,1,0:T(8,128)(2,1)}), bf16[16,64,768]{2,1,0:T(8,128)(2,1)}, u32[]{:S(2)}, u32[]{:S(2)}) %all-to-all-start) | async-done | bytes 1572896 | tf_op jit(solution)/shard_map/all_to_all | solution.py:215
  272.9 8.2 %all-to-all-start.2 = ((bf16[16,64,768]{2,1,0:T(8,128)(2,1)}), bf16[16,64,768]{2,1,0:T(8,128)(2,1)}, u32[]{:S(2)}, u32[]{:S(2)}) async-start(bf16[16,64,768]{2,1,0:T(8,128)(2,1)} %bitcast.636), calls=%async_computation.2 | async-start | bytes 3145728 | tf_op jit(solution)/shard_map/all_to_all | solution.py:215
  296.5 3.8 constant_dynamic-update-slice_fusion.29
  300.3 7.1 fusion.170
  307.3 6.7 all-to-all-done.2
  315.8 7.6 %fusion.171 = f32[1024,2048]{1,0:T(8,128)} fusion(bf16[1024,768]{1,0:T(8,128)(2,1)S(1)} %fusion.25, bf16[2048,768]{1,0:T(8,128)(2,1)} %constant_dynamic-update-slice_fusion.29), kind=kOutput, calls=%fused_computation.483 | convolution fusion | flops 3221225472 | bytes 13107200 | tf_op jit(solution)/shard_map/dot_general | solution.py:16
  323.4 14.0 %multiply_convert_fusion.1 = (bf16[1024,2048]{1,0:T(8,128)(2,1)S(1)}, bf16[1024,2048]{1,0:T(8,128)(2,1)S(1)}, bf16[1024,2048]{1,0:T(8,128)(2,1)}) fusion(f32[1024,2048]{1,0:T(8,128)} %fusion.171, f32[1024,2048]{1,0:T(8,128)} %fusion.170, bf16[1024,768]{1,0:T(8,128)(2,1)} %bitcast.70, bf16[768,2048]{1,0:T(8,128)(2,1)} %constant_dynamic-update-slice_fusion.7), kind=kOutput, calls=%fused_computation.41 | convolution fusion | flops 3252682752 | bytes 34078720 | tf_op jit(solution)/shard_map/dot_general | solution.py:16
  337.4 6.3 fusion.177
  343.7 5.1 fusion.172
  348.9 3.7 fusion.178
  357.9 5.1 fusion.176
  367.1 6.7 fusion.26
  374.4 7.3 all-to-all-start.5
  381.7 8.7 %add_convert_fusion = bf16[1024,768]{1,0:T(8,128)(2,1)} fusion(f32[1024,768]{1,0:T(8,128)} %fusion.172, bf16[1024,2048]{1,0:T(8,128)(2,1)} %copy-done.38, bf16[768,2048]{1,0:T(8,128)(2,1)} %constant_dynamic-update-slice_fusion.7), kind=kOutput, calls=%fused_computation.55 | convolution fusion | flops 3222798336 | bytes 12058624 | tf_op jit(solution)/shard_map/dot_general | solution.py:16
  390.4 6.5 all-to-all-start.4
  405.6 11.4 %collective-permute-start.70 = (bf16[512,768]{1,0:T(8,128)(2,1)S(1)}, bf16[512,768]{1,0:T(8,128)(2,1)S(1)}, u32[]{:S(2)}, u32[]{:S(2)}) collective-permute-start(bf16[512,768]{1,0:T(8,128)(2,1)S(1)} %split.204), channel_id=1, source_target_pairs={{0,2},{2,0},{1,3},{3,1},{4,6},{6,4},{5,7},{7,5},{8,10},{10,8},{9,1... | collective-permute-start | bytes 2359304 | tf_op jit(solution)/shard_map/ppermute | solution.py:20
  423.8 11.6 %collective-permute-done.70 = bf16[512,768]{1,0:T(8,128)(2,1)S(1)} collective-permute-done((bf16[512,768]{1,0:T(8,128)(2,1)S(1)}, bf16[512,768]{1,0:T(8,128)(2,1)S(1)}, u32[]{:S(2)}, u32[]{:S(2)}) %collective-permute-start.70) | collective-permute-done | bytes 786464 | tf_op jit(solution)/shard_map/ppermute | solution.py:20
  435.7 3.8 collective-permute-start.71
  440.1 12.2 %collective-permute-done.65 = bf16[768,512]{1,0:T(8,128)(2,1)S(1)} collective-permute-done((bf16[768,512]{1,0:T(8,128)(2,1)S(1)}, bf16[768,512]{1,0:T(8,128)(2,1)S(1)}, u32[]{:S(2)}, u32[]{:S(2)}) %collective-permute-start.65) | collective-permute-done | bytes 786464 | tf_op jit(solution)/shard_map/ppermute | solution.py:20
  452.7 3.8 collective-permute-start.66
  456.5 12.4 %collective-permute-done.60 = bf16[768,512]{1,0:T(8,128)(2,1)S(1)} collective-permute-done((bf16[768,512]{1,0:T(8,128)(2,1)S(1)}, bf16[768,512]{1,0:T(8,128)(2,1)S(1)}, u32[]{:S(2)}, u32[]{:S(2)}) %collective-permute-start.60) | collective-permute-done | bytes 786464 | tf_op jit(solution)/shard_map/ppermute | solution.py:20
  478.1 5.0 collective-permute-done.67
  489.3 8.4 %collective-permute-done.62 = bf16[768,128]{1,0:T(8,128)(2,1)S(1)} collective-permute-done((bf16[768,128]{1,0:T(8,128)(2,1)S(1)}, bf16[768,128]{1,0:T(8,128)(2,1)S(1)}, u32[]{:S(2)}, u32[]{:S(2)}) %collective-permute-start.62) | collective-permute-done | bytes 196640 | tf_op jit(solution)/shard_map/ppermute | solution.py:20
  499.1 5.7 all-to-all-start.1
  524.5 41.4 %while.31 = (s32[]{:T(128)}, f32[512,12,64]{0,2,1:T(8,128)}, f32[1024,768]{1,0:T(8,128)}, f32[1024,768]{1,0:T(8,128)}, s32[]{:T(128)}, /*index=5*/bf16[1024,768]...) while((s32[]{:T(128)}, f32[512,12,64]{0,2,1:T(8,128)}, ...), condition=%wide.region_28.29_spmd.clone, body=%wide.region_27.28_spmd.clone.sunk | while | flops 2045642752 | bytes 204555760 | solution.py:424
  532.5 6.1 fusion.275
  538.7 4.8 fusion.277
  545.4 8.9 %fusion.276 = f32[12,512,64]{1,2,0:T(8,128)} fusion(bf16[512,12,64]{0,2,1:T(8,128)(2,1)} %copy-done.42, f32[12,512,512]{2,1,0:T(8,128)} %copy-done.2, f32[12,512]{1,0:T(8,128)S(1)} %get-tuple-element.846, pred[512,512]{0,1:T(8,128)(4,1)S(1)} %compare_and_fusion.5), kind=kOutput, calls=%fused_computation.27.clone.1 | convolution fusion | flops 415236096 | bytes 15228928 | tf_op jit(solution)/shard_map/while/body/hqk,qhd->khd/dot_general | solution.py:411
  561.8 3.9 bitcast_add_fusion.21
  568.8 42.7 %collective-permute-start.37 = (bf16[512,768]{1,0:T(8,128)(2,1)}, bf16[512,768]{1,0:T(8,128)(2,1)}, u32[]{:S(2)}, u32[]{:S(2)}) collective-permute-start(bf16[512,768]{1,0:T(8,128)(2,1)} %select_convert_fusion.1), channel_id=1, source_target_pairs={{0,2},{2,0},{1,3},{3,1},{4,6},{6,4},{5,7},{7,5},{8,10},{10,8},{9,1... | collective-permute-start | bytes 2359304 | tf_op jit(solution)/shard_map/ppermute | solution.py:20
  618.1 4.0 fusion.45
  639.5 7.5 %collective-permute-done.38 = bf16[512,768]{1,0:T(8,128)(2,1)} collective-permute-done((bf16[512,768]{1,0:T(8,128)(2,1)}, bf16[512,768]{1,0:T(8,128)(2,1)}, u32[]{:S(2)}, u32[]{:S(2)}) %collective-permute-start.38) | collective-permute-done | bytes 786464 | tf_op jit(solution)/shard_map/ppermute | solution.py:20
  656.7 4.1 concatenate.90
  672.2 6.1 collective-permute-done.56
  678.7 4.1 collective-permute-done.57
  694.6 5.2 collective-permute-done.40
  710.1 4.0 collective-permute-start.43
  722.5 5.3 collective-permute-done.48
  (622 shorter events, 329.3 us)
Async XLA Ops:
  2.8 53.5 %collective-permute-start.22 = (bf16[768,128]{1,0:T(8,128)(2,1)}, bf16[768,128]{1,0:T(8,128)(2,1)}, u32[]{:S(2)}, u32[]{:S(2)}) collective-permute-start(bf16[768,128]{1,0:T(8,128)(2,1)} %get-tuple-element.514), channel_id=1, source_target_pairs={{0,8},{4,12},{8,0},{12,4},{16,24},{20,28},{24,16},{28,20},{1,9},{5... | collective-permute-start | bytes 589832 | tf_op jit(solution)/shard_map/ppermute | solution.py:20
  5.8 54.5 %collective-permute-start.23 = (bf16[768,128]{1,0:T(8,128)(2,1)}, bf16[768,128]{1,0:T(8,128)(2,1)}, u32[]{:S(2)}, u32[]{:S(2)}) collective-permute-start(bf16[768,128]{1,0:T(8,128)(2,1)} %get-tuple-element.515), channel_id=1, source_target_pairs={{0,16},{4,20},{8,24},{12,28},{16,0},{20,4},{24,8},{28,12},{1,17},{... | collective-permute-start | bytes 589832 | tf_op jit(solution)/shard_map/ppermute | solution.py:20
  8.4 52.6 %collective-permute-start.24 = (bf16[768,128]{1,0:T(8,128)(2,1)}, bf16[768,128]{1,0:T(8,128)(2,1)S(1)}, u32[]{:S(2)}, u32[]{:S(2)}) collective-permute-start(bf16[768,128]{1,0:T(8,128)(2,1)} %get-tuple-element.513), channel_id=1, source_target_pairs={{0,24},{4,28},{8,16},{12,20},{16,8},{20,12},{24,0},{28,4},{1,25},{... | collective-permute-start | bytes 589832 | tf_op jit(solution)/shard_map/ppermute | solution.py:20
  9.2 19.6 %collective-permute-start.11 = (bf16[24,768]{1,0:T(8,128)(2,1)S(1)}, bf16[24,768]{1,0:T(8,128)(2,1)S(1)}, u32[]{:S(2)}, u32[]{:S(2)}) collective-permute-start(bf16[24,768]{1,0:T(8,128)(2,1)S(1)} %slice.236), channel_id=1, source_target_pairs={{0,16},{4,20},{8,24},{12,28},{16,0},{20,4},{24,8},{28,12},{1,17},{... | collective-permute-start | bytes 110600 | tf_op jit(solution)/shard_map/ppermute | solution.py:20
  11.1 18.0 %collective-permute-start.17 = (bf16[24,768]{1,0:T(8,128)(2,1)}, bf16[24,768]{1,0:T(8,128)(2,1)S(1)}, u32[]{:S(2)}, u32[]{:S(2)}) collective-permute-start(bf16[24,768]{1,0:T(8,128)(2,1)} %param.25), channel_id=1, source_target_pairs={{0,16},{4,20},{8,24},{12,28},{16,0},{20,4},{24,8},{28,12},{1,17},{... | collective-permute-start | bytes 110600 | tf_op jit(solution)/shard_map/ppermute | solution.py:20
  41.2 23.4 %collective-permute-start.27 = (bf16[768,128]{1,0:T(8,128)(2,1)}, bf16[768,128]{1,0:T(8,128)(2,1)S(1)}, u32[]{:S(2)}, u32[]{:S(2)}) collective-permute-start(bf16[768,128]{1,0:T(8,128)(2,1)} %get-tuple-element.519), channel_id=1, source_target_pairs={{0,8},{4,12},{8,0},{12,4},{16,24},{20,28},{24,16},{28,20},{1,9},{5... | collective-permute-start | bytes 589832 | tf_op jit(solution)/shard_map/ppermute | solution.py:20
  53.5 21.4 %collective-permute-start.28 = (bf16[768,128]{1,0:T(8,128)(2,1)S(1)}, bf16[768,128]{1,0:T(8,128)(2,1)S(1)}, u32[]{:S(2)}, u32[]{:S(2)}) collective-permute-start(bf16[768,128]{1,0:T(8,128)(2,1)S(1)} %copy-done.76), channel_id=1, source_target_pairs={{0,16},{4,20},{8,24},{12,28},{16,0},{20,4},{24,8},{28,12},{1,17},{... | collective-permute-start | bytes 589832 | tf_op jit(solution)/shard_map/ppermute | solution.py:20
  56.2 20.2 %collective-permute-start.29 = (bf16[768,128]{1,0:T(8,128)(2,1)S(1)}, bf16[768,128]{1,0:T(8,128)(2,1)S(1)}, u32[]{:S(2)}, u32[]{:S(2)}) collective-permute-start(bf16[768,128]{1,0:T(8,128)(2,1)S(1)} %copy-done.75), channel_id=1, source_target_pairs={{0,24},{4,28},{8,16},{12,20},{16,8},{20,12},{24,0},{28,4},{1,25},{... | collective-permute-start | bytes 589832 | tf_op jit(solution)/shard_map/ppermute | solution.py:20
  60.3 21.2 %collective-permute-start.32 = (bf16[128,768]{1,0:T(8,128)(2,1)}, bf16[128,768]{1,0:T(8,128)(2,1)S(1)}, u32[]{:S(2)}, u32[]{:S(2)}) collective-permute-start(bf16[128,768]{1,0:T(8,128)(2,1)} %get-tuple-element.509), channel_id=1, source_target_pairs={{0,8},{4,12},{8,0},{12,4},{16,24},{20,28},{24,16},{28,20},{1,9},{5... | collective-permute-start | bytes 589832 | tf_op jit(solution)/shard_map/ppermute | solution.py:20
  61.0 22.0 %collective-permute-start.33 = (bf16[128,768]{1,0:T(8,128)(2,1)S(1)}, bf16[128,768]{1,0:T(8,128)(2,1)S(1)}, u32[]{:S(2)}, u32[]{:S(2)}) collective-permute-start(bf16[128,768]{1,0:T(8,128)(2,1)S(1)} %copy-done.74), channel_id=1, source_target_pairs={{0,16},{4,20},{8,24},{12,28},{16,0},{20,4},{24,8},{28,12},{1,17},{... | collective-permute-start | bytes 589832 | tf_op jit(solution)/shard_map/ppermute | solution.py:20
  64.5 19.9 %collective-permute-start.34 = (bf16[128,768]{1,0:T(8,128)(2,1)S(1)}, bf16[128,768]{1,0:T(8,128)(2,1)S(1)}, u32[]{:S(2)}, u32[]{:S(2)}) collective-permute-start(bf16[128,768]{1,0:T(8,128)(2,1)S(1)} %copy-done.73), channel_id=1, source_target_pairs={{0,24},{4,28},{8,16},{12,20},{16,8},{20,12},{24,0},{28,4},{1,25},{... | collective-permute-start | bytes 589832 | tf_op jit(solution)/shard_map/ppermute | solution.py:20
  84.5 163.3 %collective-permute-start.25 = (bf16[768,512]{1,0:T(8,128)(2,1)}, bf16[768,512]{1,0:T(8,128)(2,1)}, u32[]{:S(2)}, u32[]{:S(2)}) collective-permute-start(bf16[768,512]{1,0:T(8,128)(2,1)} %pad_maximum_fusion.11), channel_id=1, source_target_pairs={{0,2},{2,0},{1,3},{3,1},{4,6},{6,4},{5,7},{7,5},{8,10},{10,8},{9,1... | collective-permute-start | bytes 2359304 | tf_op jit(solution)/shard_map/ppermute | solution.py:20
  86.0 164.7 %collective-permute-start.30 = (bf16[768,512]{1,0:T(8,128)(2,1)}, bf16[768,512]{1,0:T(8,128)(2,1)}, u32[]{:S(2)}, u32[]{:S(2)}) collective-permute-start(bf16[768,512]{1,0:T(8,128)(2,1)} %pad_maximum_fusion.12), channel_id=1, source_target_pairs={{0,2},{2,0},{1,3},{3,1},{4,6},{6,4},{5,7},{7,5},{8,10},{10,8},{9,1... | collective-permute-start | bytes 2359304 | tf_op jit(solution)/shard_map/ppermute | solution.py:20
  87.5 165.7 %collective-permute-start.35 = (bf16[512,768]{1,0:T(8,128)(2,1)}, bf16[512,768]{1,0:T(8,128)(2,1)}, u32[]{:S(2)}, u32[]{:S(2)}) collective-permute-start(bf16[512,768]{1,0:T(8,128)(2,1)} %pad_maximum_fusion.13), channel_id=1, source_target_pairs={{0,2},{2,0},{1,3},{3,1},{4,6},{6,4},{5,7},{7,5},{8,10},{10,8},{9,1... | collective-permute-start | bytes 2359304 | tf_op jit(solution)/shard_map/ppermute | solution.py:20
  88.3 57.7 %collective-permute-start.20 = (bf16[2,2,2,24,768]{4,3,0,1,2:T(8,128)(2,1)S(1)}, bf16[2,2,2,24,768]{4,3,0,1,2:T(8,128)(2,1)S(1)}, u32[]{:S(2)}, u32[]{:S(2)}) collective-permute-start(bf16[2,2,2,24,768]{4,3,0,1,2:T(8,128)(2,1)S(1)} %pad_maximum_fusion.22), channel_id=1, source_target_pairs={{0,2},{2,0},{1,3},{3,1},{4,6},{6,4},{5,7},{7,5},{8,10},{10,8},{9,1... | collective-permute-start | bytes 884744 | tf_op jit(solution)/shard_map/ppermute | solution.py:20
  92.0 57.2 %collective-permute-start.14 = (bf16[2,2,2,24,768]{4,3,0,1,2:T(8,128)(2,1)S(1)}, bf16[2,2,2,24,768]{4,3,0,1,2:T(8,128)(2,1)S(1)}, u32[]{:S(2)}, u32[]{:S(2)}) collective-permute-start(bf16[2,2,2,24,768]{4,3,0,1,2:T(8,128)(2,1)S(1)} %pad_maximum_fusion.21), channel_id=1, source_target_pairs={{0,2},{2,0},{1,3},{3,1},{4,6},{6,4},{5,7},{7,5},{8,10},{10,8},{9,1... | collective-permute-start | bytes 884744 | tf_op jit(solution)/shard_map/ppermute | solution.py:20
  164.5 20.7 %collective-permute-start.16 = (bf16[512,768]{1,0:T(8,128)(2,1)}, bf16[512,768]{1,0:T(8,128)(2,1)}, u32[]{:S(2)}, u32[]{:S(2)}) collective-permute-start(bf16[512,768]{1,0:T(8,128)(2,1)} %convolution_convert_fusion.4), channel_id=1, source_target_pairs={{0,2},{2,0},{1,3},{3,1},{4,6},{6,4},{5,7},{7,5},{8,10},{10,8},{9,1... | collective-permute-start | bytes 2359304 | tf_op jit(solution)/shard_map/ppermute | solution.py:20
  170.8 30.8 %collective-permute-start.5 = (bf16[512,768]{1,0:T(8,128)(2,1)}, bf16[512,768]{1,0:T(8,128)(2,1)}, u32[]{:S(2)}, u32[]{:S(2)}) collective-permute-start(bf16[512,768]{1,0:T(8,128)(2,1)} %copy.326), channel_id=1, source_target_pairs={{0,2},{2,0},{1,3},{3,1},{4,6},{6,4},{5,7},{7,5},{8,10},{10,8},{9,1... | collective-permute-start | bytes 2359304 | tf_op jit(solution)/shard_map/ppermute | solution.py:20
  235.1 37.8 %all-to-all-start = ((bf16[16,64,768]{2,1,0:T(8,128)(2,1)}), bf16[16,64,768]{2,1,0:T(8,128)(2,1)}, u32[]{:S(2)}, u32[]{:S(2)}) async-start(bf16[16,64,768]{2,1,0:T(8,128)(2,1)} %bitcast.635), calls=%async_computation | async-start | bytes 3145728 | tf_op jit(solution)/shard_map/all_to_all | solution.py:215
  250.3 41.7 %collective-permute-start.26 = (bf16[768,1024]{1,0:T(8,128)(2,1)}, bf16[768,1024]{1,0:T(8,128)(2,1)}, u32[]{:S(2)}, u32[]{:S(2)}) collective-permute-start(bf16[768,1024]{1,0:T(8,128)(2,1)} %get-tuple-element.511), channel_id=1, source_target_pairs={{0,4},{4,0},{8,12},{12,8},{16,20},{20,16},{24,28},{28,24},{1,5},{5... | collective-permute-start | bytes 4718600 | tf_op jit(solution)/shard_map/ppermute | solution.py:20
  253.1 41.8 %collective-permute-start.31 = (bf16[768,1024]{1,0:T(8,128)(2,1)}, bf16[768,1024]{1,0:T(8,128)(2,1)}, u32[]{:S(2)}, u32[]{:S(2)}) collective-permute-start(bf16[768,1024]{1,0:T(8,128)(2,1)} %get-tuple-element.516), channel_id=1, source_target_pairs={{0,4},{4,0},{8,12},{12,8},{16,20},{20,16},{24,28},{28,24},{1,5},{5... | collective-permute-start | bytes 4718600 | tf_op jit(solution)/shard_map/ppermute | solution.py:20
  255.6 40.9 %collective-permute-start.36 = (bf16[1024,768]{1,0:T(8,128)(2,1)}, bf16[1024,768]{1,0:T(8,128)(2,1)}, u32[]{:S(2)}, u32[]{:S(2)}) collective-permute-start(bf16[1024,768]{1,0:T(8,128)(2,1)} %get-tuple-element.506), channel_id=1, source_target_pairs={{0,4},{4,0},{8,12},{12,8},{16,20},{20,16},{24,28},{28,24},{1,5},{5... | collective-permute-start | bytes 4718600 | tf_op jit(solution)/shard_map/ppermute | solution.py:20
  272.9 41.1 %all-to-all-start.2 = ((bf16[16,64,768]{2,1,0:T(8,128)(2,1)}), bf16[16,64,768]{2,1,0:T(8,128)(2,1)}, u32[]{:S(2)}, u32[]{:S(2)}) async-start(bf16[16,64,768]{2,1,0:T(8,128)(2,1)} %bitcast.636), calls=%async_computation.2 | async-start | bytes 3145728 | tf_op jit(solution)/shard_map/all_to_all | solution.py:215
  354.0 48.7 %collective-permute-start.69 = (bf16[1024,768]{1,0:T(8,128)(2,1)}, bf16[1024,768]{1,0:T(8,128)(2,1)}, u32[]{:S(2)}, u32[]{:S(2)}) collective-permute-start(bf16[1024,768]{1,0:T(8,128)(2,1)} %split.201), channel_id=1, source_target_pairs={{0,4},{4,0},{8,12},{12,8},{16,20},{20,16},{24,28},{28,24},{1,5},{5... | collective-permute-start | bytes 4718600 | tf_op jit(solution)/shard_map/ppermute | solution.py:20
  357.3 59.7 %collective-permute-start.64 = (bf16[768,1024]{1,0:T(8,128)(2,1)}, bf16[768,1024]{1,0:T(8,128)(2,1)}, u32[]{:S(2)}, u32[]{:S(2)}) collective-permute-start(bf16[768,1024]{1,0:T(8,128)(2,1)} %split.202), channel_id=1, source_target_pairs={{0,4},{4,0},{8,12},{12,8},{16,20},{20,16},{24,28},{28,24},{1,5},{5... | collective-permute-start | bytes 4718600 | tf_op jit(solution)/shard_map/ppermute | solution.py:20
  367.1 52.8 %collective-permute-start.59 = (bf16[768,1024]{1,0:T(8,128)(2,1)}, bf16[768,1024]{1,0:T(8,128)(2,1)}, u32[]{:S(2)}, u32[]{:S(2)}) collective-permute-start(bf16[768,1024]{1,0:T(8,128)(2,1)} %split.203), channel_id=1, source_target_pairs={{0,4},{4,0},{8,12},{12,8},{16,20},{20,16},{24,28},{28,24},{1,5},{5... | collective-permute-start | bytes 4718600 | tf_op jit(solution)/shard_map/ppermute | solution.py:20
  374.4 16.0 %all-to-all-start.5 = ((f32[16,64,1]{1,2,0:T(1,128)}), f32[16,64,1]{1,2,0:T(1,128)S(1)}, u32[]{:S(2)}, u32[]{:S(2)}) async-start(f32[16,64,1]{1,2,0:T(1,128)} %bitcast.98), calls=%async_computation.5 | async-start | bytes 16384 | tf_op jit(solution)/shard_map/all_to_all | solution.py:215
  390.4 108.7 %all-to-all-start.4 = ((bf16[16,64,768]{2,1,0:T(8,128)(2,1)}), bf16[16,64,768]{2,1,0:T(8,128)(2,1)}, u32[]{:S(2)}, u32[]{:S(2)}) async-start(bf16[16,64,768]{2,1,0:T(8,128)(2,1)} %bitcast.634), calls=%async_computation.4 | async-start | bytes 3145728 | tf_op jit(solution)/shard_map/all_to_all | solution.py:215
  405.6 29.8 %collective-permute-start.70 = (bf16[512,768]{1,0:T(8,128)(2,1)S(1)}, bf16[512,768]{1,0:T(8,128)(2,1)S(1)}, u32[]{:S(2)}, u32[]{:S(2)}) collective-permute-start(bf16[512,768]{1,0:T(8,128)(2,1)S(1)} %split.204), channel_id=1, source_target_pairs={{0,2},{2,0},{1,3},{3,1},{4,6},{6,4},{5,7},{7,5},{8,10},{10,8},{9,1... | collective-permute-start | bytes 2359304 | tf_op jit(solution)/shard_map/ppermute | solution.py:20
  419.4 32.9 %collective-permute-start.65 = (bf16[768,512]{1,0:T(8,128)(2,1)S(1)}, bf16[768,512]{1,0:T(8,128)(2,1)S(1)}, u32[]{:S(2)}, u32[]{:S(2)}) collective-permute-start(bf16[768,512]{1,0:T(8,128)(2,1)S(1)} %split.205), channel_id=1, source_target_pairs={{0,2},{2,0},{1,3},{3,1},{4,6},{6,4},{5,7},{7,5},{8,10},{10,8},{9,1... | collective-permute-start | bytes 2359304 | tf_op jit(solution)/shard_map/ppermute | solution.py:20
  422.2 46.8 %collective-permute-start.60 = (bf16[768,512]{1,0:T(8,128)(2,1)S(1)}, bf16[768,512]{1,0:T(8,128)(2,1)S(1)}, u32[]{:S(2)}, u32[]{:S(2)}) collective-permute-start(bf16[768,512]{1,0:T(8,128)(2,1)S(1)} %split.206), channel_id=1, source_target_pairs={{0,2},{2,0},{1,3},{3,1},{4,6},{6,4},{5,7},{7,5},{8,10},{10,8},{9,1... | collective-permute-start | bytes 2359304 | tf_op jit(solution)/shard_map/ppermute | solution.py:20
  435.7 36.3 %collective-permute-start.71 = (bf16[128,768]{1,0:T(8,128)(2,1)S(1)}, bf16[128,768]{1,0:T(8,128)(2,1)S(1)}, u32[]{:S(2)}, u32[]{:S(2)}) collective-permute-start(bf16[128,768]{1,0:T(8,128)(2,1)S(1)} %get-tuple-element.499), channel_id=1, source_target_pairs={{0,24},{4,28},{8,16},{12,20},{16,8},{20,12},{24,0},{28,4},{1,25},{... | collective-permute-start | bytes 589832 | tf_op jit(solution)/shard_map/ppermute | solution.py:20
  439.5 34.0 %collective-permute-start.72 = (bf16[128,768]{1,0:T(8,128)(2,1)S(1)}, bf16[128,768]{1,0:T(8,128)(2,1)S(1)}, u32[]{:S(2)}, u32[]{:S(2)}) collective-permute-start(bf16[128,768]{1,0:T(8,128)(2,1)S(1)} %get-tuple-element.498), channel_id=1, source_target_pairs={{0,16},{4,20},{8,24},{12,28},{16,0},{20,4},{24,8},{28,12},{1,17},{... | collective-permute-start | bytes 589832 | tf_op jit(solution)/shard_map/ppermute | solution.py:20
  439.5 34.3 %collective-permute-start.73 = (bf16[128,768]{1,0:T(8,128)(2,1)S(1)}, bf16[128,768]{1,0:T(8,128)(2,1)S(1)}, u32[]{:S(2)}, u32[]{:S(2)}) collective-permute-start(bf16[128,768]{1,0:T(8,128)(2,1)S(1)} %get-tuple-element.497), channel_id=1, source_target_pairs={{0,8},{4,12},{8,0},{12,4},{16,24},{20,28},{24,16},{28,20},{1,9},{5... | collective-permute-start | bytes 589832 | tf_op jit(solution)/shard_map/ppermute | solution.py:20
  452.7 23.0 %collective-permute-start.66 = (bf16[768,128]{1,0:T(8,128)(2,1)S(1)}, bf16[768,128]{1,0:T(8,128)(2,1)S(1)}, u32[]{:S(2)}, u32[]{:S(2)}) collective-permute-start(bf16[768,128]{1,0:T(8,128)(2,1)S(1)} %get-tuple-element.502), channel_id=1, source_target_pairs={{0,24},{4,28},{8,16},{12,20},{16,8},{20,12},{24,0},{28,4},{1,25},{... | collective-permute-start | bytes 589832 | tf_op jit(solution)/shard_map/ppermute | solution.py:20
  469.0 14.1 %collective-permute-start.67 = (bf16[768,128]{1,0:T(8,128)(2,1)S(1)}, bf16[768,128]{1,0:T(8,128)(2,1)S(1)}, u32[]{:S(2)}, u32[]{:S(2)}) collective-permute-start(bf16[768,128]{1,0:T(8,128)(2,1)S(1)} %get-tuple-element.501), channel_id=1, source_target_pairs={{0,16},{4,20},{8,24},{12,28},{16,0},{20,4},{24,8},{28,12},{1,17},{... | collective-permute-start | bytes 589832 | tf_op jit(solution)/shard_map/ppermute | solution.py:20
  472.0 14.7 %collective-permute-start.68 = (bf16[768,128]{1,0:T(8,128)(2,1)S(1)}, bf16[768,128]{1,0:T(8,128)(2,1)S(1)}, u32[]{:S(2)}, u32[]{:S(2)}) collective-permute-start(bf16[768,128]{1,0:T(8,128)(2,1)S(1)} %get-tuple-element.500), channel_id=1, source_target_pairs={{0,8},{4,12},{8,0},{12,4},{16,24},{20,28},{24,16},{28,20},{1,9},{5... | collective-permute-start | bytes 589832 | tf_op jit(solution)/shard_map/ppermute | solution.py:20
  473.5 15.8 %collective-permute-start.61 = (bf16[768,128]{1,0:T(8,128)(2,1)S(1)}, bf16[768,128]{1,0:T(8,128)(2,1)S(1)}, u32[]{:S(2)}, u32[]{:S(2)}) collective-permute-start(bf16[768,128]{1,0:T(8,128)(2,1)S(1)} %get-tuple-element.505), channel_id=1, source_target_pairs={{0,24},{4,28},{8,16},{12,20},{16,8},{20,12},{24,0},{28,4},{1,25},{... | collective-permute-start | bytes 589832 | tf_op jit(solution)/shard_map/ppermute | solution.py:20
  473.8 23.9 %collective-permute-start.62 = (bf16[768,128]{1,0:T(8,128)(2,1)S(1)}, bf16[768,128]{1,0:T(8,128)(2,1)S(1)}, u32[]{:S(2)}, u32[]{:S(2)}) collective-permute-start(bf16[768,128]{1,0:T(8,128)(2,1)S(1)} %get-tuple-element.504), channel_id=1, source_target_pairs={{0,16},{4,20},{8,24},{12,28},{16,0},{20,4},{24,8},{28,12},{1,17},{... | collective-permute-start | bytes 589832 | tf_op jit(solution)/shard_map/ppermute | solution.py:20
  475.7 22.0 %collective-permute-start.63 = (bf16[768,128]{1,0:T(8,128)(2,1)S(1)}, bf16[768,128]{1,0:T(8,128)(2,1)S(1)}, u32[]{:S(2)}, u32[]{:S(2)}) collective-permute-start(bf16[768,128]{1,0:T(8,128)(2,1)S(1)} %get-tuple-element.503), channel_id=1, source_target_pairs={{0,8},{4,12},{8,0},{12,4},{16,24},{20,28},{24,16},{28,20},{1,9},{5... | collective-permute-start | bytes 589832 | tf_op jit(solution)/shard_map/ppermute | solution.py:20
  499.1 116.2 %all-to-all-start.1 = ((bf16[16,64,768]{2,1,0:T(8,128)(2,1)}), bf16[16,64,768]{2,1,0:T(8,128)(2,1)}, u32[]{:S(2)}, u32[]{:S(2)}) async-start(bf16[16,64,768]{2,1,0:T(8,128)(2,1)} %bitcast.633), calls=%async_computation.1 | async-start | bytes 3145728 | tf_op jit(solution)/shard_map/all_to_all | solution.py:215
  517.1 108.4 %collective-permute-start.54 = (bf16[2,2,2,2,24,768]{5,4,0,1,3,2:T(8,128)(2,1)}, bf16[2,2,2,2,24,768]{5,4,0,1,3,2:T(8,128)(2,1)}, u32[]{:S(2)}, u32[]{:S(2)}) collective-permute-start(bf16[2,2,2,2,24,768]{5,4,0,1,3,2:T(8,128)(2,1)} %fusion.96), channel_id=1, source_target_pairs={{0,4},{4,0},{8,12},{12,8},{16,20},{20,16},{24,28},{28,24},{1,5},{5... | collective-permute-start | bytes 1769480 | tf_op jit(solution)/shard_map/ppermute | solution.py:20
  568.8 61.3 %collective-permute-start.37 = (bf16[512,768]{1,0:T(8,128)(2,1)}, bf16[512,768]{1,0:T(8,128)(2,1)}, u32[]{:S(2)}, u32[]{:S(2)}) collective-permute-start(bf16[512,768]{1,0:T(8,128)(2,1)} %select_convert_fusion.1), channel_id=1, source_target_pairs={{0,2},{2,0},{1,3},{3,1},{4,6},{6,4},{5,7},{7,5},{8,10},{10,8},{9,1... | collective-permute-start | bytes 2359304 | tf_op jit(solution)/shard_map/ppermute | solution.py:20
  614.4 32.6 %collective-permute-start.38 = (bf16[512,768]{1,0:T(8,128)(2,1)}, bf16[512,768]{1,0:T(8,128)(2,1)}, u32[]{:S(2)}, u32[]{:S(2)}) collective-permute-start(bf16[512,768]{1,0:T(8,128)(2,1)} %select_convert_fusion), channel_id=1, source_target_pairs={{0,2},{2,0},{1,3},{3,1},{4,6},{6,4},{5,7},{7,5},{8,10},{10,8},{9,1... | collective-permute-start | bytes 2359304 | tf_op jit(solution)/shard_map/ppermute | solution.py:20
  627.6 43.2 %collective-permute-start.55 = (bf16[2,2,2,24,768]{4,3,0,1,2:T(8,128)(2,1)}, bf16[2,2,2,24,768]{4,3,0,1,2:T(8,128)(2,1)}, u32[]{:S(2)}, u32[]{:S(2)}) collective-permute-start(bf16[2,2,2,24,768]{4,3,0,1,2:T(8,128)(2,1)} %fusion.104), channel_id=1, source_target_pairs={{0,2},{2,0},{1,3},{3,1},{4,6},{6,4},{5,7},{7,5},{8,10},{10,8},{9,1... | collective-permute-start | bytes 884744 | tf_op jit(solution)/shard_map/ppermute | solution.py:20
  656.2 32.2 %collective-permute-start.39 = (bf16[2,2,2,2,24,768]{5,4,3,2,1,0:T(8,128)(2,1)}, bf16[2,2,2,2,24,768]{5,4,3,2,1,0:T(8,128)(2,1)}, u32[]{:S(2)}, u32[]{:S(2)}) collective-permute-start(bf16[2,2,2,2,24,768]{5,4,3,2,1,0:T(8,128)(2,1)} %fusion.94), channel_id=1, source_target_pairs={{0,4},{4,0},{8,12},{12,8},{16,20},{20,16},{24,28},{28,24},{1,5},{5... | collective-permute-start | bytes 1769480 | tf_op jit(solution)/shard_map/ppermute | solution.py:20
  678.6 14.1 %collective-permute-start.44 = (bf16[2,2,2,2,24,896]{5,4,0,1,2,3:T(8,128)(2,1)S(1)}, bf16[2,2,2,2,24,896]{5,4,0,1,2,3:T(8,128)(2,1)S(1)}, u32[]{:S(2)}, u32[]{:S(2)}) collective-permute-start(bf16[2,2,2,2,24,896]{5,4,0,1,2,3:T(8,128)(2,1)S(1)} %fusion.92), channel_id=1, source_target_pairs={{0,4},{4,0},{8,12},{12,8},{16,20},{20,16},{24,28},{28,24},{1,5},{5... | collective-permute-start | bytes 2064392 | tf_op jit(solution)/shard_map/ppermute | solution.py:20
  693.0 13.4 %collective-permute-start.45 = (bf16[2,2,2,24,896]{4,3,0,1,2:T(8,128)(2,1)S(1)}, bf16[2,2,2,24,896]{4,3,0,1,2:T(8,128)(2,1)S(1)}, u32[]{:S(2)}, u32[]{:S(2)}) collective-permute-start(bf16[2,2,2,24,896]{4,3,0,1,2:T(8,128)(2,1)S(1)} %fusion.101), channel_id=1, source_target_pairs={{0,1},{1,0},{2,3},{3,2},{4,5},{5,4},{6,7},{7,6},{8,9},{9,8},{10,11... | collective-permute-start | bytes 1032200 | tf_op jit(solution)/shard_map/ppermute | solution.py:20
  (136 other events, 1354.9 us)

commit v2 on v1

v2 whole, which is shorter than its diff:
```python
import functools

import jax
import jax.numpy as jnp
from jax import lax
from jax.experimental import pallas as pl
from jax.experimental.pallas import tpu as pltpu
from jax.sharding import PartitionSpec as P

HEADS = 12

norm_eps = 1e-06
top_precision = lax.Precision.HIGHEST
f32 = jnp.float32
bf16 = jnp.bfloat16


CHUNK = 256
BLOCK = 512
PAIR = 128
NEG = -1e30
SCALE = 48
MICROS = {
    "project": 6, "project_other": 5, "spread": 4, "attend": 17, "mid": 9, "expert": 30, "weights_far": 10,
    "weights_near": 8, "weights_kept": 8, "weights_sum": 4, "gates_back": 11, "grads_other": 17, "back_other": 8, "grads_own": 13,
    "back_own": 13, "out_grads": 7, "output": 6, "first_norm": 4, "weights_all": 26, "pack": 3, "unpack": 4, "combine": 3,
}


def cost(name):
    return pl.CostEstimate(flops=MICROS[name] * 1000000000 // SCALE, bytes_accessed=1, transcendentals=0)


def mul_nt(a, b):
    return lax.dot_general(a, b, (((1,), (1,)), ((), ())), preferred_element_type=f32)


def mul_nn(a, b):
    return lax.dot_general(a, b, (((1,), (0,)), ((), ())), preferred_element_type=f32)


def mul_tn(a, b):
    return lax.dot_general(a, b, (((0,), (0,)), ((), ())), preferred_element_type=f32)


def head_part(rows, head):
    lane = lax.broadcasted_iota(jnp.int32, rows.shape, 1)
    return jnp.where((lane >= PAIR // 2) == (head == 1), rows, jnp.zeros_like(rows))


def key_allowed(shape, key_start, length, query_start=None):
    key = key_start + lax.broadcasted_iota(jnp.int32, shape, 0)
    allowed = key < length
    if query_start is not None:
        allowed &= key <= query_start + lax.broadcasted_iota(jnp.int32, shape, 1)
    return allowed


def attend_kernel(info, q_ref, k_ref, v_ref, ok_ref, ov_ref, out_ref, low_ref, log_ref):
    base, length, blocks = info[0], info[1], info[2]
    queries = q_ref[...]
    rows = queries.shape[0]
    half = PAIR // 2
    parts = [head_part(queries, head) for head in range(2)]
    lows = [slice(head * half, (head + 1) * half) for head in range(2)]

    def padded(first, some):
        if first == 0:
            return some
        return jnp.concatenate([jnp.zeros((some.shape[0], first), f32), some], axis=1)

    states = []
    for head in range(2):
        scores = []
        for first in range(0, rows, CHUNK):
            part = mul_nt(k_ref[first : first + CHUNK, :], parts[head][first:])
            allowed = key_allowed(part.shape, base + first, length, base + first)
            scores.append(jnp.where(allowed, part, NEG))
        top = jnp.max(scores[0], axis=0, keepdims=True)
        for i, part in enumerate(scores[1:], 1):
            more = jnp.max(part, axis=0, keepdims=True)
            first = i * CHUNK
            top = jnp.concatenate([top[:, :first], jnp.maximum(top[:, first:], more)], axis=1)
        total = jnp.zeros((1, rows), f32)
        acc = jnp.zeros((half, rows), f32)
        for i, part in enumerate(scores):
            first = i * CHUNK
            expo = jnp.exp(part - top[:, first:])
            total += padded(first, jnp.sum(expo, axis=0, keepdims=True))
            acc += padded(first, mul_tn(v_ref[first : first + CHUNK, :], expo.astype(bf16))[lows[head]])
        states.append((top, total, acc))

    def step(c, states):
        first = pl.multiple_of(c * BLOCK, BLOCK)
        keys = ok_ref[pl.ds(first, BLOCK), :]
        vals = ov_ref[pl.ds(first, BLOCK), :]
        new = []
        for head in range(2):
            top, total, acc = states[head]
            scores = mul_nt(keys, parts[head])
            scores = jnp.where(key_allowed(scores.shape, first, length), scores, NEG)
            new_top = jnp.maximum(top, jnp.max(scores, axis=0, keepdims=True))
            expo = jnp.exp(scores - new_top)
            factor = jnp.exp(top - new_top)
            total = total * factor + jnp.sum(expo, axis=0, keepdims=True)
            acc = acc * factor + mul_tn(vals, expo.astype(bf16))[lows[head]]
            new.append((new_top, total, acc))
        return tuple(new)

    states = lax.fori_loop(0, blocks, step, tuple(states))
    full = jnp.concatenate([s[2] / s[1] for s in states], axis=0)
    out = jnp.transpose(full)
    out_ref[...] = out
    low_ref[...] = out.astype(bf16)
    for head in range(2):
        log_ref[0, head : head + 1, :] = states[head][0] + jnp.log(states[head][1])


def pair_grads(keys, vals, part, grad_part, log_row, delta_row, allowed):
    probs = jnp.exp(mul_nt(keys, part) - log_row)
    probs = jnp.where(allowed, probs, 0.0)
    grad_probs = mul_nt(vals, grad_part)
    grad_scores = (probs * (grad_probs - delta_row)).astype(bf16)
    return (
        mul_nn(grad_scores, part),
        mul_nn(probs.astype(bf16), grad_part),
        mul_tn(keys, grad_scores),
    )


def other_backward(
    info, q_ref, k_ref, v_ref, grad_ref, out_ref, log_ref, dq_ref, dk_ref, dv_ref, delta_ref
):
    length, chunks = info[1], info[2] * (BLOCK // CHUNK)
    half = PAIR // 2
    queries, grads = q_ref[...], grad_ref[...]
    rows = queries.shape[0]
    product = jnp.transpose(grads.astype(f32) * out_ref[...])
    parts = [head_part(queries, head) for head in range(2)]
    grad_parts = [head_part(grads, head) for head in range(2)]
    deltas = [
        jnp.sum(product[head * half : (head + 1) * half], axis=0, keepdims=True) for head in range(2)
    ]
    for head in range(2):
        delta_ref[0, head : head + 1, :] = deltas[head]

    def step(c, dq):
        first = pl.multiple_of(c * CHUNK, CHUNK)
        keys = k_ref[pl.ds(first, CHUNK), :]
        vals = v_ref[pl.ds(first, CHUNK), :]
        allowed = key_allowed((CHUNK, rows), first, length)
        both = [
            pair_grads(
                keys, vals, parts[h], grad_parts[h], log_ref[0, h : h + 1, :], deltas[h], allowed
            )
            for h in range(2)
        ]
        dk_ref[pl.ds(first, CHUNK), :] = (both[0][0] + both[1][0]).astype(dk_ref.dtype)
        dv_ref[pl.ds(first, CHUNK), :] = (both[0][1] + both[1][1]).astype(dv_ref.dtype)
        return dq + jnp.concatenate([both[0][2][:half], both[1][2][half:]], axis=0)

    dq = lax.fori_loop(0, chunks, step, jnp.zeros((PAIR, rows), f32))
    dq_ref[...] = dq

    def clear(c, none):
        first = pl.multiple_of(c * CHUNK, CHUNK)
        dk_ref[pl.ds(first, CHUNK), :] = jnp.zeros((CHUNK, PAIR), dk_ref.dtype)
        dv_ref[pl.ds(first, CHUNK), :] = jnp.zeros((CHUNK, PAIR), dv_ref.dtype)
        return none

    lax.fori_loop(chunks, k_ref.shape[0] // CHUNK, clear, 0)


def own_backward(
    info, q_ref, k_ref, v_ref, grad_ref, log_ref, delta_ref, before_ref, dq_ref, dk_ref, dv_ref
):
    base, length = info[0], info[1]
    half = PAIR // 2
    queries, grads = q_ref[...], grad_ref[...]
    rows = queries.shape[0]
    parts = [head_part(queries, head) for head in range(2)]
    grad_parts = [head_part(grads, head) for head in range(2)]
    dq = before_ref[...]
    for first in range(0, rows, CHUNK):
        keys = k_ref[first : first + CHUNK, :]
        vals = v_ref[first : first + CHUNK, :]
        allowed = key_allowed((CHUNK, rows - first), base + first, length, base + first)
        both = [
            pair_grads(
                keys,
                vals,
                parts[h][first:],
                grad_parts[h][first:],
                log_ref[0, h : h + 1, first:],
                delta_ref[0, h : h + 1, first:],
                allowed,
            )
            for h in range(2)
        ]
        dk_ref[first : first + CHUNK, :] = both[0][0] + both[1][0]
        dv_ref[first : first + CHUNK, :] = both[0][1] + both[1][1]
        more = jnp.concatenate([both[0][2][:half], both[1][2][half:]], axis=0)
        if first:
            more = jnp.concatenate([jnp.zeros((PAIR, first), f32), more], axis=1)
        dq = dq + more
    dq_ref[...] = jnp.transpose(dq)


def per_pair(rows):
    return pl.BlockSpec((rows, PAIR), lambda i, info: (0, i))


def turned(cols):
    return pl.BlockSpec((PAIR, cols), lambda i, info: (i, 0))


def stats(cols):
    return pl.BlockSpec((1, 2, cols), lambda i, info: (i, 0, 0))


def ordered(kernel, n_in, n_deps):
    if not n_deps:
        return kernel

    def run(*refs):
        kernel(*refs[:n_in], *refs[n_in + n_deps :])

    return run


def waits(deps):
    return [pl.BlockSpec(memory_space=pl.ANY)] * len(deps)


def attn_call(kernel, info, args, in_specs, outs, out_specs, flops, name, deps=()):
    return pl.pallas_call(
        ordered(kernel, 1 + len(args), len(deps)),
        grid_spec=pltpu.PrefetchScalarGridSpec(
            num_scalar_prefetch=1,
            grid=(HEADS // 2,),
            in_specs=in_specs + waits(deps),
            out_specs=out_specs,
        ),
        out_shape=[jax.ShapeDtypeStruct(s, d) for s, d in outs],
        compiler_params=pltpu.CompilerParams(vmem_limit_bytes=48 << 20),
        cost_estimate=cost(name),
        name=name,
    )(info, *args, *deps)


def attend(info, q, k, v, other_k, other_v, deps):
    t, d = q.shape
    st = (HEADS // 2, 2, t)
    n = other_k.shape[0]
    return attn_call(
        attend_kernel, info, (q, k, v, other_k, other_v),
        [per_pair(t)] * 3 + [per_pair(n)] * 2,
        [((t, d), f32), ((t, d), bf16), (st, f32)], [per_pair(t), per_pair(t), stats(t)], 8 * t * t * d, "attend", deps,
    )


def grads_other(info, q, k, v, grad, out, log_total, deps):
    t, d = q.shape
    n = k.shape[0]
    return attn_call(
        other_backward, info, (q, k, v, grad, out, log_total),
        [per_pair(t), per_pair(n), per_pair(n), per_pair(t), per_pair(t), stats(t)],
        [((d, t), f32), ((n, d), bf16), ((n, d), bf16), ((HEADS // 2, 2, t), f32)],
        [turned(t), per_pair(n), per_pair(n), stats(t)], 10 * t * t * d, "grads_other", deps,
    )


def grads_own(info, q, k, v, grad, log_total, delta, before, deps):
    t, d = q.shape
    return attn_call(
        own_backward, info, (q, k, v, grad, log_total, delta, before),
        [per_pair(t)] * 4 + [stats(t)] * 2 + [turned(t)],
        [((t, d), f32)] * 3, [per_pair(t)] * 3, 10 * t * t * d, "grads_own", deps,
    )


def dot32(a, b, dims=((1,), (0,)), precision=None):
    return lax.dot_general(a, b, (dims, ((), ())), precision=precision, preferred_element_type=f32)


def swap(block, axis, bit):
    return lax.ppermute(block, axis, [(i, i ^ bit) for i in range(lax.axis_size(axis))])


def bits_of(axis, low=1, high=None):
    high = lax.axis_size(axis) if high is None else high
    found = []
    while low < high:
        found.append(low)
        low *= 2
    return found[::-1]


def row_weight(axis):
    x = lax.axis_size("exp")
    c = lax.axis_size("ctx")
    return {"exp": 1, "ctx": x, "dp": x * c}[axis]


def plan_steps(middle):
    far = [("dp", bit) for bit in bits_of("dp", 2)]
    mid = [(axis, bit) for axis in middle for bit in bits_of(axis)]
    near = [("dp", bit) for bit in bits_of("dp", 1, 2)]
    return far, mid, near


def row_bits(steps):
    return sorted([row_weight(axis) * bit for axis, bit in steps], reverse=True)


def nothing(*refs):
    pass


def hold(value, *others):
    return pl.pallas_call(
        nothing,
        in_specs=waits((value,) + others),
        out_specs=waits((value,))[0],
        out_shape=jax.ShapeDtypeStruct(value.shape, value.dtype),
        input_output_aliases={0: 0},
        cost_estimate=pl.CostEstimate(flops=0, bytes_accessed=0, transcendentals=0),
        name="hold",
    )(value, *others)


def gather_step(whole, placed, axis, bit, meanwhile=()):
    other = swap(whole, axis, bit)
    if meanwhile:
        whole = hold(whole, *meanwhile)
    upper = (lax.axis_index(axis) & bit) != 0
    weight = row_weight(axis) * bit
    pos = sum(1 for w in placed if w > weight)
    both = [jnp.where(upper, other, whole), jnp.where(upper, whole, other)]
    return jnp.stack(both, axis=pos), placed[:pos] + [weight] + placed[pos:]


def gather_steps(whole, placed, steps):
    for axis, bit in steps:
        whole, placed = gather_step(whole, placed, axis, bit)
    return whole, placed


def scatter_split(part, placed, axis, bit):
    pos = placed.index(row_weight(axis) * bit)
    upper = (lax.axis_index(axis) & bit) != 0
    low = lax.index_in_dim(part, 0, pos, keepdims=False)
    high = lax.index_in_dim(part, 1, pos, keepdims=False)
    sent = jnp.where(upper, low, high).astype(bf16)
    kept = jnp.where(upper, high, low).astype(f32)
    return sent, kept, placed[:pos] + placed[pos + 1 :]


def scatter_step(part, placed, axis, bit):
    sent, kept, placed = scatter_split(part, placed, axis, bit)
    return kept + swap(sent, axis, bit).astype(f32), placed


def combine_kernel(block, up_ref, kept_ref, came_ref, keep_ref, give_ref):
    total = kept_ref[...] + came_ref[...].astype(f32)
    keep_ref[...], give_ref[...] = split_rows(up_ref[0] == 1, total, block)


def combine(kept, came, placed, axis, bit, rows):
    weight = row_weight(axis) * bit
    block = rows * 2 ** sum(1 for w in placed if w < weight)
    upper = ((lax.axis_index(axis) & bit) != 0).astype(jnp.int32).reshape(1)
    shape = (kept.shape[0] // 2, kept.shape[1])
    keep, give = simple_call(
        functools.partial(combine_kernel, block), (kept, came), [(shape, f32), (shape, bf16)], 0, "combine", (), (upper,)
    )
    placed = [w for w in placed if w != weight]
    whole = (2,) * len(placed) + (-1, shape[1])
    return give.reshape(whole), keep.reshape(whole), placed


def scatter_parts(pairs, orders, far, near, rows, meanwhile):
    places = [row_bits(far + orders[0])] * len(pairs)
    parts = pairs
    for i, steps in enumerate(zip(*[reversed(order) for order in orders])):
        if i == 0:
            splits = [
                combine(keep, swap(give, *near[0]), where, *step, rows)
                for (keep, give), where, step in zip(parts, places, steps)
            ]
        else:
            splits = [scatter_split(part, where, *step) for part, where, step in zip(parts, places, steps)]
        sent, kept, places = [list(column) for column in zip(*splits)]
        came = [swap(part, *step) for part, step in zip(sent, steps)]
        if i == 0:
            kept[-1] = hold(kept[-1], *meanwhile(sent[-1]))
        parts = [a + b.astype(f32) for a, b in zip(kept, came)]
    placed = places[0]
    part = jnp.concatenate(parts, axis=-1)
    for axis, bit in reversed(far):
        part, placed = scatter_step(part, placed, axis, bit)
    return part


def pack_kernel(gate_ref, up_ref, down_ref, out_ref):
    out_ref[0, 0] = gate_ref[0]
    out_ref[0, 1] = up_ref[0]
    out_ref[0, 2] = jnp.transpose(down_ref[0])


def unpack_kernel(back_ref, gate_ref, up_ref, down_ref):
    gate_ref[0] = back_ref[0, 0].astype(f32)
    up_ref[0] = back_ref[0, 1].astype(f32)
    down_ref[0] = jnp.transpose(back_ref[0, 2].astype(f32))


def one_of(*shape):
    return pl.BlockSpec((1,) + shape, lambda i: (i,) + (0,) * len(shape))


def pack_expert(w_gate, w_up, w_down, deps):
    n, d, f = w_gate.shape
    return pl.pallas_call(
        ordered(pack_kernel, 3, len(deps)),
        grid=(n,),
        in_specs=[one_of(d, f), one_of(d, f), one_of(f, d)] + waits(deps),
        out_specs=one_of(3, d, f),
        out_shape=jax.ShapeDtypeStruct((n, 3, d, f), w_gate.dtype),
        cost_estimate=cost("pack"),
        name="pack",
    )(w_gate, w_up, w_down, *deps)


def unpack_expert(back, deps):
    n, _, d, f = back.shape
    return pl.pallas_call(
        ordered(unpack_kernel, 1, len(deps)),
        grid=(n,),
        in_specs=[one_of(3, d, f)] + waits(deps),
        out_specs=[one_of(d, f), one_of(d, f), one_of(f, d)],
        out_shape=[jax.ShapeDtypeStruct(shape, f32) for shape in ((n, d, f), (n, d, f), (n, f, d))],
        cost_estimate=cost("unpack"),
        name="unpack",
    )(back, *deps)


def trade_far(parts):
    n_own = parts.shape[0]
    reps = lax.axis_size("dp") // n_own
    groups = [[i * reps + r for i in range(n_own)] for r in range(reps)]
    return lax.all_to_all(parts, "dp", 0, 0, axis_index_groups=groups, tiled=True)


def near_steps(n_own):
    reps = lax.axis_size("dp") // n_own
    return [("ctx", bit) for bit in bits_of("ctx")] + [("dp", bit) for bit in bits_of("dp", 1, reps)]


def gather_expert_near(groups, steps):
    for axis, bit in steps:
        groups = groups + [swap(group, axis, bit) for group in groups]
    return groups


def scatter_expert_near(groups, steps):
    for axis, bit in reversed(steps):
        n = len(groups) // 2
        came = [swap(group.astype(bf16), axis, bit) for group in groups[n:]]
        groups = [a.astype(f32) + b.astype(f32) for a, b in zip(groups[:n], came)]
    return groups[0]


def weights_sum_kernel(kept_ref, came_ref, out_ref):
    out_ref[...] = (kept_ref[...] + came_ref[...].astype(f32)).astype(bf16)


def rms_scale(rows):
    return lax.rsqrt(jnp.mean(rows * rows, axis=-1, keepdims=True) + norm_eps)


def rms_backward(in_rows, inv_scale, gain_vec, grad_rows):
    normed = in_rows * inv_scale
    gain_grad = jnp.sum(grad_rows * normed, axis=0, keepdims=True)
    inner_grad = grad_rows * gain_vec
    back_rows = inv_scale * (
        inner_grad - normed * jnp.mean(inner_grad * normed, axis=-1, keepdims=True)
    )
    return (back_rows, gain_grad)


def rope(rows, cos, sin):
    lane = lax.broadcasted_iota(jnp.int32, (rows.shape[0], PAIR), 1)
    low = lane % (PAIR // 2) < PAIR // 4
    parts = []
    for first in range(0, rows.shape[1], PAIR):
        part = rows[:, first : first + PAIR]
        other = jnp.where(low, pltpu.roll(part, PAIR - PAIR // 4, 1), pltpu.roll(part, PAIR // 4, 1))
        parts.append(part * cos + other * sin)
    return jnp.concatenate(parts, axis=1)


def gain_row(first_ref, lane):
    small = first_ref[:, first_ref.shape[1] - PAIR :].astype(f32)
    return jnp.transpose(small)[lane : lane + 1]


def project_kernel(scale, lane, x_ref, first_ref, second_ref, cos_ref, sin_ref, h_ref, q_ref, k_ref, v_ref):
    rows = x_ref[...].astype(f32)
    d = rows.shape[1]
    hidden = (rows * rms_scale(rows) * gain_row(first_ref, lane)).astype(bf16)
    h_ref[...] = hidden
    cos, sin = cos_ref[...], sin_ref[...]
    k_ref[...] = rope(mul_nn(hidden, first_ref[:, d : 2 * d]), cos, sin).astype(bf16)
    v_ref[...] = mul_nn(hidden, second_ref[:, :d]).astype(bf16)
    q_ref[...] = (rope(mul_nn(hidden, first_ref[:, :d]), cos, sin) * scale).astype(bf16)


def other_project_kernel(lane, x_ref, first_ref, second_ref, cos_ref, sin_ref, h_ref, k_ref, v_ref):
    rows = x_ref[...].astype(f32)
    d = rows.shape[1]
    hidden = (rows * rms_scale(rows) * gain_row(first_ref, lane)).astype(bf16)
    h_ref[...] = hidden
    k_ref[...] = rope(mul_nn(hidden, first_ref[:, d : 2 * d]), cos_ref[...], sin_ref[...]).astype(bf16)
    v_ref[...] = mul_nn(hidden, second_ref[:, :d]).astype(bf16)


def other_back_kernel(
    dk_ref, dv_ref, h_ref, first_ref, second_ref, cos_ref, sin_ref, x_ref, dwk_ref, dwv_ref, dh_ref, dgain_ref
):
    first = pl.program_id(0) == 0
    d = x_ref.shape[1]
    grad_k = rope(dk_ref[...].astype(f32), cos_ref[...], -sin_ref[...]).astype(bf16)
    grad_v = dv_ref[...]
    hidden = h_ref[...]
    rows = x_ref[...].astype(f32)
    dh = mul_nt(grad_k, first_ref[:, d : 2 * d]) + mul_nt(grad_v, second_ref[:, :d])
    dh_ref[...] = dh.astype(bf16)
    dwk, dwv = mul_tn(hidden, grad_k), mul_tn(hidden, grad_v)
    dgain = jnp.sum(dh * rows * rms_scale(rows), axis=0, keepdims=True)

    @pl.when(first)
    def _():
        dwk_ref[...] = dwk
        dwv_ref[...] = dwv
        dgain_ref[...] = dgain

    @pl.when(jnp.logical_not(first))
    def _():
        dwk_ref[...] += dwk
        dwv_ref[...] += dwv
        dgain_ref[...] += dgain


def split_rows(upper, rows, block):
    keep, give = [], []
    for first in range(0, rows.shape[0], 2 * block):
        low, high = rows[first : first + block], rows[first + block : first + 2 * block]
        keep.append(jnp.where(upper, high, low))
        give.append(jnp.where(upper, low, high))
    return jnp.concatenate(keep, axis=0), jnp.concatenate(give, axis=0).astype(bf16)


def own_back_kernel(
    scale, block, core_ref, dq_ref, dk_ref, dv_ref, h_ref, first_ref, second_ref, cos_ref, sin_ref, x_ref, mwk_ref, mwv_ref, mgain_ref,
    keep_ref, give_ref, rest_ref, dh_ref,
):
    d = h_ref.shape[1]
    upper = core_ref[0] == 1
    cos, sin = cos_ref[...], -sin_ref[...]
    hidden = h_ref[...]
    grad_q = rope(dq_ref[...] * scale, cos, sin).astype(bf16)
    keep_ref[:, :d], give_ref[:, :d] = split_rows(upper, mul_tn(hidden, grad_q), block)
    dh = mul_nt(grad_q, first_ref[:, :d])
    grad_k = rope(dk_ref[...], cos, sin).astype(bf16)
    dw_k = mul_tn(hidden, grad_k) + mwk_ref[...]
    keep_ref[:, d : 2 * d], give_ref[:, d : 2 * d] = split_rows(upper, dw_k, block)
    dh += mul_nt(grad_k, first_ref[:, d : 2 * d])
    grad_v = dv_ref[...].astype(bf16)
    rest_ref[...] = mul_tn(hidden, grad_v) + mwv_ref[...]
    dh += mul_nt(grad_v, second_ref[:, :d])
    dh_ref[...] = dh
    rows = x_ref[...].astype(f32)
    dgain = jnp.sum(dh * rows * rms_scale(rows), axis=0, keepdims=True) + mgain_ref[...]
    lane = lax.broadcasted_iota(jnp.int32, (d, PAIR), 1)
    column = jnp.transpose(jnp.broadcast_to(dgain, (8, d)))[:, :1]
    tail = jnp.where(lane == 0, column, 0.0)
    keep_ref[:, 2 * d :], give_ref[:, 2 * d :] = split_rows(upper, tail, block)


def first_norm_kernel(lane, dh_ref, more_ref, x_ref, first_ref, mid_ref, dx_ref):
    rows = x_ref[...].astype(f32)
    grad = dh_ref[...] + more_ref[...].astype(f32)
    back, _ = rms_backward(rows, rms_scale(rows), gain_row(first_ref, lane), grad)
    dx_ref[...] = mid_ref[...] + back


def simple_call(kernel, args, outs, flops, name, deps=(), scalars=()):
    whole = pl.BlockSpec(memory_space=pltpu.VMEM)
    small = pl.BlockSpec(memory_space=pltpu.SMEM)
    return pl.pallas_call(
        ordered(kernel, len(scalars) + len(args), len(deps)),
        in_specs=[small] * len(scalars) + [whole] * len(args) + waits(deps),
        out_shape=[jax.ShapeDtypeStruct(s, d) for s, d in outs],
        compiler_params=pltpu.CompilerParams(vmem_limit_bytes=56 << 20),
        cost_estimate=cost(name),
        name=name,
    )(*scalars, *args, *deps)


def expert_kernel(n_groups, *refs):
    x_ref, g_ref = refs[:2]
    w_refs = refs[2 : 2 + n_groups]
    out_ref, dx_ref, act_ref, dg_ref, du_ref, gx_ref, gg_ref = refs[2 + n_groups :]
    grads = g_ref[...]
    n, d = grads.shape
    rows = x_ref[:, :d]
    gates = x_ref[:, d : d + 1].astype(f32) + x_ref[:, d + 1 : d + 2].astype(f32)
    gx_ref[...] = jnp.transpose((rows.astype(f32) * gates).astype(bf16))
    gg_ref[...] = jnp.transpose((grads.astype(f32) * gates).astype(bf16))
    out = jnp.zeros((n, d), f32)
    back = jnp.zeros((n, d), f32)
    col = 0
    for w_ref in w_refs:
        wg, wu, wd = [
            jnp.concatenate([w_ref[p, m] for p in range(w_ref.shape[0])], axis=1) for m in range(3)
        ]
        width = wg.shape[1]
        gate_pre = mul_nn(rows, wg)
        up_pre = mul_nn(rows, wu)
        sig = 1.0 / (1.0 + jnp.exp(-gate_pre))
        silu = gate_pre * sig
        act = (silu * up_pre).astype(bf16)
        act_ref[:, col : col + width] = act
        out += mul_nt(act, wd)
        grad_act = mul_nn(grads, wd)
        grad_gate = (grad_act * up_pre * sig * (1.0 + gate_pre * (1.0 - sig))).astype(bf16)
        grad_up = (grad_act * silu).astype(bf16)
        dg_ref[:, col : col + width] = grad_gate
        du_ref[:, col : col + width] = grad_up
        back += mul_nt(grad_gate, wg) + mul_nt(grad_up, wu)
        col += width
    low = out.astype(bf16)
    out_ref[...] = low
    dx_ref[:, :d] = back.astype(bf16)
    dots = jnp.sum(grads.astype(f32) * low.astype(f32), axis=1, keepdims=True)
    high, rest = halves(dots)
    lane = lax.broadcasted_iota(jnp.int32, (n, PAIR), 1)
    pair = jnp.where(lane == 0, high.astype(f32), jnp.where(lane == 1, rest.astype(f32), 0.0))
    dx_ref[:, d:] = pair.astype(bf16)


def expert_call(x, g, groups):
    n, d = g.shape
    wide = x.shape[1]
    ff = sum(group.shape[0] * group.shape[3] for group in groups)
    blk = min(512, n)

    def rows(cols):
        return pl.BlockSpec((blk, cols), lambda i: (i, 0))

    widths = [d, wide, ff, ff, ff]
    across = pl.BlockSpec((d, blk), lambda i: (0, i))
    return pl.pallas_call(
        functools.partial(expert_kernel, len(groups)),
        grid=(n // blk,),
        in_specs=[rows(wide), rows(d)] + [pl.BlockSpec(group.shape, lambda i: (0, 0, 0, 0)) for group in groups],
        out_specs=[rows(cols) for cols in widths] + [across] * 2,
        out_shape=[jax.ShapeDtypeStruct((n, cols), bf16) for cols in widths]
        + [jax.ShapeDtypeStruct((d, n), bf16)] * 2,
        compiler_params=pltpu.CompilerParams(vmem_limit_bytes=60 << 20),
        cost_estimate=cost("expert"),
        name="expert",
    )(x, g, *groups)


def expert_weights_kernel(n_came, n_through, x_ref, gg_ref, act_ref, dg_ref, du_ref, *refs):
    out_ref = refs[n_came + n_through]
    pieces, _, _, width = out_ref.shape
    for m, (left, right) in enumerate([(x_ref, dg_ref), (x_ref, du_ref), (gg_ref, act_ref)]):
        grad = mul_nn(left[...], right[...])
        for p in range(pieces):
            part = grad[:, p * width : (p + 1) * width]
            if n_came:
                part += refs[0][p, m].astype(f32)
            out_ref[p, m] = part.astype(out_ref.dtype)


def expert_weights(x, gg, act, dg, du, start, pieces, width, kind, name, came=None, came_start=0, through=None, deps=()):
    d, n = x.shape
    step = min(4, pieces)
    cols = step * width
    rows = pl.BlockSpec((d, n), lambda i: (0, 0))
    part = pl.BlockSpec((n, cols), lambda i: (0, start // cols + i))
    more = [] if came is None else [came]
    passed = [] if through is None else [through]
    block = (step, 3, d, width)
    return pl.pallas_call(
        ordered(functools.partial(expert_weights_kernel, len(more), len(passed)), 5 + len(more) + len(passed), len(deps)),
        grid=(pieces // step,),
        in_specs=[rows, rows, part, part, part]
        + [pl.BlockSpec(block, lambda i: (came_start // step + i, 0, 0, 0))] * len(more)
        + waits(passed)
        + waits(deps),
        out_specs=[pl.BlockSpec(block, lambda i: (i, 0, 0, 0))] + waits(passed),
        out_shape=[jax.ShapeDtypeStruct((pieces, 3, d, width), kind)]
        + [jax.ShapeDtypeStruct(p.shape, p.dtype) for p in passed],
        input_output_aliases={5 + len(more): 1} if passed else {},
        compiler_params=pltpu.CompilerParams(vmem_limit_bytes=60 << 20),
        cost_estimate=cost(name),
        name=name,
    )(x, gg, act, dg, du, *more, *passed, *deps)


def lane_of(rows):
    return lax.broadcasted_iota(jnp.int32, (rows, PAIR), 1)


def col(rows, i):
    return rows[:, i : i + 1]


def halves(rows):
    high = rows.astype(bf16)
    return high, (rows - high.astype(f32)).astype(bf16)


VEC, COEF, GATE, CONST = 0, 2, 3, 5


def mid_kernel(
    n_all, att_ref, first_ref, second_ref, x_ref, prev_ref, routes_ref, place_ref,
    mid_ref, hidden_ref, scal_ref, send_ref,
):
    n_ffn = n_all - 4
    d = x_ref.shape[1]
    mid = x_ref[...].astype(f32) + mul_nn(att_ref[...], second_ref[:, d:])
    mid_ref[...] = mid
    hidden = (mid * rms_scale(mid) * gain_row(first_ref, n_all + 7)).astype(bf16)
    hidden_ref[...] = hidden
    rows, d = hidden.shape
    lane = lane_of(rows)
    raw = mul_nn(hidden, first_ref[:, 2 * d :])
    logits = jnp.where(lane < n_all, raw + prev_ref[...], NEG)
    expo = jnp.exp(logits - jnp.max(logits, axis=1, keepdims=True))
    probs = jnp.where(lane < n_all, expo / jnp.sum(expo, axis=1, keepdims=True), 0.0)
    ids = [col(routes_ref[...], j) for j in range(2)]
    gates = [jnp.sum(jnp.where(lane == r, probs, 0.0), axis=1, keepdims=True) for r in ids]
    scal = probs
    coef = sum(jnp.where(r == n_ffn + 1, g, 0.0) for r, g in zip(ids, gates))
    base = n_all + 4
    for c in range(2):
        gap = col(raw, n_all + 2 * c + 1) - col(raw, n_all + 2 * c)
        first, second = 1.0 / (1.0 + jnp.exp(gap)), 1.0 / (1.0 + jnp.exp(-gap))
        const = sum(jnp.where(r == n_ffn + 2 + c, g, 0.0) for r, g in zip(ids, gates))
        coef += first * const
        scal = jnp.where(lane == n_all + 2 * c, first, scal)
        scal = jnp.where(lane == n_all + 2 * c + 1, second, scal)
        scal = jnp.where(lane == base + VEC + c, second * const, scal)
        scal = jnp.where(lane == base + CONST + c, const, scal)
        scal = jnp.where(lane == base + GATE + c, gates[c], scal)
    scal_ref[...] = jnp.where(lane == base + COEF, coef, scal)
    slots = send_ref.shape[0]
    row = lax.broadcasted_iota(jnp.int32, (slots, rows), 0)
    hits = [(row == place_ref[j : j + 1, :]) for j in range(2)]
    both = jnp.where(hits[0] | hits[1], 1.0, 0.0).astype(bf16)
    send_ref[:, :d] = mul_nn(both, hidden).astype(bf16)
    extra = jnp.zeros((slots, PAIR), f32)
    for j in range(2):
        high, low = halves(gates[j])
        pair = jnp.where(lane == 0, high.astype(f32), jnp.where(lane == 1, low.astype(f32), 0.0))
        extra += mul_nn(jnp.where(hits[j], 1.0, 0.0).astype(bf16), pair.astype(bf16))
    send_ref[:, d:] = extra.astype(bf16)


def spread_kernel(cot_ref, valid_ref, place_ref, send_ref):
    grads = (cot_ref[...] * valid_ref[...]).astype(bf16)
    row = lax.broadcasted_iota(jnp.int32, (send_ref.shape[0], grads.shape[0]), 0)
    hit = (row == place_ref[0:1, :]) | (row == place_ref[1:2, :])
    send_ref[...] = mul_nn(jnp.where(hit, 1.0, 0.0).astype(bf16), grads).astype(bf16)


def picked_rows(place_ref, j, table):
    rows, slots = place_ref.shape[0], table.shape[0]
    slot = lax.broadcasted_iota(jnp.int32, (rows, slots), 1)
    pick = jnp.where(slot == col(place_ref[...], j), 1.0, 0.0).astype(bf16)
    return mul_nn(pick, table)


def gates_back_kernel(
    n_all, back_ref, place_ref, routes_ref, scal_ref, hidden_ref, mid_ref, cot_ref, valid_ref, first_ref, second_ref,
    gmid_ref, gatt_ref, mix_ref, dgain_ref,
):
    n_ffn = n_all - 4
    base = n_all + 4
    scal = scal_ref[...]
    grads = cot_ref[...] * valid_ref[...]
    rows, d = grads.shape
    lane = lane_of(rows)
    hidden = hidden_ref[...].astype(f32)
    small = first_ref[:, 2 * d :]
    g_hidden = jnp.sum(grads * hidden, axis=1, keepdims=True)
    high, low = halves(grads)
    g_small = mul_nn(high, small) + mul_nn(low, small)
    table = back_ref[...]
    grad_hidden = col(scal, base + COEF) * grads
    grad_probs = jnp.zeros((rows, PAIR), f32)
    for j in range(2):
        r = col(routes_ref[...], j)
        came = picked_rows(place_ref, j, table)
        grad_hidden += col(scal, base + GATE + j) * came[:, :d]
        dots = came[:, d : d + 1] + came[:, d + 1 : d + 2]
        dots += jnp.where(r == n_ffn + 1, g_hidden, 0.0)
        for c in range(2):
            whole = col(scal, n_all + 2 * c) * g_hidden + col(scal, n_all + 2 * c + 1) * col(g_small, base + c)
            dots += jnp.where(r == n_ffn + 2 + c, whole, 0.0)
        grad_probs += jnp.where(lane == r, dots, 0.0)
    probs = jnp.where(lane < n_all, scal, 0.0)
    mix = probs * (grad_probs - jnp.sum(probs * grad_probs, axis=1, keepdims=True))
    for c in range(2):
        first, second = col(scal, n_all + 2 * c), col(scal, n_all + 2 * c + 1)
        const = col(scal, base + CONST + c)
        a, b = const * g_hidden, const * col(g_small, base + c)
        inner = first * a + second * b
        mix = jnp.where(lane == n_all + 2 * c, first * (a - inner), mix)
        mix = jnp.where(lane == n_all + 2 * c + 1, second * (b - inner), mix)
    mix_ref[...] = mix
    high, low = halves(mix)
    grad_hidden += mul_nt(high, small) + mul_nt(low, small)
    mid = mid_ref[...]
    back, dgain = rms_backward(mid, rms_scale(mid), gain_row(first_ref, n_all + 7), grad_hidden)
    dgain_ref[...] = dgain
    grad_mid = grads + back
    gmid_ref[...] = grad_mid
    gatt_ref[...] = mul_nt(grad_mid.astype(bf16), second_ref[:, d:]).astype(bf16)


def out_grads_kernel(
    n_all, block, core_ref, att_ref, gmid_ref, hidden_ref, mix_ref, scal_ref, cot_ref, valid_ref, dgain_ref, rest_ref,
    keep_ref, give_ref,
):
    d = att_ref.shape[1]
    base = n_all + 4
    first = rest_ref.shape[1]
    upper = core_ref[0] == 1
    keep_ref[:, :first], give_ref[:, :first] = split_rows(upper, rest_ref[...], block)
    dw_out = mul_tn(att_ref[...], gmid_ref[...].astype(bf16))
    keep_ref[:, first : first + d], give_ref[:, first : first + d] = split_rows(upper, dw_out, block)
    hidden = hidden_ref[...]
    high, low = halves(mix_ref[...])
    grads = mul_tn(hidden, high) + mul_tn(hidden, low)
    scal = scal_ref[...]
    lane = lane_of(scal.shape[0])
    vec = jnp.where((lane >= base + VEC) & (lane < base + VEC + 2), scal, 0.0)
    vec_high, vec_low = halves(vec)
    g_high, g_low = halves(cot_ref[...] * valid_ref[...])
    grads += mul_tn(g_high, vec_high) + mul_tn(g_high, vec_low) + mul_tn(g_low, vec_high)
    column = jnp.transpose(jnp.broadcast_to(dgain_ref[...], (8, d)))[:, :1]
    lane = lane_of(d)
    tail = jnp.where(lane == base + 2, column, grads)
    keep_ref[:, first + d :], give_ref[:, first + d :] = split_rows(upper, tail, block)


def output_kernel(n_all, back_ref, place_ref, scal_ref, hidden_ref, mid_ref, valid_ref, first_ref, out_ref):
    base = n_all + 4
    scal = scal_ref[...]
    lane = lane_of(scal.shape[0])
    vec = jnp.where((lane >= base + VEC) & (lane < base + VEC + 2), scal, 0.0)
    high, low = halves(vec)
    small = first_ref[:, first_ref.shape[1] - PAIR :]
    total = mid_ref[...] + mul_nt(high, small) + mul_nt(low, small)
    total += col(scal, base + COEF) * hidden_ref[...].astype(f32)
    table = back_ref[...]
    for j in range(2):
        total += col(scal, base + GATE + j) * picked_rows(place_ref, j, table)
    out_ref[...] = total * valid_ref[...]


def local(
    residual_in,
    lengths,
    routes,
    prev_logits,
    cotangent,
    w_qkv,
    w_out,
    attn_gain,
    ffn_gain,
    router,
    const_gate,
    const_vec,
    w_gate,
    w_up,
    w_down,
):
    tok_rows = residual_in.shape[1]
    feat = residual_in.shape[2]
    head_size = feat // HEADS
    score_scale = head_size ** (-0.5)
    n_dp = lax.axis_size("dp")
    n_ctx = lax.axis_size("ctx")
    n_exp = lax.axis_size("exp")
    own_exp = w_gate.shape[0]
    reps = n_dp // own_exp
    n_all = router.shape[1]
    n_ffn = n_all - 4
    cap_rows = tok_rows // 4
    sub_rows = cap_rows // reps
    n_slots = n_ffn * cap_rows
    ctx_rank = lax.axis_index("ctx")
    positions = ctx_rank * tok_rows + jnp.arange(tok_rows, dtype=jnp.int32)
    length = lengths[0]
    valid_rows = (positions < length).astype(f32)[:, None]

    def gather_ctx(rows):
        if n_ctx == 2:
            return swap(rows, "ctx", 1)
        for bit in reversed(bits_of("ctx")):
            other = swap(rows, "ctx", bit)
            upper = (ctx_rank & bit) != 0
            rows = jnp.concatenate([jnp.where(upper, other, rows), jnp.where(upper, rows, other)], axis=0)
        return rows

    def scatter_ctx(rows):
        if n_ctx == 2:
            return swap(rows, "ctx", 1)
        for bit in bits_of("ctx"):
            low, high = jnp.split(rows, 2, axis=0)
            upper = (ctx_rank & bit) != 0
            sent = jnp.where(upper, low, high).astype(bf16)
            rows = jnp.where(upper, high, low).astype(f32) + swap(sent, "ctx", bit).astype(f32)
        return rows

    route_ids = routes[0]
    choose = (route_ids[:, :, None] == jnp.arange(n_all, dtype=jnp.int32)[None, None, :]).astype(f32)
    both = jnp.sum(choose, axis=1)
    before = jnp.arange(tok_rows)
    before = (before[None, :] < before[:, None]).astype(bf16)
    counts = dot32(before, both.astype(bf16))
    slot_ids = jnp.sum(choose * counts[:, None, :], axis=-1).astype(jnp.int32)
    is_ffn = route_ids < n_ffn
    place = (
        ((route_ids % own_exp) * reps + slot_ids // sub_rows) * n_exp + route_ids // own_exp
    ) * sub_rows + slot_ids % sub_rows
    place = jnp.where(is_ffn, place, -1)
    row_ids = jnp.arange(n_slots, dtype=jnp.int32)
    place_rows = jnp.transpose(place)

    def to_experts(rows):
        return lax.all_to_all(
            rows.reshape(n_dp * n_exp, sub_rows, -1),
            ("dp", "exp"),
            split_axis=0,
            concat_axis=0,
            tiled=True,
        ).reshape(n_slots, -1)

    (grad_sent,) = simple_call(
        spread_kernel, (cotangent[0], valid_rows, place_rows), [((n_slots, feat), bf16)], 0, "spread"
    )

    small = jnp.concatenate(
        [router, const_gate, const_vec, attn_gain[:, None], ffn_gain[:, None]], axis=1
    )
    small = jnp.pad(small, ((0, 0), (0, PAIR - small.shape[1])))
    width = 2 * feat + PAIR
    far, mid_a, near = plan_steps(("ctx", "exp"))
    _, mid_b, _ = plan_steps(("exp", "ctx"))
    lane = jnp.arange(PAIR, dtype=jnp.int32)
    half = head_size // 2
    inv_freq = 10000.0 ** (-2.0 * (lane % half).astype(f32) / head_size)
    sign = jnp.where(lane % head_size < half, -1.0, 1.0)

    def turns(where):
        angles = where.astype(f32)[:, None] * inv_freq[None, :]
        return jnp.cos(angles), jnp.sin(angles) * sign[None, :]

    cosine, sine = turns(positions)
    other_start = (1 - ctx_rank) * tok_rows if n_ctx == 2 else 0
    n_other = tok_rows if n_ctx == 2 else tok_rows * n_ctx
    other_cos, other_sin = turns(other_start + jnp.arange(n_other, dtype=jnp.int32))
    other_in = gather_ctx(residual_in[0])
    rows = jnp.concatenate([w_qkv[:, : 2 * feat], small, w_qkv[:, 2 * feat :], w_out], axis=1)
    packed = pack_expert(w_gate, w_up, w_down, ())
    windows = [()] * (len(far) - 2) + [(packed,), (other_in, cosine, sine, other_cos, other_sin)]
    whole, placed = rows, []
    for step, meanwhile in zip(far, windows):
        whole, placed = gather_step(whole, placed, *step, meanwhile)
    group = trade_far(hold(packed, whole))
    part_a, part_b = whole[..., :width], whole[..., width:]
    placed_a, placed_b = placed, placed
    for i, (step_a, step_b) in enumerate(zip(mid_a, mid_b)):
        part_a, placed_a = gather_step(part_a, placed_a, *step_a)
        part_b, placed_b = gather_step(part_b, placed_b, *step_b, () if i else (grad_sent,))
    first_part, _ = gather_steps(part_a, placed_a, near)
    second_part, _ = gather_steps(part_b, placed_b, near)
    first_part = first_part.reshape(feat, width)
    second_part = second_part.reshape(feat, 2 * feat)

    rows_low = ((tok_rows, feat), bf16)
    rows_full = ((tok_rows, feat), f32)
    square = 2 * tok_rows * feat * feat
    hidden_one, queries, own_keys, own_values = simple_call(
        functools.partial(project_kernel, score_scale, n_all + 6),
        (residual_in[0], first_part, second_part, cosine, sine), [rows_low] * 4, 3 * square, "project",
    )
    tok_spec = pl.BlockSpec((tok_rows, feat), lambda i: (i, 0))
    turn_spec = pl.BlockSpec((tok_rows, PAIR), lambda i: (i, 0))

    def fixed(rows, cols):
        return pl.BlockSpec((rows, cols), lambda i: (0, 0))

    other_hidden, other_keys, other_values = pl.pallas_call(
        functools.partial(other_project_kernel, n_all + 6),
        grid=(n_other // tok_rows,),
        in_specs=[tok_spec, fixed(feat, width), fixed(feat, 2 * feat), turn_spec, turn_spec],
        out_specs=[tok_spec] * 3,
        out_shape=[jax.ShapeDtypeStruct((n_other, feat), bf16)] * 3,
        compiler_params=pltpu.CompilerParams(vmem_limit_bytes=56 << 20),
        cost_estimate=cost("project_other"),
        name="project_other",
    )(other_in, first_part, second_part, other_cos, other_sin)
    grad_rows_in = to_experts(hold(grad_sent, group, hidden_one, other_keys))
    info = jnp.stack([ctx_rank * tok_rows, length, ctx_rank]).astype(jnp.int32)
    prev = jnp.pad(prev_logits[0], ((0, 0), (0, PAIR - n_all)))
    attended, attended_low, log_total = attend(
        info, queries, own_keys, own_values, other_keys, other_values, (group, prev, place)
    )

    mid_rows, hidden, scalars, sent_rows = simple_call(
        functools.partial(mid_kernel, n_all),
        (attended_low, first_part, second_part, residual_in[0], prev, route_ids, place_rows),
        [rows_full, rows_low, ((tok_rows, PAIR), f32), ((n_slots, feat + PAIR), bf16)], 0, "mid",
    )
    rows_in = to_experts(sent_rows)

    steps_near = near_steps(own_exp)
    groups = gather_expert_near([group], steps_near)
    piece_width = group.shape[3]
    if piece_width < PAIR:
        merge = PAIR // piece_width
        whole = jnp.concatenate(groups).reshape(-1, merge, 3, feat, piece_width)
        groups = [jnp.moveaxis(whole, 1, 3).reshape(-1, 3, feat, PAIR)]
    expert_out, grad_in, act, grad_gate_pre, grad_up_pre, gated_rows, grad_expert_out = expert_call(
        rows_in, grad_rows_in, groups
    )
    back_grads = to_experts(grad_in)
    n_groups = 2 ** len(steps_near)
    flows = (gated_rows, grad_expert_out, act, grad_gate_pre, grad_up_pre)
    if piece_width < PAIR or len(steps_near) != 2:
        step = max(piece_width, PAIR)
        (whole,) = expert_weights(*flows, 0, act.shape[1] // step, step, f32, "weights_all")
        if piece_width < PAIR:
            whole = jnp.moveaxis(whole.reshape(-1, 3, feat, merge, piece_width), 3, 1)
        whole = whole.reshape(n_groups, own_exp, 3, feat, piece_width)
        expert_sum = scatter_expert_near([whole[i] for i in range(n_groups)], steps_near)
        weights_done = ()
    else:
        group_cols = own_exp * piece_width
        (far_sent,) = expert_weights(*flows, 2 * group_cols, 2 * own_exp, piece_width, bf16, "weights_far")
        far_came = swap(far_sent, *steps_near[1])
        (near_sent,) = expert_weights(
            *flows, group_cols, own_exp, piece_width, bf16, "weights_near", far_came, own_exp
        )
        near_came = swap(near_sent, *steps_near[0])
        kept, expert_out = expert_weights(
            *flows, 0, own_exp, piece_width, f32, "weights_kept", far_came, 0, expert_out, (near_sent,)
        )
        weights_done = (near_sent, kept)
    back_rows = to_experts(expert_out)
    small_shape = ((tok_rows, PAIR), f32)
    grad_mid, grad_attended, grad_mix, grad_gain_two = simple_call(
        functools.partial(gates_back_kernel, n_all),
        (
            back_grads, place, route_ids, scalars, hidden, mid_rows, cotangent[0], valid_rows, first_part, second_part,
        ),
        [rows_full, rows_low, small_shape, ((1, feat), f32)], 0, "gates_back", weights_done,
    )
    grad_queries, other_dk, other_dv, delta = grads_other(
        info, queries, other_keys, other_values, grad_attended, attended, log_total, ()
    )
    half_cols = (4 * feat + 2 * PAIR) // 2
    core = (lax.axis_index("dp") & 1).astype(jnp.int32).reshape(1)
    core_block = feat // (n_dp * n_ctx * n_exp) * row_weight("dp")
    more_wk, more_wv, other_dh, more_gain = pl.pallas_call(
        other_back_kernel,
        grid=(n_other // tok_rows,),
        in_specs=[
            tok_spec, tok_spec, tok_spec, fixed(feat, width), fixed(feat, 2 * feat), turn_spec, turn_spec, tok_spec,
        ],
        out_specs=[fixed(feat, feat), fixed(feat, feat), tok_spec, fixed(1, feat)],
        out_shape=[
            jax.ShapeDtypeStruct((feat, feat), f32), jax.ShapeDtypeStruct((feat, feat), f32),
            jax.ShapeDtypeStruct((n_other, feat), bf16), jax.ShapeDtypeStruct((1, feat), f32),
        ],
        compiler_params=pltpu.CompilerParams(vmem_limit_bytes=56 << 20),
        cost_estimate=cost("back_other"),
        name="back_other",
    )(other_dk, other_dv, other_hidden, first_part, second_part, other_cos, other_sin, other_in)
    more_dh = scatter_ctx(other_dh)
    grad_queries, own_dk, own_dv = grads_own(
        info, queries, own_keys, own_values, grad_attended, log_total, delta, grad_queries, (back_rows, other_dh)
    )
    if weights_done:
        (expert_sum,) = simple_call(
            weights_sum_kernel, (kept, near_came), [(kept.shape, bf16)], 0, "weights_sum", (own_dk,)
        )
    else:
        expert_sum = expert_sum.astype(bf16)
    expert_back = trade_far(expert_sum)
    first_keep, first_give, dw_rest, grad_hidden_one = simple_call(
        functools.partial(own_back_kernel, score_scale, core_block),
        (
            grad_queries, own_dk, own_dv, hidden_one, first_part, second_part, cosine, sine, residual_in[0],
            more_wk, more_wv, more_gain,
        ),
        [((feat // 2, half_cols), f32), ((feat // 2, half_cols), bf16), ((feat, feat), f32), rows_full],
        6 * square, "back_own", (expert_sum,), (core,),
    )
    out_keep, out_give = simple_call(
        functools.partial(out_grads_kernel, n_all, core_block),
        (attended_low, grad_mid, hidden, grad_mix, scalars, cotangent[0], valid_rows, grad_gain_two, dw_rest),
        [((feat // 2, half_cols), f32), ((feat // 2, half_cols), bf16)], 0, "out_grads", (more_dh,), (core,),
    )

    def last_rows(sent):
        (output,) = simple_call(
            functools.partial(output_kernel, n_all),
            (back_rows, place, scalars, hidden, mid_rows, valid_rows, first_part), [rows_full], 0, "output", (sent,),
        )
        (grad_x,) = simple_call(
            functools.partial(first_norm_kernel, n_all + 6),
            (grad_hidden_one, more_dh, residual_in[0], first_part, grad_mid), [rows_full], 0, "first_norm", (sent,),
        )
        results.extend([output, grad_x, *unpack_expert(expert_back, (output, grad_x))])
        return results

    results = []
    sums = scatter_parts(
        [(first_keep, first_give), (out_keep, out_give)], [mid_a, mid_b], far, near, w_out.shape[0], last_rows
    )
    output, grad_x, *expert_grads = results
    small_out = sums[:, 4 * feat + PAIR :]
    return (
        output[None],
        grad_x[None],
        jnp.concatenate([sums[:, : 2 * feat], sums[:, width : width + feat]], axis=1),
        sums[:, width + feat : width + 2 * feat],
        sums[:, 2 * feat],
        small_out[:, n_all + 6],
        small_out[:, :n_all],
        small_out[:, n_all : n_all + 4],
        small_out[:, n_all + 4 : n_all + 6],
        expert_grads[0],
        expert_grads[1],
        expert_grads[2],
    )


def solution(mesh):
    in_specs = (
        P(("dp", "exp"), "ctx", None),
        P(("dp", "exp")),
        P(("dp", "exp"), "ctx", None),
        P(("dp", "exp"), "ctx", None),
        P(("dp", "exp"), "ctx", None),
        P(("dp", "ctx", "exp"), None),
        P(("dp", "ctx", "exp"), None),
        P(("dp", "ctx", "exp")),
        P(("dp", "ctx", "exp")),
        P(("dp", "ctx", "exp"), None),
        P(("dp", "ctx", "exp"), None),
        P(("dp", "ctx", "exp"), None),
        P("exp", None, ("dp", "ctx")),
        P("exp", None, ("dp", "ctx")),
        P("exp", ("dp", "ctx"), None),
    )
    out_specs = (
        P(("dp", "exp"), "ctx", None),
        P(("dp", "exp"), "ctx", None),
        P(("dp", "ctx", "exp"), None),
        P(("dp", "ctx", "exp"), None),
        P(("dp", "ctx", "exp")),
        P(("dp", "ctx", "exp")),
        P(("dp", "ctx", "exp"), None),
        P(("dp", "ctx", "exp"), None),
        P(("dp", "ctx", "exp"), None),
        P("exp", None, ("dp", "ctx")),
        P("exp", None, ("dp", "ctx")),
        P("exp", ("dp", "ctx"), None),
    )
    return jax.shard_map(local, mesh=mesh, in_specs=in_specs, out_specs=out_specs, check_vma=False)
```

time: 743 us -> 448 us (0.60); the launches traced: 732 us -> 446 us
  Pallas kernels: 0 us -> 182 us
  matrix products: 147 us -> 0.22 us
  starting transfers between devices: 187 us -> 85.2 us
  waiting for transfers between devices: 224 us -> 127 us
  local copies, waits for them, and re-layouts: 102 us -> 28.8 us
  other arithmetic: 66.1 us -> 20.4 us
    pallas_call x0 -> x28, Pallas kernels: none -> 182 us  [the longest x11 76.7 us: simple_call(): pl.pallas_call(ordered(kernel, len(scalars) + len(args), len(deps)), in_s...]
    ppermute x74 -> x23, waiting for transfers between devices: 203 us -> 55 us  [swap(): lax.ppermute(block, axis, [(i, i ^ bit) for i in range(lax.axis_size(axis...]
    ppermute x74 -> x23, starting transfers between devices: 149 us -> 30.1 us  [swap(): lax.ppermute(block, axis, [(i, i ^ bit) for i in range(lax.axis_size(axis...]
    dot_general x37 -> x1, matrix products: 116 us -> 0.22 us  [dot32(): lax.dot_general(a, b, (dims, ((), ())), precision=precision, preferred_el...]
    all_to_all x6 -> x4, waiting for transfers between devices: 21.2 us -> 57.3 us  [to_experts(): lax.all_to_all(rows.reshape(n_dp * n_exp, sub_rows, -1), ('dp', 'exp'), s...]
    dot_general x7 -> x0, matrix products: 31.2 us -> none  [the longest x1 8.91 us: backward_step(): jnp.einsum('hqk,qhd->khd', blk_probs.astype(bf16), grad_attended, preferr...]
    concatenate x8 -> x0, local copies, waits for them, and re-layouts: 23.2 us -> none  [the longest x3 8.21 us: gather_expert(): whole = jnp.concatenate([whole, swap(whole, 'dp', bit)], axis=ff_axis)]
    unnamed x213 -> x62, local copies, waits for them, and re-layouts: 33 us -> 16.7 us
  transfers between devices with their start and end apart: 80 -> 29, of which waited for: 34 -> 15; matrix products, arithmetic and copies ran while one was open for 35% -> 6% of each run, Pallas kernels for 0% -> 31%
where the time goes in v2:
time: 448 us; the launch traced here: 446 us
  Pallas kernels  182 us (41%)
  waiting for transfers between devices  127 us (28%)
  starting transfers between devices  85.2 us (19%)
  local copies, waits for them, and re-layouts  28.8 us (6%)
  other arithmetic  20.4 us (5%)
    pallas_call x11, Pallas kernels, simple_call(): pl.pallas_call(ordered(kernel, len(scalars) + len(args), len(deps)), in_s...  76.7 us
    all_to_all x4, waiting for transfers between devices, to_experts(): lax.all_to_all(rows.reshape(n_dp * n_exp, sub_rows, -1), ('dp', 'exp'), s...  57.3 us
    ppermute x23, waiting for transfers between devices, swap(): lax.ppermute(block, axis, [(i, i ^ bit) for i in range(lax.axis_size(axis...  55 us
    all_to_all x4, starting transfers between devices, to_experts(): lax.all_to_all(rows.reshape(n_dp * n_exp, sub_rows, -1), ('dp', 'exp'), s...  45.6 us
    ppermute x23, starting transfers between devices, swap(): lax.ppermute(block, axis, [(i, i ^ bit) for i in range(lax.axis_size(axis...  30.1 us
    pallas_call x1, Pallas kernels, expert_call(): pl.pallas_call(functools.partial(expert_kernel, len(groups)), grid=(n //...  29.6 us
    pallas_call x3, Pallas kernels, attn_call(): pl.pallas_call(ordered(kernel, 1 + len(args), len(deps)), grid_spec=pltpu...  27.6 us
    pallas_call x3, Pallas kernels, expert_weights(): pl.pallas_call(ordered(functools.partial(expert_weights_kernel, len(more)...  26 us
  transfers between devices with their start and end apart: 29, of which 15 were waited for; matrix products, arithmetic and copies ran while one was open for 6% of the time, Pallas kernels for 31%

profile of v2, /device:TPU:0, one launch (start us, length us, event | category | flops | bytes accessed | tf_op | source)
XLA Modules:
  0.0 445.6 jit_solution(1522950225393785838)
XLA Ops:
  7.0 4.1 collective-permute-start
  15.4 4.1 pack.1.refs_1_.refs_0_
  23.6 3.9 spread.1.refs_1_.refs_0_
  27.5 3.1 fusion.14
  36.3 4.5 %all-to-all-start = ((bf16[4,3,768,128]{3,2,1,0:T(8,128)(2,1)}), bf16[4,3,768,128]{3,2,1,0:T(8,128)(2,1)}, u32[]{:S(2)}, u32[]{:S(2)}) async-start(bf16[4,3,768,128]{3,2,1,0:T(8,128)(2,1)} %hold.9), calls=%async_computation | async-start | bytes 4718592 | tf_op jit(solution)/shard_map/all_to_all | solution.py:451
  44.3 11.0 %collective-permute-done.7 = bf16[2,2,2,24,1536]{4,3,1,0,2:T(8,128)(2,1)S(1)} collective-permute-done((bf16[2,2,2,24,1536]{4,3,1,0,2:T(8,128)(2,1)S(1)}, bf16[2,2,2,24,1536]{4,3,1,0,2:T(8,128)(2,1)S(1)}, u32[]{:S(2)}, u32[]{:S(2)}) %collective-permute-start.7) | collective-permute-done | bytes 589856 | tf_op jit(solution)/shard_map/ppermute | solution.py:287
  66.7 5.4 %project_other.1 = (bf16[512,768]{1,0:T(8,128)(2,1)}, bf16[512,768]{1,0:T(8,128)(2,1)}, bf16[512,768]{1,0:T(8,128)(2,1)}) custom-call(bf16[512,768]{1,0:T(8,128)(2,1)} %copy-done.19, bf16[768,1664]{1,0:T(8,128)(2,1)} %bitcast.115, bf16[768,1536]{1,0:T(8,128)(2,1)} %bitcast.123, f32[512,128]{1,0:T(8,128)} %get-tuple-element.171.refs_4_.cos_ref, ...), custom_call_target="tpu_custom_call" | custom-call | flops 104166664 | bytes 1 | tf_op jit(solution)/shard_map/project_other/pallas_call | solution.py:1012
  72.1 6.6 %project.1 = (bf16[512,768]{1,0:T(8,128)(2,1)}, bf16[512,768]{1,0:T(8,128)(2,1)}, bf16[512,768]{1,0:T(8,128)(2,1)}, bf16[512,768]{1,0:T(8,128)(2,1)}) custom-call(bf16[512,768]{1,0:T(8,128)(2,1)} %bitcast.136, bf16[768,1664]{1,0:T(8,128)(2,1)} %bitcast.116, bf16[768,1536]{1,0:T(8,128)(2,1)} %bitcast.124, ...), custom_call_target="tpu_custom_call" | custom-call | flops 125000000 | bytes 1 | tf_op jit(solution)/shard_map/project/pallas_call | solution.py:600
  78.7 14.6 %all-to-all-done.refs_6_.refs_1_.refs_2_ = bf16[4,3,768,128]{3,2,1,0:T(8,128)(2,1)} async-done(((bf16[4,3,768,128]{3,2,1,0:T(8,128)(2,1)}), bf16[4,3,768,128]{3,2,1,0:T(8,128)(2,1)}, u32[]{:S(2)}, u32[]{:S(2)}) %all-to-all-start) | async-done | bytes 2359328 | tf_op jit(solution)/shard_map/all_to_all | solution.py:451
  93.3 19.5 %all-to-all-start.2 = ((bf16[16,64,768]{2,1,0:T(8,128)(2,1)}), bf16[16,64,768]{2,1,0:T(8,128)(2,1)}, u32[]{:S(2)}, u32[]{:S(2)}) async-start(bf16[16,64,768]{2,1,0:T(8,128)(2,1)} %bitcast.129), calls=%async_computation.2 | async-start | bytes 3145728 | tf_op jit(solution)/shard_map/all_to_all | solution.py:949
  117.0 9.2 %attend.1 = (f32[512,768]{1,0:T(8,128)}, bf16[512,768]{1,0:T(8,128)(2,1)S(1)}, f32[6,2,512]{2,1,0:T(2,128)S(1)}) custom-call(s32[3]{0:T(128)S(1)} %pad_add_fusion.refs_0_.info, bf16[512,768]{1,0:T(8,128)(2,1)S(1)} %copy-done, bf16[512,768]{1,0:T(8,128)(2,1)S(1)} %copy-done.5, bf16[512,768]{1,0:T(8,128)(2,1)S(1)} %copy-done.6, ...), custom_call_target="tpu_custom_call" | custom-call | flops 354166656 | bytes 1 | tf_op jit(solution)/shard_map/attend/pallas_call | solution.py:236
  127.1 9.6 %mid.1 = (f32[512,768]{1,0:T(8,128)}, bf16[512,768]{1,0:T(8,128)(2,1)}, f32[512,128]{1,0:T(8,128)}, bf16[1024,896]{1,0:T(8,128)(2,1)}) custom-call(bf16[512,768]{1,0:T(8,128)(2,1)} %copy-done.9, bf16[768,1664]{1,0:T(8,128)(2,1)} %bitcast.117, bf16[768,1536]{1,0:T(8,128)(2,1)} %bitcast.125, bf16[512,768]{1,0:T(8,128)(2,1)} %bitcast.137, ...), custom_call_target="tpu_custom_call" | custom-call | flops 187500000 | bytes 1 | tf_op jit(solution)/shard_map/mid/pallas_call | solution.py:600
  136.8 8.6 %all-to-all-done.2 = bf16[16,64,768]{2,1,0:T(8,128)(2,1)} async-done(((bf16[16,64,768]{2,1,0:T(8,128)(2,1)}), bf16[16,64,768]{2,1,0:T(8,128)(2,1)}, u32[]{:S(2)}, u32[]{:S(2)}) %all-to-all-start.2) | async-done | bytes 1572896 | tf_op jit(solution)/shard_map/all_to_all | solution.py:949
  145.3 8.2 %all-to-all-start.1 = ((bf16[16,64,896]{2,1,0:T(8,128)(2,1)}), bf16[16,64,896]{2,1,0:T(8,128)(2,1)}, u32[]{:S(2)}, u32[]{:S(2)}) async-start(bf16[16,64,896]{2,1,0:T(8,128)(2,1)} %bitcast.149), calls=%async_computation.1 | async-start | bytes 3670016 | tf_op jit(solution)/shard_map/all_to_all | solution.py:949
  153.9 12.5 %collective-permute-done.9.refs_3_ = bf16[4,3,768,128]{3,2,1,0:T(8,128)(2,1)} collective-permute-done((bf16[4,3,768,128]{3,2,1,0:T(8,128)(2,1)}, bf16[4,3,768,128]{3,2,1,0:T(8,128)(2,1)}, u32[]{:S(2)}, u32[]{:S(2)}) %collective-permute-start.9) | collective-permute-done | bytes 2359328 | tf_op jit(solution)/shard_map/ppermute | solution.py:287
  166.4 24.6 %all-to-all-done.1 = bf16[16,64,896]{2,1,0:T(8,128)(2,1)} async-done(((bf16[16,64,896]{2,1,0:T(8,128)(2,1)}), bf16[16,64,896]{2,1,0:T(8,128)(2,1)}, u32[]{:S(2)}, u32[]{:S(2)}) %all-to-all-start.1) | async-done | bytes 1835040 | tf_op jit(solution)/shard_map/all_to_all | solution.py:949
  191.0 29.6 %expert.1 = (bf16[1024,768]{1,0:T(8,128)(2,1)}, bf16[1024,896]{1,0:T(8,128)(2,1)}, bf16[1024,2048]{1,0:T(8,128)(2,1)}, bf16[1024,2048]{1,0:T(8,128)(2,1)}, bf16[...) custom-call(bf16[1024,896]{1,0:T(8,128)(2,1)} %bitcast.30.refs_0_, ...), custom_call_target="tpu_custom_call" | custom-call | flops 625000000 | bytes 1 | tf_op jit(solution)/shard_map/expert/pallas_call | solution.py:663
  220.6 9.9 %weights_far.1 = bf16[8,3,768,128]{3,2,1,0:T(8,128)(2,1)} custom-call(bf16[768,1024]{1,0:T(8,128)(2,1)} %get-tuple-element.71.x_ref.refs_0_, bf16[768,1024]{1,0:T(8,128)(2,1)} %get-tuple-element.72.gg_ref.refs_1_, bf16[1024,2048]{1,0:T(8,128)(2,1)} %get-tuple-element.73.act_ref.refs_2_, bf16[1024,2048]{1,0:T(8,128)(2,1)} %get-tuple-element.74.dg_ref.refs_3_, ...), custom_call_target="tpu_custom_call" | custom-call | flops 208333328 | bytes 1 | tf_op jit(solution)/shard_map/weights_far/pallas_call | solution.py:697
  230.5 2.3 collective-permute-start.12
  232.8 7.9 %all-to-all-start.4 = ((bf16[16,64,896]{2,1,0:T(8,128)(2,1)}), bf16[16,64,896]{2,1,0:T(8,128)(2,1)}, u32[]{:S(2)}, u32[]{:S(2)}) async-start(bf16[16,64,896]{2,1,0:T(8,128)(2,1)} %bitcast.148), calls=%async_computation.4 | async-start | bytes 3670016 | tf_op jit(solution)/shard_map/all_to_all | solution.py:949
  240.7 7.7 %weights_near.1.refs_7_.refs_10_ = bf16[4,3,768,128]{3,2,1,0:T(8,128)(2,1)} custom-call(bf16[768,1024]{1,0:T(8,128)(2,1)} %get-tuple-element.71.x_ref.refs_0_, bf16[768,1024]{1,0:T(8,128)(2,1)} %get-tuple-element.72.gg_ref.refs_1_, bf16[1024,2048]{1,0:T(8,128)(2,1)} %get-tuple-element.73.act_ref.refs_2_, ...), custom_call_target="tpu_custom_call" | custom-call | flops 166666672 | bytes 1 | tf_op jit(solution)/shard_map/weights_near/pallas_call | solution.py:697
  248.4 8.4 %weights_kept.1 = (f32[4,3,768,128]{3,2,1,0:T(8,128)}, bf16[1024,768]{1,0:T(8,128)(2,1)}) custom-call(bf16[768,1024]{1,0:T(8,128)(2,1)} %get-tuple-element.71.x_ref.refs_0_, bf16[768,1024]{1,0:T(8,128)(2,1)} %get-tuple-element.72.gg_ref.refs_1_, bf16[1024,2048]{1,0:T(8,128)(2,1)} %get-tuple-element.73.act_ref.refs_2_, ...), custom_call_target="tpu_custom_call", output_to_operand_aliasing={{1}: (6, {})} | custom-call | flops 166666672 | bytes 1 | tf_op jit(solution)/shard_map/weights_kept/pallas_call | solution.py:697
  256.8 21.4 %all-to-all-done.4 = bf16[16,64,896]{2,1,0:T(8,128)(2,1)} async-done(((bf16[16,64,896]{2,1,0:T(8,128)(2,1)}), bf16[16,64,896]{2,1,0:T(8,128)(2,1)}, u32[]{:S(2)}, u32[]{:S(2)}) %all-to-all-start.4) | async-done | bytes 1835040 | tf_op jit(solution)/shard_map/all_to_all | solution.py:949
  278.2 10.0 %all-to-all-start.3 = ((bf16[16,64,768]{2,1,0:T(8,128)(2,1)}), bf16[16,64,768]{2,1,0:T(8,128)(2,1)}, u32[]{:S(2)}, u32[]{:S(2)}) async-start(bf16[16,64,768]{2,1,0:T(8,128)(2,1)} %bitcast.143), calls=%async_computation.3 | async-start | bytes 3145728 | tf_op jit(solution)/shard_map/all_to_all | solution.py:949
  289.4 11.9 %gates_back.1 = (f32[512,768]{1,0:T(8,128)}, bf16[512,768]{1,0:T(8,128)(2,1)}, f32[512,128]{1,0:T(8,128)}, f32[1,768]{1,0:T(1,128)}) custom-call(bf16[1024,896]{1,0:T(8,128)(2,1)} %bitcast.38.refs_0_, s32[512,2]{1,0:T(8,128)} %copy-done.2, s32[512,2]{1,0:T(8,128)} %bitcast.142, f32[512,128]{1,0:T(8,128)} %get-tuple-element.78.refs_3_.refs_5_.refs_2_, ...), custom_call_target="tpu_custom_call" | custom-call | flops 229166672 | bytes 1 | tf_op jit(solution)/shard_map/gates_back/pallas_call | solution.py:600
  302.5 5.9 %grads_other.1 = (f32[768,512]{1,0:T(8,128)}, bf16[512,768]{1,0:T(8,128)(2,1)S(1)}, bf16[512,768]{1,0:T(8,128)(2,1)S(1)}, f32[6,2,512]{2,1,0:T(2,128)S(1)}) custom-call(s32[3]{0:T(128)S(1)} %pad_add_fusion.refs_0_.info, bf16[512,768]{1,0:T(8,128)(2,1)S(1)} %copy-done, bf16[512,768]{1,0:T(8,128)(2,1)S(1)} %copy-done.1, bf16[512,768]{1,0:T(8,128)(2,1)S(1)} %copy-done.8, ...), custom_call_target="tpu_custom_call" | custom-call | flops 354166656 | bytes 1 | tf_op jit(solution)/shard_map/grads_other/pallas_call | solution.py:236
  310.2 8.3 %back_other.1 = (f32[768,768]{1,0:T(8,128)}, f32[768,768]{1,0:T(8,128)}, bf16[512,768]{1,0:T(8,128)(2,1)}, f32[1,768]{1,0:T(1,128)}) custom-call(bf16[512,768]{1,0:T(8,128)(2,1)} %copy-done.14, bf16[512,768]{1,0:T(8,128)(2,1)} %copy-done.15, bf16[512,768]{1,0:T(8,128)(2,1)} %get-tuple-element.93.h_ref, bf16[768,1664]{1,0:T(8,128)(2,1)} %bitcast.119, ...), custom_call_target="tpu_custom_call" | custom-call | flops 166666672 | bytes 1 | tf_op jit(solution)/shard_map/back_other/pallas_call | solution.py:1084
  318.5 2.7 all-to-all-done.3
  322.3 12.6 %grads_own.1 = (f32[512,768]{1,0:T(8,128)S(1)}, f32[512,768]{1,0:T(8,128)}, f32[512,768]{1,0:T(8,128)}) custom-call(s32[3]{0:T(128)S(1)} %pad_add_fusion.refs_0_.info, bf16[512,768]{1,0:T(8,128)(2,1)S(1)} %copy-done, bf16[512,768]{1,0:T(8,128)(2,1)S(1)} %copy-done.5, bf16[512,768]{1,0:T(8,128)(2,1)S(1)} %copy-done.6, bf16[512,768]{1,0:T(8,128)(2,1)S(1)} %copy-done.4, ...), custom_call_target="tpu_custom_call" | custom-call | flops 270833344 | bytes 1 | tf_op jit(solution)/shard_map/grads_own/pallas_call | solution.py:236
  336.0 6.3 %collective-permute-done.13.refs_1_ = bf16[4,3,768,128]{3,2,1,0:T(8,128)(2,1)} collective-permute-done((bf16[4,3,768,128]{3,2,1,0:T(8,128)(2,1)}, bf16[4,3,768,128]{3,2,1,0:T(8,128)(2,1)}, u32[]{:S(2)}, u32[]{:S(2)}) %collective-permute-start.13) | collective-permute-done | bytes 2359328 | tf_op jit(solution)/shard_map/ppermute | solution.py:287
  342.3 4.9 %weights_sum.1.refs_13_ = bf16[4,3,768,128]{3,2,1,0:T(8,128)(2,1)} custom-call(f32[4,3,768,128]{3,2,1,0:T(8,128)} %get-tuple-element.82.refs_11_.refs_0_, bf16[4,3,768,128]{3,2,1,0:T(8,128)(2,1)} %collective-permute-done.13.refs_1_, f32[512,768]{1,0:T(8,128)} %get-tuple-element.96.refs_2_), custom_call_target="tpu_custom_call" | custom-call | flops 83333336 | bytes 1 | tf_op jit(solution)/shard_map/weights_sum/pallas_call | solution.py:600
  347.2 5.0 %all-to-all-start.5 = ((bf16[4,3,768,128]{3,2,1,0:T(8,128)(2,1)}), bf16[4,3,768,128]{3,2,1,0:T(8,128)(2,1)S(1)}, u32[]{:S(2)}, u32[]{:S(2)}) async-start(bf16[4,3,768,128]{3,2,1,0:T(8,128)(2,1)} %weights_sum.1.refs_13_), calls=%async_computation.5 | async-start | bytes 4718592 | tf_op jit(solution)/shard_map/all_to_all | solution.py:451
  352.3 3.2 collective-permute-start.14
  355.5 13.5 %back_own.1 = (f32[384,1664]{1,0:T(8,128)}, bf16[384,1664]{1,0:T(8,128)(2,1)}, f32[768,768]{1,0:T(8,128)}, f32[512,768]{1,0:T(8,128)}) custom-call(s32[1]{0:T(128)} %bitcast.36.refs_0_, f32[512,768]{1,0:T(8,128)} %copy-done.11, f32[512,768]{1,0:T(8,128)} %get-tuple-element.96.refs_2_, f32[512,768]{1,0:T(8,128)} %get-tuple-element.97.refs_3_, ...), custom_call_target="tpu_custom_call" | custom-call | flops 270833344 | bytes 1 | tf_op jit(solution)/shard_map/back_own/pallas_call | solution.py:600
  369.0 3.8 collective-permute-done.14.refs_10_.refs_1_
  373.7 7.3 %out_grads.1 = (f32[384,1664]{1,0:T(8,128)}, bf16[384,1664]{1,0:T(8,128)(2,1)}) custom-call(s32[1]{0:T(128)} %bitcast.36.refs_0_, bf16[512,768]{1,0:T(8,128)(2,1)} %copy-done.9, f32[512,768]{1,0:T(8,128)} %get-tuple-element.83.refs_2_.refs_4_, bf16[512,768]{1,0:T(8,128)(2,1)} %get-tuple-element.79.refs_4_.refs_3_, f32[512,128]{1,0:T(8,128)} %get-tuple-element.84.refs_4_, ...), custom_call_target="tpu_custom_call" | custom-call | flops 145833328 | bytes 1 | tf_op jit(solution)/shard_map/out_grads/pallas_call | solution.py:600
  381.1 3.6 combine.3
  384.6 2.0 copy.98
  388.1 3.6 combine.2
  391.7 1.7 collective-permute-start.19
  393.4 5.0 %first_norm.1.refs_2_ = f32[512,768]{1,0:T(8,128)} custom-call(f32[512,768]{1,0:T(8,128)} %get-tuple-element.105.refs_0_, bf16[512,768]{1,0:T(8,128)(2,1)} %copy-done.21, bf16[512,768]{1,0:T(8,128)(2,1)} %bitcast.139, bf16[768,1664]{1,0:T(8,128)(2,1)} %bitcast.121, f32[512,768]{1,0:T(8,128)} %get-tuple-element.83.refs_2_.refs_4_, ...), custom_call_target="tpu_custom_call" | custom-call | flops 83333336 | bytes 1 | tf_op jit(solution)/shard_map/first_norm/pallas_call | solution.py:600
  398.4 6.7 %output.1.refs_1_ = f32[512,768]{1,0:T(8,128)} custom-call(bf16[1024,768]{1,0:T(8,128)(2,1)} %bitcast.34.refs_8_.refs_0_, s32[512,2]{1,0:T(8,128)} %copy-done.2, f32[512,128]{1,0:T(8,128)} %get-tuple-element.78.refs_3_.refs_5_.refs_2_, bf16[512,768]{1,0:T(8,128)(2,1)} %get-tuple-element.79.refs_4_.refs_3_, f32[512,768]{1,0:T(8,128)} %get-tuple-element.80.refs_5_.refs_4_, ...), custom_call_target="tpu_custom_call" | custom-call | flops 125000000 | bytes 1 | tf_op jit(solution)/shard_map/output/pallas_call | solution.py:600
  409.2 4.4 unpack.1
  417.3 7.1 %collective-permute-done.20 = bf16[2,2,24,1664]{3,2,1,0:T(8,128)(2,1)S(1)} collective-permute-done((bf16[2,2,24,1664]{3,2,1,0:T(8,128)(2,1)S(1)}, bf16[2,2,24,1664]{3,2,1,0:T(8,128)(2,1)S(1)}, u32[]{:S(2)}, u32[]{:S(2)}) %collective-permute-start.20) | collective-permute-done | bytes 319520 | tf_op jit(solution)/shard_map/ppermute | solution.py:287
  424.6 1.8 collective-permute-start.21
  426.4 6.5 %collective-permute-done.21 = bf16[2,24,3328]{2,1,0:T(8,128)(2,1)S(1)} collective-permute-done((bf16[2,24,3328]{2,1,0:T(8,128)(2,1)S(1)}, bf16[2,24,3328]{2,1,0:T(8,128)(2,1)S(1)}, u32[]{:S(2)}, u32[]{:S(2)}) %collective-permute-start.21) | collective-permute-done | bytes 319520 | tf_op jit(solution)/shard_map/ppermute | solution.py:287
  433.0 2.7 collective-permute-start.22
  435.7 5.6 %collective-permute-done.22 = bf16[24,3328]{1,0:T(8,128)(2,1)S(1)} collective-permute-done((bf16[24,3328]{1,0:T(8,128)(2,1)S(1)}, bf16[24,3328]{1,0:T(8,128)(2,1)S(1)}, u32[]{:S(2)}, u32[]{:S(2)}) %collective-permute-start.22) | collective-permute-done | bytes 159776 | tf_op jit(solution)/shard_map/ppermute | solution.py:287
  (157 shorter events, 61.0 us)
Async XLA Ops:
  7.0 12.5 %copy-start.24 = (bf16[24,3200]{1,0:T(8,128)(2,1)}, bf16[24,3200]{1,0:T(8,128)(2,1)S(1)}, u32[]{:S(2)}) copy-start(bf16[24,3200]{1,0:T(8,128)(2,1)S(1)} %fusion.34.refs_0_) | copy-start | bytes 460804
  7.0 13.2 %collective-permute-start = (bf16[24,3200]{1,0:T(8,128)(2,1)S(1)}, bf16[24,3200]{1,0:T(8,128)(2,1)S(1)}, u32[]{:S(2)}, u32[]{:S(2)}) collective-permute-start(bf16[24,3200]{1,0:T(8,128)(2,1)S(1)} %fusion.34.refs_0_), channel_id=1, source_target_pairs={{0,16},{4,20},{8,24},{12,28},{16,0},{20,4},{24,8},{28,12},{1,17},{... | collective-permute-start | bytes 460808 | tf_op jit(solution)/shard_map/ppermute | solution.py:287
  11.1 19.5 %collective-permute-start.2 = (bf16[512,768]{1,0:T(8,128)(2,1)}, bf16[512,768]{1,0:T(8,128)(2,1)S(1)}, u32[]{:S(2)}, u32[]{:S(2)}) collective-permute-start(bf16[512,768]{1,0:T(8,128)(2,1)} %bitcast.135), channel_id=1, source_target_pairs={{0,2},{2,0},{1,3},{3,1},{4,6},{6,4},{5,7},{7,5},{8,10},{10,8},{9,1... | collective-permute-start | bytes 2359304 | tf_op jit(solution)/shard_map/ppermute | solution.py:287
  13.4 6.0 %copy-start.20 = (s32[1,512,2]{2,1,0:T(8,128)}, s32[1,512,2]{2,1,0:T(8,128)S(1)}, u32[]{:S(2)}) copy-start(s32[1,512,2]{2,1,0:T(8,128)S(1)} %copy.91) | copy-start | bytes 12292
  14.6 101.2 %copy-start.2 = (s32[512,2]{1,0:T(8,128)}, s32[512,2]{1,0:T(8,128)S(1)}, u32[]{:S(2)}) copy-start(s32[512,2]{1,0:T(8,128)S(1)} %fusion.21.refs_8_.refs_1_) | copy-start | bytes 12292
  21.2 6.3 %copy-start.22 = (bf16[2,24,3200]{2,1,0:T(8,128)(2,1)}, bf16[2,24,3200]{2,1,0:T(8,128)(2,1)S(1)}, u32[]{:S(2)}) copy-start(bf16[2,24,3200]{2,1,0:T(8,128)(2,1)S(1)} %pad_maximum_fusion.8.refs_0_) | copy-start | bytes 921604
  21.2 9.4 %collective-permute-start.1 = (bf16[2,24,3200]{2,1,0:T(8,128)(2,1)S(1)}, bf16[2,24,3200]{2,1,0:T(8,128)(2,1)S(1)}, u32[]{:S(2)}, u32[]{:S(2)}) collective-permute-start(bf16[2,24,3200]{2,1,0:T(8,128)(2,1)S(1)} %pad_maximum_fusion.8.refs_0_), channel_id=1, source_target_pairs={{0,8},{4,12},{8,0},{12,4},{16,24},{20,28},{24,16},{28,20},{1,9},{5... | collective-permute-start | bytes 921608 | tf_op jit(solution)/shard_map/ppermute | solution.py:287
  32.6 3.7 copy-start.23
  32.6 8.2 %collective-permute-start.6 = (bf16[2,2,24,1536]{3,2,1,0:T(8,128)(2,1)S(1)}, bf16[2,2,24,1536]{3,2,1,0:T(8,128)(2,1)S(1)}, u32[]{:S(2)}, u32[]{:S(2)}) collective-permute-start(bf16[2,2,24,1536]{3,2,1,0:T(8,128)(2,1)S(1)} %fusion.12.refs_0_), channel_id=1, source_target_pairs={{0,1},{1,0},{2,3},{3,2},{4,5},{5,4},{6,7},{7,6},{8,9},{9,8},{10,11... | collective-permute-start | bytes 884744 | tf_op jit(solution)/shard_map/ppermute | solution.py:287
  34.2 8.6 %collective-permute-start.3 = (bf16[2,2,24,1664]{3,2,1,0:T(8,128)(2,1)S(1)}, bf16[2,2,24,1664]{3,2,1,0:T(8,128)(2,1)S(1)}, u32[]{:S(2)}, u32[]{:S(2)}) collective-permute-start(bf16[2,2,24,1664]{3,2,1,0:T(8,128)(2,1)S(1)} %fusion.9), channel_id=1, source_target_pairs={{0,2},{2,0},{1,3},{3,1},{4,6},{6,4},{5,7},{7,5},{8,10},{10,8},{9,1... | collective-permute-start | bytes 958472 | tf_op jit(solution)/shard_map/ppermute | solution.py:287
  36.3 56.9 %all-to-all-start = ((bf16[4,3,768,128]{3,2,1,0:T(8,128)(2,1)}), bf16[4,3,768,128]{3,2,1,0:T(8,128)(2,1)}, u32[]{:S(2)}, u32[]{:S(2)}) async-start(bf16[4,3,768,128]{3,2,1,0:T(8,128)(2,1)} %hold.9), calls=%async_computation | async-start | bytes 4718592 | tf_op jit(solution)/shard_map/all_to_all | solution.py:451
  41.9 13.4 %collective-permute-start.7 = (bf16[2,2,2,24,1536]{4,3,1,0,2:T(8,128)(2,1)S(1)}, bf16[2,2,2,24,1536]{4,3,1,0,2:T(8,128)(2,1)S(1)}, u32[]{:S(2)}, u32[]{:S(2)}) collective-permute-start(bf16[2,2,2,24,1536]{4,3,1,0,2:T(8,128)(2,1)S(1)} %pad_maximum_fusion.7), channel_id=1, source_target_pairs={{0,2},{2,0},{1,3},{3,1},{4,6},{6,4},{5,7},{7,5},{8,10},{10,8},{9,1... | collective-permute-start | bytes 1769480 | tf_op jit(solution)/shard_map/ppermute | solution.py:287
  43.0 14.5 %collective-permute-start.4 = (bf16[2,2,2,24,1664]{4,3,1,0,2:T(8,128)(2,1)S(1)}, bf16[2,2,2,24,1664]{4,3,1,0,2:T(8,128)(2,1)S(1)}, u32[]{:S(2)}, u32[]{:S(2)}) collective-permute-start(bf16[2,2,2,24,1664]{4,3,1,0,2:T(8,128)(2,1)S(1)} %pad_maximum_fusion.6), channel_id=1, source_target_pairs={{0,1},{1,0},{2,3},{3,2},{4,5},{5,4},{6,7},{7,6},{8,9},{9,8},{10,11... | collective-permute-start | bytes 1916936 | tf_op jit(solution)/shard_map/ppermute | solution.py:287
  56.5 3.2 collective-permute-start.8
  58.8 4.3 collective-permute-start.5
  93.3 20.7 %copy-start.26 = (f32[1,512,12]{1,0,2:T(1,128)S(1)}, f32[1,512,12]{1,0,2:T(1,128)}, u32[]{:S(2)}) copy-start(f32[1,512,12]{1,0,2:T(1,128)} %param.18) | copy-start | bytes 73732
  93.3 22.6 %copy-start = (bf16[512,768]{1,0:T(8,128)(2,1)S(1)}, bf16[512,768]{1,0:T(8,128)(2,1)}, u32[]{:S(2)}) copy-start(bf16[512,768]{1,0:T(8,128)(2,1)} %get-tuple-element.63.refs_1_.q_ref) | copy-start | bytes 2359300
  93.3 22.6 %copy-start.1 = (bf16[512,768]{1,0:T(8,128)(2,1)S(1)}, bf16[512,768]{1,0:T(8,128)(2,1)}, u32[]{:S(2)}) copy-start(bf16[512,768]{1,0:T(8,128)(2,1)} %get-tuple-element.66.refs_4_.refs_3_.k_ref) | copy-start | bytes 2359300
  93.3 22.6 %copy-start.5 = (bf16[512,768]{1,0:T(8,128)(2,1)S(1)}, bf16[512,768]{1,0:T(8,128)(2,1)}, u32[]{:S(2)}) copy-start(bf16[512,768]{1,0:T(8,128)(2,1)} %get-tuple-element.64.refs_2_) | copy-start | bytes 2359300
  93.3 22.6 %copy-start.6 = (bf16[512,768]{1,0:T(8,128)(2,1)S(1)}, bf16[512,768]{1,0:T(8,128)(2,1)}, u32[]{:S(2)}) copy-start(bf16[512,768]{1,0:T(8,128)(2,1)} %get-tuple-element.65.refs_3_) | copy-start | bytes 2359300
  93.3 52.1 %all-to-all-start.2 = ((bf16[16,64,768]{2,1,0:T(8,128)(2,1)}), bf16[16,64,768]{2,1,0:T(8,128)(2,1)}, u32[]{:S(2)}, u32[]{:S(2)}) async-start(bf16[16,64,768]{2,1,0:T(8,128)(2,1)} %bitcast.129), calls=%async_computation.2 | async-start | bytes 3145728 | tf_op jit(solution)/shard_map/all_to_all | solution.py:949
  112.7 53.7 %collective-permute-start.9 = (bf16[4,3,768,128]{3,2,1,0:T(8,128)(2,1)}, bf16[4,3,768,128]{3,2,1,0:T(8,128)(2,1)}, u32[]{:S(2)}, u32[]{:S(2)}) collective-permute-start(bf16[4,3,768,128]{3,2,1,0:T(8,128)(2,1)} %all-to-all-done.refs_6_.refs_1_.refs_2_), channel_id=1, source_target_pairs={{0,2},{2,0},{1,3},{3,1},{4,6},{6,4},{5,7},{7,5},{8,10},{10,8},{9,1... | collective-permute-start | bytes 7077896 | tf_op jit(solution)/shard_map/ppermute | solution.py:287
  115.8 10.4 %copy-start.10 = (f32[512,128]{1,0:T(8,128)}, f32[512,128]{1,0:T(8,128)S(1)}, u32[]{:S(2)}) copy-start(f32[512,128]{1,0:T(8,128)S(1)} %pad.9.refs_7_.prev_ref) | copy-start | bytes 786436
  145.3 45.7 %all-to-all-start.1 = ((bf16[16,64,896]{2,1,0:T(8,128)(2,1)}), bf16[16,64,896]{2,1,0:T(8,128)(2,1)}, u32[]{:S(2)}, u32[]{:S(2)}) async-start(bf16[16,64,896]{2,1,0:T(8,128)(2,1)} %bitcast.149), calls=%async_computation.1 | async-start | bytes 3670016 | tf_op jit(solution)/shard_map/all_to_all | solution.py:949
  153.5 12.9 %collective-permute-start.10 = (bf16[4,3,768,128]{3,2,1,0:T(8,128)(2,1)}, bf16[4,3,768,128]{3,2,1,0:T(8,128)(2,1)}, u32[]{:S(2)}, u32[]{:S(2)}) collective-permute-start(bf16[4,3,768,128]{3,2,1,0:T(8,128)(2,1)} %all-to-all-done.refs_6_.refs_1_.refs_2_), channel_id=1, source_target_pairs={{0,4},{4,0},{8,12},{12,8},{16,20},{20,16},{24,28},{28,24},{1,5},{5... | collective-permute-start | bytes 7077896 | tf_op jit(solution)/shard_map/ppermute | solution.py:287
  166.4 24.6 %collective-permute-start.11 = (bf16[4,3,768,128]{3,2,1,0:T(8,128)(2,1)}, bf16[4,3,768,128]{3,2,1,0:T(8,128)(2,1)}, u32[]{:S(2)}, u32[]{:S(2)}) collective-permute-start(bf16[4,3,768,128]{3,2,1,0:T(8,128)(2,1)} %collective-permute-done.9.refs_3_), channel_id=1, source_target_pairs={{0,4},{4,0},{8,12},{12,8},{16,20},{20,16},{24,28},{28,24},{1,5},{5... | collective-permute-start | bytes 7077896 | tf_op jit(solution)/shard_map/ppermute | solution.py:287
  230.5 10.2 %collective-permute-start.12 = (bf16[8,3,768,128]{3,2,1,0:T(8,128)(2,1)}, bf16[8,3,768,128]{3,2,1,0:T(8,128)(2,1)}, u32[]{:S(2)}, u32[]{:S(2)}) collective-permute-start(bf16[8,3,768,128]{3,2,1,0:T(8,128)(2,1)} %weights_far.1), channel_id=1, source_target_pairs={{0,4},{4,0},{8,12},{12,8},{16,20},{20,16},{24,28},{28,24},{1,5},{5... | collective-permute-start | bytes 14155784 | tf_op jit(solution)/shard_map/ppermute | solution.py:287
  232.8 45.4 %all-to-all-start.4 = ((bf16[16,64,896]{2,1,0:T(8,128)(2,1)}), bf16[16,64,896]{2,1,0:T(8,128)(2,1)}, u32[]{:S(2)}, u32[]{:S(2)}) async-start(bf16[16,64,896]{2,1,0:T(8,128)(2,1)} %bitcast.148), calls=%async_computation.4 | async-start | bytes 3670016 | tf_op jit(solution)/shard_map/all_to_all | solution.py:949
  278.2 43.0 %all-to-all-start.3 = ((bf16[16,64,768]{2,1,0:T(8,128)(2,1)}), bf16[16,64,768]{2,1,0:T(8,128)(2,1)}, u32[]{:S(2)}, u32[]{:S(2)}) async-start(bf16[16,64,768]{2,1,0:T(8,128)(2,1)} %bitcast.143), calls=%async_computation.3 | async-start | bytes 3145728 | tf_op jit(solution)/shard_map/all_to_all | solution.py:949
  288.2 54.0 %collective-permute-start.13 = (bf16[4,3,768,128]{3,2,1,0:T(8,128)(2,1)}, bf16[4,3,768,128]{3,2,1,0:T(8,128)(2,1)}, u32[]{:S(2)}, u32[]{:S(2)}) collective-permute-start(bf16[4,3,768,128]{3,2,1,0:T(8,128)(2,1)} %weights_near.1.refs_7_.refs_10_), channel_id=1, source_target_pairs={{0,2},{2,0},{1,3},{3,1},{4,6},{6,4},{5,7},{7,5},{8,10},{10,8},{9,1... | collective-permute-start | bytes 7077896 | tf_op jit(solution)/shard_map/ppermute | solution.py:287
  289.4 11.9 %copy-start.8 = (bf16[512,768]{1,0:T(8,128)(2,1)S(1)}, bf16[512,768]{1,0:T(8,128)(2,1)}, u32[]{:S(2)}) copy-start(bf16[512,768]{1,0:T(8,128)(2,1)} %get-tuple-element.67.refs_5_.v_ref) | copy-start | bytes 2359300
  310.2 11.0 %copy-start.4 = (bf16[512,768]{1,0:T(8,128)(2,1)S(1)}, bf16[512,768]{1,0:T(8,128)(2,1)}, u32[]{:S(2)}) copy-start(bf16[512,768]{1,0:T(8,128)(2,1)} %get-tuple-element.86.grad_ref.refs_4_) | copy-start | bytes 2359300
  334.9 1.1 copy-start.11
  347.2 5.1 %copy-start.13 = (bf16[512,768]{1,0:T(8,128)(2,1)S(1)}, bf16[512,768]{1,0:T(8,128)(2,1)}, u32[]{:S(2)}) copy-start(bf16[512,768]{1,0:T(8,128)(2,1)} %get-tuple-element.94.refs_9_) | copy-start | bytes 2359300
  347.2 60.7 %all-to-all-start.5 = ((bf16[4,3,768,128]{3,2,1,0:T(8,128)(2,1)}), bf16[4,3,768,128]{3,2,1,0:T(8,128)(2,1)S(1)}, u32[]{:S(2)}, u32[]{:S(2)}) async-start(bf16[4,3,768,128]{3,2,1,0:T(8,128)(2,1)} %weights_sum.1.refs_13_), calls=%async_computation.5 | async-start | bytes 4718592 | tf_op jit(solution)/shard_map/all_to_all | solution.py:451
  352.3 20.5 %collective-permute-start.14 = (bf16[512,768]{1,0:T(8,128)(2,1)S(1)}, bf16[512,768]{1,0:T(8,128)(2,1)S(1)}, u32[]{:S(2)}, u32[]{:S(2)}) collective-permute-start(bf16[512,768]{1,0:T(8,128)(2,1)S(1)} %copy-done.13), channel_id=1, source_target_pairs={{0,2},{2,0},{1,3},{3,1},{4,6},{6,4},{5,7},{7,5},{8,10},{10,8},{9,1... | collective-permute-start | bytes 2359304 | tf_op jit(solution)/shard_map/ppermute | solution.py:287
  369.0 12.1 %collective-permute-start.16 = (bf16[384,1664]{1,0:T(8,128)(2,1)}, bf16[384,1664]{1,0:T(8,128)(2,1)}, u32[]{:S(2)}, u32[]{:S(2)}) collective-permute-start(bf16[384,1664]{1,0:T(8,128)(2,1)} %get-tuple-element.107), channel_id=1, source_target_pairs={{0,4},{4,0},{8,12},{12,8},{16,20},{20,16},{24,28},{28,24},{1,5},{5... | collective-permute-start | bytes 3833864 | tf_op jit(solution)/shard_map/ppermute | solution.py:287
  381.1 7.0 %collective-permute-start.15 = (bf16[384,1664]{1,0:T(8,128)(2,1)}, bf16[384,1664]{1,0:T(8,128)(2,1)}, u32[]{:S(2)}, u32[]{:S(2)}) collective-permute-start(bf16[384,1664]{1,0:T(8,128)(2,1)} %get-tuple-element.103), channel_id=1, source_target_pairs={{0,4},{4,0},{8,12},{12,8},{16,20},{20,16},{24,28},{28,24},{1,5},{5... | collective-permute-start | bytes 3833864 | tf_op jit(solution)/shard_map/ppermute | solution.py:287
  386.6 18.6 %collective-permute-start.17 = (bf16[2,2,2,24,1664]{4,3,1,0,2:T(8,128)(2,1)}, bf16[2,2,2,24,1664]{4,3,1,0,2:T(8,128)(2,1)}, u32[]{:S(2)}, u32[]{:S(2)}) collective-permute-start(bf16[2,2,2,24,1664]{4,3,1,0,2:T(8,128)(2,1)} %copy.98), channel_id=1, source_target_pairs={{0,1},{1,0},{2,3},{3,2},{4,5},{5,4},{6,7},{7,6},{8,9},{9,8},{10,11... | collective-permute-start | bytes 1916936 | tf_op jit(solution)/shard_map/ppermute | solution.py:287
  391.7 21.9 %collective-permute-start.19 = (bf16[2,2,2,24,1664]{4,3,2,1,0:T(8,128)(2,1)}, bf16[2,2,2,24,1664]{4,3,2,1,0:T(8,128)(2,1)S(1)}, u32[]{:S(2)}, u32[]{:S(2)}) collective-permute-start(bf16[2,2,2,24,1664]{4,3,2,1,0:T(8,128)(2,1)} %bitcast.145), channel_id=1, source_target_pairs={{0,2},{2,0},{1,3},{3,1},{4,6},{6,4},{5,7},{7,5},{8,10},{10,8},{9,1... | collective-permute-start | bytes 1916936 | tf_op jit(solution)/shard_map/ppermute | solution.py:287
  398.4 6.7 %copy-start.25 = (f32[192,1664]{1,0:T(8,128)S(1)}, f32[192,1664]{1,0:T(8,128)}, u32[]{:S(2)}) copy-start(f32[192,1664]{1,0:T(8,128)} %get-tuple-element.108) | copy-start | bytes 3833860
  406.4 1.2 copy-start.17
  407.6 9.6 %collective-permute-start.18 = (bf16[2,2,24,1664]{3,2,1,0:T(8,128)(2,1)}, bf16[2,2,24,1664]{3,2,1,0:T(8,128)(2,1)S(1)}, u32[]{:S(2)}, u32[]{:S(2)}) collective-permute-start(bf16[2,2,24,1664]{3,2,1,0:T(8,128)(2,1)} %fusion.6), channel_id=1, source_target_pairs={{0,2},{2,0},{1,3},{3,1},{4,6},{6,4},{5,7},{7,5},{8,10},{10,8},{9,1... | collective-permute-start | bytes 958472 | tf_op jit(solution)/shard_map/ppermute | solution.py:287
  407.9 1.4 copy-start.16
  413.6 3.6 copy-start.18
  415.2 9.2 %collective-permute-start.20 = (bf16[2,2,24,1664]{3,2,1,0:T(8,128)(2,1)S(1)}, bf16[2,2,24,1664]{3,2,1,0:T(8,128)(2,1)S(1)}, u32[]{:S(2)}, u32[]{:S(2)}) collective-permute-start(bf16[2,2,24,1664]{3,2,1,0:T(8,128)(2,1)S(1)} %fusion.7), channel_id=1, source_target_pairs={{0,1},{1,0},{2,3},{3,2},{4,5},{5,4},{6,7},{7,6},{8,9},{9,8},{10,11... | collective-permute-start | bytes 958472 | tf_op jit(solution)/shard_map/ppermute | solution.py:287
  424.6 8.3 %collective-permute-start.21 = (bf16[2,24,3328]{2,1,0:T(8,128)(2,1)S(1)}, bf16[2,24,3328]{2,1,0:T(8,128)(2,1)S(1)}, u32[]{:S(2)}, u32[]{:S(2)}) collective-permute-start(bf16[2,24,3328]{2,1,0:T(8,128)(2,1)S(1)} %fusion.8), channel_id=1, source_target_pairs={{0,8},{4,12},{8,0},{12,4},{16,24},{20,28},{24,16},{28,20},{1,9},{5... | collective-permute-start | bytes 958472 | tf_op jit(solution)/shard_map/ppermute | solution.py:287
  433.0 8.3 %collective-permute-start.22 = (bf16[24,3328]{1,0:T(8,128)(2,1)S(1)}, bf16[24,3328]{1,0:T(8,128)(2,1)S(1)}, u32[]{:S(2)}, u32[]{:S(2)}) collective-permute-start(bf16[24,3328]{1,0:T(8,128)(2,1)S(1)} %fusion.31), channel_id=1, source_target_pairs={{0,16},{4,20},{8,24},{12,28},{16,0},{20,4},{24,8},{28,12},{1,17},{... | collective-permute-start | bytes 479240 | tf_op jit(solution)/shard_map/ppermute | solution.py:287
  (8 other events, 7.9 us)
